TPU v7x, 512 devices: a whole 4x4x16 slice. The times are simulated.
512 devices in a mesh: gx: 16 (over z), gy: 8 (over x, core), gz: 4 (over y).
Axes of the slice: x: 4, y: 4, z: 16, core: 2. Of those that a mesh axis runs over, the one named last changes fastest.
Arguments:
- box_counts: int32 [32], replicated, may hold values from 2 to 4, as said below
- viscosity: float32 [3], replicated, may hold values from 0.5 to 2
- implicit_coef: float32 [16, 128, 32, 512], P('gx', ('gy', 'gz')), may hold values from 0.02 to 0.5
- right_side: float32 [16, 128, 3, 32, 512], P('gx', ('gy', 'gz')), may hold values from -8 to 8
- old_direction: float32 [16, 128, 3, 32, 512], P('gx', ('gy', 'gz')), may hold values from -6 to 6
- previous_dot: float32 [1], replicated, may hold values from 0.05 to 0.5
Outputs:
- smoothed: float32 [16, 128, 3, 32, 512], P('gx', ('gy', 'gz'))
- direction: float32 [16, 128, 3, 32, 512], P('gx', ('gy', 'gz'))
Inputs may be any that keep to these rules, and one draw needn't show every extreme that they name: `box_counts`: every device holds from 2 to 4 columns; in every draw one device holds exactly 4 and another exactly 2; the total is even.
All inputs are finite; a program needn't handle non-finite values.
Results may differ from a plain program's by a relative error of at most 0.00005.
Values sent between devices are 32-bit elements; how exact they have to be, the bound alone decides.
No kernel may reach another device: no remote copies, remote signals or barrier semaphores. Data moves between devices by JAX's collectives and lax.ppermute only.
A program may use at most 64 MiB of HBM per device.

v0:
```python
import jax
import jax.numpy as jnp
from jax import lax
from jax.sharding import PartitionSpec as P

EDGE = 16
SWEEPS_FINE = 2
SWEEPS_COARSE = 4


def padded_2(cells, sides, width):
    for axis, dim in sides:
        count = lax.axis_size(axis)
        ends = count - 1
        head = lax.slice_in_dim(cells, 0, width, axis=dim)
        tail = lax.slice_in_dim(cells, cells.shape[dim] - width, cells.shape[dim], axis=dim)
        cells = jnp.concatenate(
            [
                lax.ppermute(tail, axis, [(i, (i + 1) % count) for i in range(ends)]),
                cells,
                lax.ppermute(head, axis, [((i + 1) % count, i) for i in range(ends)]),
            ],
            axis=dim,
        )
    return cells


def from_behind(value, axis, steps):
    count = lax.axis_size(axis)
    initial, last = (max(0, -steps), min(count, count - steps))
    return lax.ppermute(value, axis, [(source, source + steps) for source in range(initial, last)])


def colour_mask(layers, row_count, row_len):
    layer_ids = jnp.arange(layers, dtype=jnp.int32)[:, None]
    flat_ids = jnp.arange(row_count * row_len, dtype=jnp.int32)[None, :]
    return (layer_ids + flat_ids // row_len + flat_ids % row_len) % 2


def pair_matrix(row_count, row_len):
    flat_ids = jnp.arange(row_count * row_len, dtype=jnp.int32)
    target = flat_ids // row_len // 2 * (row_len // 2) + flat_ids % row_len // 2
    cells = jnp.arange(row_count * row_len // 4, dtype=jnp.int32)
    return (target[:, None] == cells[None, :]).astype(jnp.float32)


def shrink(values, pairs):
    summed = values[:, :, 0::2] + values[:, :, 1::2]
    return jnp.einsum("sczl,lm->sczm", summed, pairs, precision=lax.Precision.HIGHEST) * 0.125


def expand(values, pairs):
    spread = jnp.einsum("sczm,lm->sczl", values, pairs, precision=lax.Precision.HIGHEST)
    return jnp.repeat(spread, 2, axis=2)


def neighbor_sum(values, held_count, row_len, level):
    flat_len = values.shape[-1]
    slot_count = values.shape[0]
    first_rows = values[..., :row_len]
    last_rows = values[..., flat_len - row_len :]
    ends = jnp.stack(
        [first_rows[0], lax.dynamic_index_in_dim(last_rows, held_count - 1, 0, keepdims=False)]
    )
    if level == "fine":
        padded = padded_2(values, (("gx", 2),), 1)
        beside_all = padded_2(ends, ((("gy", "gz"), 0),), 1)
    else:
        padded = padded_2(values, (("gx", 2),), 1)
        beside_all = padded_2(ends, ((("gy", "gz"), 0),), 1)
    from_left = beside_all[0]
    from_right = beside_all[3]
    position = jnp.arange(slot_count, dtype=jnp.int32)[:, None, None, None]
    left_planes = jnp.concatenate([from_left[None], last_rows[:-1]], axis=0)
    right_planes = jnp.concatenate([first_rows[1:], jnp.zeros_like(first_rows[:1])], axis=0)
    right_planes = jnp.where(position == held_count - 1, from_right[None], right_planes)
    minus_x = jnp.concatenate([left_planes, values[..., : flat_len - row_len]], axis=-1)
    plus_x = jnp.concatenate([values[..., row_len:], right_planes], axis=-1)
    row_pos = jnp.arange(flat_len, dtype=jnp.int32) % row_len
    zero_col = jnp.zeros_like(values[..., :1])
    minus_y = jnp.where(row_pos == 0, 0.0, jnp.concatenate([zero_col, values[..., :-1]], axis=-1))
    plus_y = jnp.where(
        row_pos == row_len - 1, 0.0, jnp.concatenate([values[..., 1:], zero_col], axis=-1)
    )
    return padded[:, :, 2:] + padded[:, :, :-2] + minus_x + plus_x + minus_y + plus_y


def sweep_colour(values, source, diagonal, factor, chosen, held_count, row_len, level):
    updated = (source + factor * neighbor_sum(values, held_count, row_len, level)) / diagonal
    return jnp.where(chosen, updated, values)


def per_device(box_counts, viscosity, implicit_coef, right_side, old_direction, previous_dot):
    group_n = lax.axis_size(("gy", "gz"))
    my_index = lax.axis_index(("gy", "gz"))
    slab_n = lax.axis_size("gx")
    starts = jnp.cumsum(box_counts) - box_counts
    mine = jnp.arange(group_n, dtype=jnp.int32) == my_index
    first_col = jnp.sum(jnp.where(mine, starts, 0))
    held_count = jnp.sum(jnp.where(mine, box_counts, 0))
    total_cols = jnp.sum(box_counts)
    source = right_side[0]
    slot_count, _, layers, flat_len = source.shape
    row_len = flat_len // EDGE
    half_len = flat_len // 4
    coef_fine = implicit_coef[0][:, None]
    factor = viscosity[None, :, None, None]
    diagonal = coef_fine + 6.0 * factor
    usable = (jnp.arange(slot_count, dtype=jnp.int32) < held_count)[:, None, None, None]
    colours = colour_mask(layers, EDGE, row_len)
    red_cells = usable & (colours == 0)
    black_cells = usable & (colours == 1)
    values = jnp.zeros_like(source)
    for sweep_no in range(SWEEPS_FINE):
        values = sweep_colour(
            values, source, diagonal, factor, red_cells, held_count, row_len, "fine"
        )
        values = sweep_colour(
            values, source, diagonal, factor, black_cells, held_count, row_len, "fine"
        )
    remain = jnp.where(
        usable,
        source - (diagonal * values - factor * neighbor_sum(values, held_count, row_len, "fine")),
        0.0,
    )
    pairs = pair_matrix(EDGE, row_len)
    halves = shrink(jnp.concatenate([remain, coef_fine], axis=1), pairs)
    coarse_slots = slot_count // 2
    coarse_first = (first_col + 1) // 2
    coarse_count = (first_col + held_count + 1) // 2 - coarse_first
    coarse_factor = factor * 0.25
    coarse_colours = colour_mask(EDGE, EDGE, EDGE)
    own_columns = first_col + jnp.arange(slot_count, dtype=jnp.int32)
    half_pick = (own_columns % 2)[:, None, None, None]
    moved = from_behind(halves[0], ("gy", "gz"), -1)
    coarse_pos = jnp.arange(coarse_slots, dtype=jnp.int32)
    lower_at = jnp.clip(2 * (coarse_first + coarse_pos) - first_col, 0, slot_count - 1)
    upper_at = 2 * (coarse_first + coarse_pos) + 1 - first_col
    lower = jnp.take(halves, lower_at, axis=0)
    upper_local = jnp.take(halves, jnp.clip(upper_at, 0, slot_count - 1), axis=0)
    upper = jnp.where((upper_at < held_count)[:, None, None, None], upper_local, moved[None])
    box_live = (coarse_pos < coarse_count)[:, None, None, None]
    joined = jnp.where(box_live, jnp.concatenate([lower, upper], axis=-1), 0.0)
    coarse_source = joined[:, :3]
    coarse_diag = joined[:, 3:] + 6.0 * coarse_factor
    coarse_red = box_live & (coarse_colours == 0)
    coarse_black = box_live & (coarse_colours == 1)
    correction = jnp.zeros_like(coarse_source)
    for sweep_no in range(SWEEPS_COARSE):
        correction = sweep_colour(
            correction,
            coarse_source,
            coarse_diag,
            coarse_factor,
            coarse_red,
            coarse_count,
            EDGE,
            "coarse",
        )
        correction = sweep_colour(
            correction,
            coarse_source,
            coarse_diag,
            coarse_factor,
            coarse_black,
            coarse_count,
            EDGE,
            "coarse",
        )
    tail = lax.dynamic_index_in_dim(correction, coarse_count - 1, 0, keepdims=False)[..., half_len:]
    from_left = from_behind(tail, ("gy", "gz"), 1)
    coarse_index = own_columns // 2 - coarse_first
    picked = jnp.take(correction, jnp.clip(coarse_index, 0, coarse_slots - 1), axis=0)
    piece = jnp.where(half_pick == 0, picked[..., :half_len], picked[..., half_len:])
    piece = jnp.where((coarse_index < 0)[:, None, None, None], from_left[None], piece)
    values = values + jnp.where(usable, expand(piece, pairs), 0.0)
    for sweep_no in range(SWEEPS_FINE):
        values = sweep_colour(
            values, source, diagonal, factor, black_cells, held_count, row_len, "fine"
        )
        values = sweep_colour(
            values, source, diagonal, factor, red_cells, held_count, row_len, "fine"
        )
    local_dot = jnp.sum(jnp.where(usable, source * values, 0.0))
    dot_total = lax.psum(local_dot, ("gx", "gy", "gz"))
    cell_total = total_cols.astype(jnp.float32) * (3.0 * slab_n * layers * flat_len)
    ratio = dot_total / cell_total / previous_dot[0]
    direction = jnp.where(usable, values + ratio * old_direction[0], 0.0)
    return (values[None], direction[None])


def solution(mesh):
    placed = (
        P(),
        P(),
        P("gx", ("gy", "gz"), None, None),
        P("gx", ("gy", "gz"), None, None, None),
        P("gx", ("gy", "gz"), None, None, None),
        P(),
    )
    return jax.shard_map(
        per_device,
        mesh=mesh,
        in_specs=placed,
        out_specs=(
            P("gx", ("gy", "gz"), None, None, None),
            P("gx", ("gy", "gz"), None, None, None),
        ),
        check_vma=False,
    )
```

profile of v0, /device:TPU:1, one launch (start us, length us, event | category | flops | bytes accessed | tf_op | source)
XLA Modules:
  0.0 436.1 jit_solution(6051526462258166405)
XLA Ops:
  0.7 6.2 %collective-permute-start.3 = (f32[1,3,32,32]{3,2,1,0:T(8,128)S(1)}, f32[1,3,32,32]{3,2,1,0:T(8,128)S(1)}, u32[]{:S(2)}, u32[]{:S(2)}) collective-permute-start(f32[1,3,32,32]{3,2,1,0:T(8,128)S(1)} %dynamic_slice.57), channel_id=1, source_target_pairs={{1,0},{2,1},{3,2},{4,3},{5,4},{6,5},{7,6},{8,7},{9,8},{10,9},{11,1... | collective-permute-start | bytes 36872 | tf_op jit(solution)/shard_map/ppermute | solution.py:21
  6.8 1.9 collective-permute-start.2
  10.1 4.2 collective-permute-start.1
  14.9 5.2 %collective-permute-start.24 = (f32[1,3,16,16]{3,2,1,0:T(8,128)}, f32[1,3,16,16]{3,2,1,0:T(8,128)S(1)}, u32[]{:S(2)}, u32[]{:S(2)}) collective-permute-start(f32[1,3,16,16]{3,2,1,0:T(8,128)} %dynamic_slice.62), channel_id=1, source_target_pairs={{1,0},{2,1},{3,2},{4,3},{5,4},{6,5},{7,6},{8,7},{9,8},{10,9},{11,1... | collective-permute-start | bytes 9224 | tf_op jit(solution)/shard_map/ppermute | solution.py:21
  37.8 1.9 collective-permute-start.23
  45.2 5.0 %collective-permute-start.7 = (f32[1,3,32,32]{3,2,1,0:T(8,128)S(1)}, f32[1,3,32,32]{3,2,1,0:T(8,128)S(1)}, u32[]{:S(2)}, u32[]{:S(2)}) collective-permute-start(f32[1,3,32,32]{3,2,1,0:T(8,128)S(1)} %slice.875), channel_id=1, source_target_pairs={{1,0},{2,1},{3,2},{4,3},{5,4},{6,5},{7,6},{8,7},{9,8},{10,9},{11,1... | collective-permute-start | bytes 36872 | tf_op jit(solution)/shard_map/ppermute | solution.py:21
  50.2 1.9 collective-permute-start.6
  53.5 4.9 %collective-permute-start.5 = (f32[4,3,1,512]{3,2,1,0:T(1,128)S(1)}, f32[4,3,1,512]{3,2,1,0:T(1,128)S(1)}, u32[]{:S(2)}, u32[]{:S(2)}) collective-permute-start(f32[4,3,1,512]{3,2,1,0:T(1,128)S(1)} %get-tuple-element.75), channel_id=1, source_target_pairs={{0,32},{32,64},{64,96},{96,128},{128,160},{160,192},{192,224},{224... | collective-permute-start | bytes 73736 | tf_op jit(solution)/shard_map/ppermute | solution.py:19
  61.1 5.7 %collective-permute-start.11 = (f32[1,3,32,32]{3,2,1,0:T(8,128)S(1)}, f32[1,3,32,32]{3,2,1,0:T(8,128)S(1)}, u32[]{:S(2)}, u32[]{:S(2)}) collective-permute-start(f32[1,3,32,32]{3,2,1,0:T(8,128)S(1)} %slice.885), channel_id=1, source_target_pairs={{1,0},{2,1},{3,2},{4,3},{5,4},{6,5},{7,6},{8,7},{9,8},{10,9},{11,1... | collective-permute-start | bytes 36872 | tf_op jit(solution)/shard_map/ppermute | solution.py:21
  66.9 1.9 collective-permute-start.10
  70.1 4.6 %collective-permute-start.9 = (f32[4,3,1,512]{3,2,1,0:T(1,128)S(1)}, f32[4,3,1,512]{3,2,1,0:T(1,128)S(1)}, u32[]{:S(2)}, u32[]{:S(2)}) collective-permute-start(f32[4,3,1,512]{3,2,1,0:T(1,128)S(1)} %get-tuple-element.67), channel_id=1, source_target_pairs={{0,32},{32,64},{64,96},{96,128},{128,160},{160,192},{192,224},{224... | collective-permute-start | bytes 73736 | tf_op jit(solution)/shard_map/ppermute | solution.py:19
  77.4 5.7 %collective-permute-start.15 = (f32[1,3,32,32]{3,2,1,0:T(8,128)S(1)}, f32[1,3,32,32]{3,2,1,0:T(8,128)S(1)}, u32[]{:S(2)}, u32[]{:S(2)}) collective-permute-start(f32[1,3,32,32]{3,2,1,0:T(8,128)S(1)} %slice.895), channel_id=1, source_target_pairs={{1,0},{2,1},{3,2},{4,3},{5,4},{6,5},{7,6},{8,7},{9,8},{10,9},{11,1... | collective-permute-start | bytes 36872 | tf_op jit(solution)/shard_map/ppermute | solution.py:21
  83.1 1.9 collective-permute-start.14
  86.4 4.9 %collective-permute-start.13 = (f32[4,3,1,512]{3,2,1,0:T(1,128)S(1)}, f32[4,3,1,512]{3,2,1,0:T(1,128)S(1)}, u32[]{:S(2)}, u32[]{:S(2)}) collective-permute-start(f32[4,3,1,512]{3,2,1,0:T(1,128)S(1)} %get-tuple-element.59), channel_id=1, source_target_pairs={{0,32},{32,64},{64,96},{96,128},{128,160},{160,192},{192,224},{224... | collective-permute-start | bytes 73736 | tf_op jit(solution)/shard_map/ppermute | solution.py:19
  94.0 5.7 %collective-permute-start.19 = (f32[1,3,32,32]{3,2,1,0:T(8,128)S(1)}, f32[1,3,32,32]{3,2,1,0:T(8,128)S(1)}, u32[]{:S(2)}, u32[]{:S(2)}) collective-permute-start(f32[1,3,32,32]{3,2,1,0:T(8,128)S(1)} %slice.905), channel_id=1, source_target_pairs={{1,0},{2,1},{3,2},{4,3},{5,4},{6,5},{7,6},{8,7},{9,8},{10,9},{11,1... | collective-permute-start | bytes 36872 | tf_op jit(solution)/shard_map/ppermute | solution.py:21
  99.7 1.9 collective-permute-start.18
  102.9 5.5 %collective-permute-start.17 = (f32[4,3,1,512]{3,2,1,0:T(1,128)S(1)}, f32[4,3,1,512]{3,2,1,0:T(1,128)S(1)}, u32[]{:S(2)}, u32[]{:S(2)}) collective-permute-start(f32[4,3,1,512]{3,2,1,0:T(1,128)S(1)} %get-tuple-element.51), channel_id=1, source_target_pairs={{0,32},{32,64},{64,96},{96,128},{128,160},{160,192},{192,224},{224... | collective-permute-start | bytes 73736 | tf_op jit(solution)/shard_map/ppermute | solution.py:19
  108.5 5.7 %collective-permute-start.22 = (f32[2,3,1,256]{3,2,1,0:T(1,128)}, f32[2,3,1,256]{3,2,1,0:T(1,128)}, u32[]{:S(2)}, u32[]{:S(2)}) collective-permute-start(f32[2,3,1,256]{3,2,1,0:T(1,128)} %broadcast.952), channel_id=1, source_target_pairs={{0,32},{32,64},{64,96},{96,128},{128,160},{160,192},{192,224},{224... | collective-permute-start | bytes 18440 | tf_op jit(solution)/shard_map/ppermute | solution.py:19
  119.2 5.4 %collective-permute-start.20 = (f32[4,16,128]{2,1,0:T(8,128)S(1)}, f32[4,16,128]{2,1,0:T(8,128)S(1)}, u32[]{:S(2)}, u32[]{:S(2)}) collective-permute-start(f32[4,16,128]{2,1,0:T(8,128)S(1)} %slice_bitcast_fusion.1), channel_id=1, source_target_pairs={{1,0},{2,1},{3,2},{4,3},{5,4},{6,5},{7,6},{8,7},{9,8},{10,9},{11,1... | collective-permute-start | bytes 98312 | tf_op jit(solution)/shard_map/ppermute | solution.py:31
  129.0 5.4 %collective-permute-start.28 = (f32[1,3,16,16]{3,2,1,0:T(8,128)S(1)}, f32[1,3,16,16]{3,2,1,0:T(8,128)S(1)}, u32[]{:S(2)}, u32[]{:S(2)}) collective-permute-start(f32[1,3,16,16]{3,2,1,0:T(8,128)S(1)} %get-tuple-element.134), channel_id=1, source_target_pairs={{1,0},{2,1},{3,2},{4,3},{5,4},{6,5},{7,6},{8,7},{9,8},{10,9},{11,1... | collective-permute-start | bytes 9224 | tf_op jit(solution)/shard_map/ppermute | solution.py:21
  134.5 1.9 collective-permute-start.27
  137.7 5.2 %collective-permute-start.26 = (f32[2,3,1,256]{3,2,1,0:T(1,128)S(1)}, f32[2,3,1,256]{3,2,1,0:T(1,128)S(1)}, u32[]{:S(2)}, u32[]{:S(2)}) collective-permute-start(f32[2,3,1,256]{3,2,1,0:T(1,128)S(1)} %get-tuple-element.138), channel_id=1, source_target_pairs={{0,32},{32,64},{64,96},{96,128},{128,160},{160,192},{192,224},{224... | collective-permute-start | bytes 18440 | tf_op jit(solution)/shard_map/ppermute | solution.py:19
  144.8 5.7 %collective-permute-start.32 = (f32[1,3,16,16]{3,2,1,0:T(8,128)S(1)}, f32[1,3,16,16]{3,2,1,0:T(8,128)S(1)}, u32[]{:S(2)}, u32[]{:S(2)}) collective-permute-start(f32[1,3,16,16]{3,2,1,0:T(8,128)S(1)} %get-tuple-element.125), channel_id=1, source_target_pairs={{1,0},{2,1},{3,2},{4,3},{5,4},{6,5},{7,6},{8,7},{9,8},{10,9},{11,1... | collective-permute-start | bytes 9224 | tf_op jit(solution)/shard_map/ppermute | solution.py:21
  153.8 5.8 %collective-permute-start.30 = (f32[2,3,1,256]{3,2,1,0:T(1,128)S(1)}, f32[2,3,1,256]{3,2,1,0:T(1,128)S(1)}, u32[]{:S(2)}, u32[]{:S(2)}) collective-permute-start(f32[2,3,1,256]{3,2,1,0:T(1,128)S(1)} %get-tuple-element.129), channel_id=1, source_target_pairs={{0,32},{32,64},{64,96},{96,128},{128,160},{160,192},{192,224},{224... | collective-permute-start | bytes 18440 | tf_op jit(solution)/shard_map/ppermute | solution.py:19
  160.8 5.7 %collective-permute-start.36 = (f32[1,3,16,16]{3,2,1,0:T(8,128)S(1)}, f32[1,3,16,16]{3,2,1,0:T(8,128)S(1)}, u32[]{:S(2)}, u32[]{:S(2)}) collective-permute-start(f32[1,3,16,16]{3,2,1,0:T(8,128)S(1)} %get-tuple-element.116), channel_id=1, source_target_pairs={{1,0},{2,1},{3,2},{4,3},{5,4},{6,5},{7,6},{8,7},{9,8},{10,9},{11,1... | collective-permute-start | bytes 9224 | tf_op jit(solution)/shard_map/ppermute | solution.py:21
  166.6 1.9 collective-permute-start.35
  169.8 4.5 %collective-permute-start.34 = (f32[2,3,1,256]{3,2,1,0:T(1,128)S(1)}, f32[2,3,1,256]{3,2,1,0:T(1,128)S(1)}, u32[]{:S(2)}, u32[]{:S(2)}) collective-permute-start(f32[2,3,1,256]{3,2,1,0:T(1,128)S(1)} %get-tuple-element.120), channel_id=1, source_target_pairs={{0,32},{32,64},{64,96},{96,128},{128,160},{160,192},{192,224},{224... | collective-permute-start | bytes 18440 | tf_op jit(solution)/shard_map/ppermute | solution.py:19
  175.6 5.7 %collective-permute-start.40 = (f32[1,3,16,16]{3,2,1,0:T(8,128)S(1)}, f32[1,3,16,16]{3,2,1,0:T(8,128)S(1)}, u32[]{:S(2)}, u32[]{:S(2)}) collective-permute-start(f32[1,3,16,16]{3,2,1,0:T(8,128)S(1)} %get-tuple-element.107), channel_id=1, source_target_pairs={{1,0},{2,1},{3,2},{4,3},{5,4},{6,5},{7,6},{8,7},{9,8},{10,9},{11,1... | collective-permute-start | bytes 9224 | tf_op jit(solution)/shard_map/ppermute | solution.py:21
  181.4 1.9 collective-permute-start.39
  184.6 5.4 %collective-permute-start.38 = (f32[2,3,1,256]{3,2,1,0:T(1,128)S(1)}, f32[2,3,1,256]{3,2,1,0:T(1,128)S(1)}, u32[]{:S(2)}, u32[]{:S(2)}) collective-permute-start(f32[2,3,1,256]{3,2,1,0:T(1,128)S(1)} %get-tuple-element.111), channel_id=1, source_target_pairs={{0,32},{32,64},{64,96},{96,128},{128,160},{160,192},{192,224},{224... | collective-permute-start | bytes 18440 | tf_op jit(solution)/shard_map/ppermute | solution.py:19
  191.3 5.7 %collective-permute-start.44 = (f32[1,3,16,16]{3,2,1,0:T(8,128)S(1)}, f32[1,3,16,16]{3,2,1,0:T(8,128)S(1)}, u32[]{:S(2)}, u32[]{:S(2)}) collective-permute-start(f32[1,3,16,16]{3,2,1,0:T(8,128)S(1)} %get-tuple-element.98), channel_id=1, source_target_pairs={{1,0},{2,1},{3,2},{4,3},{5,4},{6,5},{7,6},{8,7},{9,8},{10,9},{11,1... | collective-permute-start | bytes 9224 | tf_op jit(solution)/shard_map/ppermute | solution.py:21
  200.2 5.7 %collective-permute-start.42 = (f32[2,3,1,256]{3,2,1,0:T(1,128)S(1)}, f32[2,3,1,256]{3,2,1,0:T(1,128)S(1)}, u32[]{:S(2)}, u32[]{:S(2)}) collective-permute-start(f32[2,3,1,256]{3,2,1,0:T(1,128)S(1)} %get-tuple-element.102), channel_id=1, source_target_pairs={{0,32},{32,64},{64,96},{96,128},{128,160},{160,192},{192,224},{224... | collective-permute-start | bytes 18440 | tf_op jit(solution)/shard_map/ppermute | solution.py:19
  207.2 5.7 %collective-permute-start.48 = (f32[1,3,16,16]{3,2,1,0:T(8,128)S(1)}, f32[1,3,16,16]{3,2,1,0:T(8,128)S(1)}, u32[]{:S(2)}, u32[]{:S(2)}) collective-permute-start(f32[1,3,16,16]{3,2,1,0:T(8,128)S(1)} %get-tuple-element.89), channel_id=1, source_target_pairs={{1,0},{2,1},{3,2},{4,3},{5,4},{6,5},{7,6},{8,7},{9,8},{10,9},{11,1... | collective-permute-start | bytes 9224 | tf_op jit(solution)/shard_map/ppermute | solution.py:21
  216.2 5.7 %collective-permute-start.46 = (f32[2,3,1,256]{3,2,1,0:T(1,128)S(1)}, f32[2,3,1,256]{3,2,1,0:T(1,128)S(1)}, u32[]{:S(2)}, u32[]{:S(2)}) collective-permute-start(f32[2,3,1,256]{3,2,1,0:T(1,128)S(1)} %get-tuple-element.93), channel_id=1, source_target_pairs={{0,32},{32,64},{64,96},{96,128},{128,160},{160,192},{192,224},{224... | collective-permute-start | bytes 18440 | tf_op jit(solution)/shard_map/ppermute | solution.py:19
  223.2 5.7 %collective-permute-start.52 = (f32[1,3,16,16]{3,2,1,0:T(8,128)S(1)}, f32[1,3,16,16]{3,2,1,0:T(8,128)S(1)}, u32[]{:S(2)}, u32[]{:S(2)}) collective-permute-start(f32[1,3,16,16]{3,2,1,0:T(8,128)S(1)} %get-tuple-element.80), channel_id=1, source_target_pairs={{1,0},{2,1},{3,2},{4,3},{5,4},{6,5},{7,6},{8,7},{9,8},{10,9},{11,1... | collective-permute-start | bytes 9224 | tf_op jit(solution)/shard_map/ppermute | solution.py:21
  232.2 5.7 %collective-permute-start.50 = (f32[2,3,1,256]{3,2,1,0:T(1,128)S(1)}, f32[2,3,1,256]{3,2,1,0:T(1,128)S(1)}, u32[]{:S(2)}, u32[]{:S(2)}) collective-permute-start(f32[2,3,1,256]{3,2,1,0:T(1,128)S(1)} %get-tuple-element.84), channel_id=1, source_target_pairs={{0,32},{32,64},{64,96},{96,128},{128,160},{160,192},{192,224},{224... | collective-permute-start | bytes 18440 | tf_op jit(solution)/shard_map/ppermute | solution.py:19
  238.9 1.9 collective-permute-start.53
  241.6 4.5 %collective-permute-done.53 = f32[3,16,128]{2,1,0:T(8,128)S(1)} collective-permute-done((f32[3,16,128]{2,1,0:T(8,128)S(1)}, f32[3,16,128]{2,1,0:T(8,128)S(1)}, u32[]{:S(2)}, u32[]{:S(2)}) %collective-permute-start.53) | collective-permute-done | bytes 24608 | tf_op jit(solution)/shard_map/ppermute | solution.py:31
  249.3 4.2 collective-permute-start.57
  256.8 5.7 %collective-permute-start.55 = (f32[4,3,1,512]{3,2,1,0:T(1,128)S(1)}, f32[4,3,1,512]{3,2,1,0:T(1,128)S(1)}, u32[]{:S(2)}, u32[]{:S(2)}) collective-permute-start(f32[4,3,1,512]{3,2,1,0:T(1,128)S(1)} %get-tuple-element.43), channel_id=1, source_target_pairs={{0,32},{32,64},{64,96},{96,128},{128,160},{160,192},{192,224},{224... | collective-permute-start | bytes 73736 | tf_op jit(solution)/shard_map/ppermute | solution.py:19
  265.9 5.7 %collective-permute-start.61 = (f32[1,3,32,32]{3,2,1,0:T(8,128)S(1)}, f32[1,3,32,32]{3,2,1,0:T(8,128)S(1)}, u32[]{:S(2)}, u32[]{:S(2)}) collective-permute-start(f32[1,3,32,32]{3,2,1,0:T(8,128)S(1)} %slice.1001), channel_id=1, source_target_pairs={{1,0},{2,1},{3,2},{4,3},{5,4},{6,5},{7,6},{8,7},{9,8},{10,9},{11,1... | collective-permute-start | bytes 36872 | tf_op jit(solution)/shard_map/ppermute | solution.py:21
  271.7 1.9 collective-permute-start.60
  274.9 5.8 %collective-permute-start.59 = (f32[4,3,1,512]{3,2,1,0:T(1,128)S(1)}, f32[4,3,1,512]{3,2,1,0:T(1,128)S(1)}, u32[]{:S(2)}, u32[]{:S(2)}) collective-permute-start(f32[4,3,1,512]{3,2,1,0:T(1,128)S(1)} %get-tuple-element.35), channel_id=1, source_target_pairs={{0,32},{32,64},{64,96},{96,128},{128,160},{160,192},{192,224},{224... | collective-permute-start | bytes 73736 | tf_op jit(solution)/shard_map/ppermute | solution.py:19
  283.4 5.7 %collective-permute-start.65 = (f32[1,3,32,32]{3,2,1,0:T(8,128)S(1)}, f32[1,3,32,32]{3,2,1,0:T(8,128)S(1)}, u32[]{:S(2)}, u32[]{:S(2)}) collective-permute-start(f32[1,3,32,32]{3,2,1,0:T(8,128)S(1)} %slice.1011), channel_id=1, source_target_pairs={{1,0},{2,1},{3,2},{4,3},{5,4},{6,5},{7,6},{8,7},{9,8},{10,9},{11,1... | collective-permute-start | bytes 36872 | tf_op jit(solution)/shard_map/ppermute | solution.py:21
  292.4 5.8 %collective-permute-start.63 = (f32[4,3,1,512]{3,2,1,0:T(1,128)S(1)}, f32[4,3,1,512]{3,2,1,0:T(1,128)S(1)}, u32[]{:S(2)}, u32[]{:S(2)}) collective-permute-start(f32[4,3,1,512]{3,2,1,0:T(1,128)S(1)} %get-tuple-element.27), channel_id=1, source_target_pairs={{0,32},{32,64},{64,96},{96,128},{128,160},{160,192},{192,224},{224... | collective-permute-start | bytes 73736 | tf_op jit(solution)/shard_map/ppermute | solution.py:19
  300.9 5.7 %collective-permute-start.69 = (f32[1,3,32,32]{3,2,1,0:T(8,128)S(1)}, f32[1,3,32,32]{3,2,1,0:T(8,128)S(1)}, u32[]{:S(2)}, u32[]{:S(2)}) collective-permute-start(f32[1,3,32,32]{3,2,1,0:T(8,128)S(1)} %slice.1021), channel_id=1, source_target_pairs={{1,0},{2,1},{3,2},{4,3},{5,4},{6,5},{7,6},{8,7},{9,8},{10,9},{11,1... | collective-permute-start | bytes 36872 | tf_op jit(solution)/shard_map/ppermute | solution.py:21
  309.8 5.8 %collective-permute-start.67 = (f32[4,3,1,512]{3,2,1,0:T(1,128)S(1)}, f32[4,3,1,512]{3,2,1,0:T(1,128)S(1)}, u32[]{:S(2)}, u32[]{:S(2)}) collective-permute-start(f32[4,3,1,512]{3,2,1,0:T(1,128)S(1)} %get-tuple-element.13), channel_id=1, source_target_pairs={{0,32},{32,64},{64,96},{96,128},{128,160},{160,192},{192,224},{224... | collective-permute-start | bytes 73736 | tf_op jit(solution)/shard_map/ppermute | solution.py:19
  318.7 115.5 %psum.7 = f32[]{:T(128)} all-reduce(f32[]{:T(128)} %get-tuple-element.6), channel_id=1, replica_groups=mesh['gx'=16,'gy'=8,'gz'=4] {'gx','gy','gz'}, use_global_device_ids=true, to_apply=%region_4.6 | all-reduce | flops 1 | bytes 8 | tf_op jit(solution)/shard_map/psum | solution.py:185
  (344 shorter events, 96.3 us)
Async XLA Ops:
  0.7 39.8 %collective-permute-start.3 = (f32[1,3,32,32]{3,2,1,0:T(8,128)S(1)}, f32[1,3,32,32]{3,2,1,0:T(8,128)S(1)}, u32[]{:S(2)}, u32[]{:S(2)}) collective-permute-start(f32[1,3,32,32]{3,2,1,0:T(8,128)S(1)} %dynamic_slice.57), channel_id=1, source_target_pairs={{1,0},{2,1},{3,2},{4,3},{5,4},{6,5},{7,6},{8,7},{9,8},{10,9},{11,1... | collective-permute-start | bytes 36872 | tf_op jit(solution)/shard_map/ppermute | solution.py:21
  6.8 35.6 %collective-permute-start.2 = (f32[1,3,32,32]{3,2,1,0:T(8,128)S(1)}, f32[1,3,32,32]{3,2,1,0:T(8,128)S(1)}, u32[]{:S(2)}, u32[]{:S(2)}) collective-permute-start(f32[1,3,32,32]{3,2,1,0:T(8,128)S(1)} %dynamic_slice.57), channel_id=1, source_target_pairs={{0,1},{1,2},{2,3},{3,4},{4,5},{5,6},{6,7},{7,8},{8,9},{9,10},{10,1... | collective-permute-start | bytes 36872 | tf_op jit(solution)/shard_map/ppermute | solution.py:19
  8.8 33.6 %collective-permute-start = (f32[4,3,1,512]{3,2,1,0:T(1,128)S(1)}, f32[4,3,1,512]{3,2,1,0:T(1,128)S(1)}, u32[]{:S(2)}, u32[]{:S(2)}) collective-permute-start(f32[4,3,1,512]{3,2,1,0:T(1,128)S(1)} %broadcast.941), channel_id=1, source_target_pairs={{32,0},{64,32},{96,64},{128,96},{160,128},{192,160},{224,192},{256... | collective-permute-start | bytes 73736 | tf_op jit(solution)/shard_map/ppermute | solution.py:21
  10.1 32.3 %collective-permute-start.1 = (f32[4,3,1,512]{3,2,1,0:T(1,128)S(1)}, f32[4,3,1,512]{3,2,1,0:T(1,128)S(1)}, u32[]{:S(2)}, u32[]{:S(2)}) collective-permute-start(f32[4,3,1,512]{3,2,1,0:T(1,128)S(1)} %broadcast.941), channel_id=1, source_target_pairs={{0,32},{32,64},{64,96},{96,128},{128,160},{160,192},{192,224},{224... | collective-permute-start | bytes 73736 | tf_op jit(solution)/shard_map/ppermute | solution.py:19
  14.9 22.9 %collective-permute-start.24 = (f32[1,3,16,16]{3,2,1,0:T(8,128)}, f32[1,3,16,16]{3,2,1,0:T(8,128)S(1)}, u32[]{:S(2)}, u32[]{:S(2)}) collective-permute-start(f32[1,3,16,16]{3,2,1,0:T(8,128)} %dynamic_slice.62), channel_id=1, source_target_pairs={{1,0},{2,1},{3,2},{4,3},{5,4},{6,5},{7,6},{8,7},{9,8},{10,9},{11,1... | collective-permute-start | bytes 9224 | tf_op jit(solution)/shard_map/ppermute | solution.py:21
  37.8 89.2 %collective-permute-start.23 = (f32[1,3,16,16]{3,2,1,0:T(8,128)}, f32[1,3,16,16]{3,2,1,0:T(8,128)}, u32[]{:S(2)}, u32[]{:S(2)}) collective-permute-start(f32[1,3,16,16]{3,2,1,0:T(8,128)} %dynamic_slice.62), channel_id=1, source_target_pairs={{0,1},{1,2},{2,3},{3,4},{4,5},{5,6},{6,7},{7,8},{8,9},{9,10},{10,1... | collective-permute-start | bytes 9224 | tf_op jit(solution)/shard_map/ppermute | solution.py:19
  41.0 86.0 %collective-permute-start.21 = (f32[2,3,1,256]{3,2,1,0:T(1,128)}, f32[2,3,1,256]{3,2,1,0:T(1,128)}, u32[]{:S(2)}, u32[]{:S(2)}) collective-permute-start(f32[2,3,1,256]{3,2,1,0:T(1,128)} %broadcast.952), channel_id=1, source_target_pairs={{32,0},{64,32},{96,64},{128,96},{160,128},{192,160},{224,192},{256... | collective-permute-start | bytes 18440 | tf_op jit(solution)/shard_map/ppermute | solution.py:21
  45.2 8.2 %collective-permute-start.7 = (f32[1,3,32,32]{3,2,1,0:T(8,128)S(1)}, f32[1,3,32,32]{3,2,1,0:T(8,128)S(1)}, u32[]{:S(2)}, u32[]{:S(2)}) collective-permute-start(f32[1,3,32,32]{3,2,1,0:T(8,128)S(1)} %slice.875), channel_id=1, source_target_pairs={{1,0},{2,1},{3,2},{4,3},{5,4},{6,5},{7,6},{8,7},{9,8},{10,9},{11,1... | collective-permute-start | bytes 36872 | tf_op jit(solution)/shard_map/ppermute | solution.py:21
  50.2 8.2 %collective-permute-start.6 = (f32[1,3,32,32]{3,2,1,0:T(8,128)S(1)}, f32[1,3,32,32]{3,2,1,0:T(8,128)S(1)}, u32[]{:S(2)}, u32[]{:S(2)}) collective-permute-start(f32[1,3,32,32]{3,2,1,0:T(8,128)S(1)} %constant_dynamic-slice_fusion.14), channel_id=1, source_target_pairs={{0,1},{1,2},{2,3},{3,4},{4,5},{5,6},{6,7},{7,8},{8,9},{9,10},{10,1... | collective-permute-start | bytes 36872 | tf_op jit(solution)/shard_map/ppermute | solution.py:19
  61.1 9.0 %collective-permute-start.11 = (f32[1,3,32,32]{3,2,1,0:T(8,128)S(1)}, f32[1,3,32,32]{3,2,1,0:T(8,128)S(1)}, u32[]{:S(2)}, u32[]{:S(2)}) collective-permute-start(f32[1,3,32,32]{3,2,1,0:T(8,128)S(1)} %slice.885), channel_id=1, source_target_pairs={{1,0},{2,1},{3,2},{4,3},{5,4},{6,5},{7,6},{8,7},{9,8},{10,9},{11,1... | collective-permute-start | bytes 36872 | tf_op jit(solution)/shard_map/ppermute | solution.py:21
  66.9 7.9 %collective-permute-start.10 = (f32[1,3,32,32]{3,2,1,0:T(8,128)S(1)}, f32[1,3,32,32]{3,2,1,0:T(8,128)S(1)}, u32[]{:S(2)}, u32[]{:S(2)}) collective-permute-start(f32[1,3,32,32]{3,2,1,0:T(8,128)S(1)} %constant_dynamic-slice_fusion.13), channel_id=1, source_target_pairs={{0,1},{1,2},{2,3},{3,4},{4,5},{5,6},{6,7},{7,8},{8,9},{9,10},{10,1... | collective-permute-start | bytes 36872 | tf_op jit(solution)/shard_map/ppermute | solution.py:19
  77.4 9.0 %collective-permute-start.15 = (f32[1,3,32,32]{3,2,1,0:T(8,128)S(1)}, f32[1,3,32,32]{3,2,1,0:T(8,128)S(1)}, u32[]{:S(2)}, u32[]{:S(2)}) collective-permute-start(f32[1,3,32,32]{3,2,1,0:T(8,128)S(1)} %slice.895), channel_id=1, source_target_pairs={{1,0},{2,1},{3,2},{4,3},{5,4},{6,5},{7,6},{8,7},{9,8},{10,9},{11,1... | collective-permute-start | bytes 36872 | tf_op jit(solution)/shard_map/ppermute | solution.py:21
  83.1 8.2 %collective-permute-start.14 = (f32[1,3,32,32]{3,2,1,0:T(8,128)S(1)}, f32[1,3,32,32]{3,2,1,0:T(8,128)S(1)}, u32[]{:S(2)}, u32[]{:S(2)}) collective-permute-start(f32[1,3,32,32]{3,2,1,0:T(8,128)S(1)} %constant_dynamic-slice_fusion.12), channel_id=1, source_target_pairs={{0,1},{1,2},{2,3},{3,4},{4,5},{5,6},{6,7},{7,8},{8,9},{9,10},{10,1... | collective-permute-start | bytes 36872 | tf_op jit(solution)/shard_map/ppermute | solution.py:19
  94.0 9.0 %collective-permute-start.19 = (f32[1,3,32,32]{3,2,1,0:T(8,128)S(1)}, f32[1,3,32,32]{3,2,1,0:T(8,128)S(1)}, u32[]{:S(2)}, u32[]{:S(2)}) collective-permute-start(f32[1,3,32,32]{3,2,1,0:T(8,128)S(1)} %slice.905), channel_id=1, source_target_pairs={{1,0},{2,1},{3,2},{4,3},{5,4},{6,5},{7,6},{8,7},{9,8},{10,9},{11,1... | collective-permute-start | bytes 36872 | tf_op jit(solution)/shard_map/ppermute | solution.py:21
  99.7 8.8 %collective-permute-start.18 = (f32[1,3,32,32]{3,2,1,0:T(8,128)S(1)}, f32[1,3,32,32]{3,2,1,0:T(8,128)S(1)}, u32[]{:S(2)}, u32[]{:S(2)}) collective-permute-start(f32[1,3,32,32]{3,2,1,0:T(8,128)S(1)} %constant_dynamic-slice_fusion.11), channel_id=1, source_target_pairs={{0,1},{1,2},{2,3},{3,4},{4,5},{5,6},{6,7},{7,8},{8,9},{9,10},{10,1... | collective-permute-start | bytes 36872 | tf_op jit(solution)/shard_map/ppermute | solution.py:19
  101.6 12.6 %collective-permute-start.16 = (f32[4,3,1,512]{3,2,1,0:T(1,128)S(1)}, f32[4,3,1,512]{3,2,1,0:T(1,128)S(1)}, u32[]{:S(2)}, u32[]{:S(2)}) collective-permute-start(f32[4,3,1,512]{3,2,1,0:T(1,128)S(1)} %get-tuple-element.50), channel_id=1, source_target_pairs={{32,0},{64,32},{96,64},{128,96},{160,128},{192,160},{224,192},{256... | collective-permute-start | bytes 73736 | tf_op jit(solution)/shard_map/ppermute | solution.py:21
  102.9 11.3 %collective-permute-start.17 = (f32[4,3,1,512]{3,2,1,0:T(1,128)S(1)}, f32[4,3,1,512]{3,2,1,0:T(1,128)S(1)}, u32[]{:S(2)}, u32[]{:S(2)}) collective-permute-start(f32[4,3,1,512]{3,2,1,0:T(1,128)S(1)} %get-tuple-element.51), channel_id=1, source_target_pairs={{0,32},{32,64},{64,96},{96,128},{128,160},{160,192},{192,224},{224... | collective-permute-start | bytes 73736 | tf_op jit(solution)/shard_map/ppermute | solution.py:19
  108.5 18.5 %collective-permute-start.22 = (f32[2,3,1,256]{3,2,1,0:T(1,128)}, f32[2,3,1,256]{3,2,1,0:T(1,128)}, u32[]{:S(2)}, u32[]{:S(2)}) collective-permute-start(f32[2,3,1,256]{3,2,1,0:T(1,128)} %broadcast.952), channel_id=1, source_target_pairs={{0,32},{32,64},{64,96},{96,128},{128,160},{160,192},{192,224},{224... | collective-permute-start | bytes 18440 | tf_op jit(solution)/shard_map/ppermute | solution.py:19
  129.0 13.9 %collective-permute-start.28 = (f32[1,3,16,16]{3,2,1,0:T(8,128)S(1)}, f32[1,3,16,16]{3,2,1,0:T(8,128)S(1)}, u32[]{:S(2)}, u32[]{:S(2)}) collective-permute-start(f32[1,3,16,16]{3,2,1,0:T(8,128)S(1)} %get-tuple-element.134), channel_id=1, source_target_pairs={{1,0},{2,1},{3,2},{4,3},{5,4},{6,5},{7,6},{8,7},{9,8},{10,9},{11,1... | collective-permute-start | bytes 9224 | tf_op jit(solution)/shard_map/ppermute | solution.py:21
  134.5 9.1 %collective-permute-start.27 = (f32[1,3,16,16]{3,2,1,0:T(8,128)S(1)}, f32[1,3,16,16]{3,2,1,0:T(8,128)S(1)}, u32[]{:S(2)}, u32[]{:S(2)}) collective-permute-start(f32[1,3,16,16]{3,2,1,0:T(8,128)S(1)} %constant_dynamic-slice_fusion.10), channel_id=1, source_target_pairs={{0,1},{1,2},{2,3},{3,4},{4,5},{5,6},{6,7},{7,8},{8,9},{9,10},{10,1... | collective-permute-start | bytes 9224 | tf_op jit(solution)/shard_map/ppermute | solution.py:19
  136.4 7.2 %collective-permute-start.25 = (f32[2,3,1,256]{3,2,1,0:T(1,128)S(1)}, f32[2,3,1,256]{3,2,1,0:T(1,128)S(1)}, u32[]{:S(2)}, u32[]{:S(2)}) collective-permute-start(f32[2,3,1,256]{3,2,1,0:T(1,128)S(1)} %get-tuple-element.137), channel_id=1, source_target_pairs={{32,0},{64,32},{96,64},{128,96},{160,128},{192,160},{224,192},{256... | collective-permute-start | bytes 18440 | tf_op jit(solution)/shard_map/ppermute | solution.py:21
  144.8 14.7 %collective-permute-start.32 = (f32[1,3,16,16]{3,2,1,0:T(8,128)S(1)}, f32[1,3,16,16]{3,2,1,0:T(8,128)S(1)}, u32[]{:S(2)}, u32[]{:S(2)}) collective-permute-start(f32[1,3,16,16]{3,2,1,0:T(8,128)S(1)} %get-tuple-element.125), channel_id=1, source_target_pairs={{1,0},{2,1},{3,2},{4,3},{5,4},{6,5},{7,6},{8,7},{9,8},{10,9},{11,1... | collective-permute-start | bytes 9224 | tf_op jit(solution)/shard_map/ppermute | solution.py:21
  150.6 9.1 %collective-permute-start.31 = (f32[1,3,16,16]{3,2,1,0:T(8,128)S(1)}, f32[1,3,16,16]{3,2,1,0:T(8,128)S(1)}, u32[]{:S(2)}, u32[]{:S(2)}) collective-permute-start(f32[1,3,16,16]{3,2,1,0:T(8,128)S(1)} %constant_dynamic-slice_fusion.9), channel_id=1, source_target_pairs={{0,1},{1,2},{2,3},{3,4},{4,5},{5,6},{6,7},{7,8},{8,9},{9,10},{10,1... | collective-permute-start | bytes 9224 | tf_op jit(solution)/shard_map/ppermute | solution.py:19
  152.5 7.2 %collective-permute-start.29 = (f32[2,3,1,256]{3,2,1,0:T(1,128)S(1)}, f32[2,3,1,256]{3,2,1,0:T(1,128)S(1)}, u32[]{:S(2)}, u32[]{:S(2)}) collective-permute-start(f32[2,3,1,256]{3,2,1,0:T(1,128)S(1)} %get-tuple-element.128), channel_id=1, source_target_pairs={{32,0},{64,32},{96,64},{128,96},{160,128},{192,160},{224,192},{256... | collective-permute-start | bytes 18440 | tf_op jit(solution)/shard_map/ppermute | solution.py:21
  160.8 13.5 %collective-permute-start.36 = (f32[1,3,16,16]{3,2,1,0:T(8,128)S(1)}, f32[1,3,16,16]{3,2,1,0:T(8,128)S(1)}, u32[]{:S(2)}, u32[]{:S(2)}) collective-permute-start(f32[1,3,16,16]{3,2,1,0:T(8,128)S(1)} %get-tuple-element.116), channel_id=1, source_target_pairs={{1,0},{2,1},{3,2},{4,3},{5,4},{6,5},{7,6},{8,7},{9,8},{10,9},{11,1... | collective-permute-start | bytes 9224 | tf_op jit(solution)/shard_map/ppermute | solution.py:21
  166.6 7.9 %collective-permute-start.35 = (f32[1,3,16,16]{3,2,1,0:T(8,128)S(1)}, f32[1,3,16,16]{3,2,1,0:T(8,128)S(1)}, u32[]{:S(2)}, u32[]{:S(2)}) collective-permute-start(f32[1,3,16,16]{3,2,1,0:T(8,128)S(1)} %constant_dynamic-slice_fusion.8), channel_id=1, source_target_pairs={{0,1},{1,2},{2,3},{3,4},{4,5},{5,6},{6,7},{7,8},{8,9},{9,10},{10,1... | collective-permute-start | bytes 9224 | tf_op jit(solution)/shard_map/ppermute | solution.py:19
  175.6 14.4 %collective-permute-start.40 = (f32[1,3,16,16]{3,2,1,0:T(8,128)S(1)}, f32[1,3,16,16]{3,2,1,0:T(8,128)S(1)}, u32[]{:S(2)}, u32[]{:S(2)}) collective-permute-start(f32[1,3,16,16]{3,2,1,0:T(8,128)S(1)} %get-tuple-element.107), channel_id=1, source_target_pairs={{1,0},{2,1},{3,2},{4,3},{5,4},{6,5},{7,6},{8,7},{9,8},{10,9},{11,1... | collective-permute-start | bytes 9224 | tf_op jit(solution)/shard_map/ppermute | solution.py:21
  181.4 8.7 %collective-permute-start.39 = (f32[1,3,16,16]{3,2,1,0:T(8,128)S(1)}, f32[1,3,16,16]{3,2,1,0:T(8,128)S(1)}, u32[]{:S(2)}, u32[]{:S(2)}) collective-permute-start(f32[1,3,16,16]{3,2,1,0:T(8,128)S(1)} %constant_dynamic-slice_fusion.7), channel_id=1, source_target_pairs={{0,1},{1,2},{2,3},{3,4},{4,5},{5,6},{6,7},{7,8},{8,9},{9,10},{10,1... | collective-permute-start | bytes 9224 | tf_op jit(solution)/shard_map/ppermute | solution.py:19
  191.3 14.7 %collective-permute-start.44 = (f32[1,3,16,16]{3,2,1,0:T(8,128)S(1)}, f32[1,3,16,16]{3,2,1,0:T(8,128)S(1)}, u32[]{:S(2)}, u32[]{:S(2)}) collective-permute-start(f32[1,3,16,16]{3,2,1,0:T(8,128)S(1)} %get-tuple-element.98), channel_id=1, source_target_pairs={{1,0},{2,1},{3,2},{4,3},{5,4},{6,5},{7,6},{8,7},{9,8},{10,9},{11,1... | collective-permute-start | bytes 9224 | tf_op jit(solution)/shard_map/ppermute | solution.py:21
  197.0 9.1 %collective-permute-start.43 = (f32[1,3,16,16]{3,2,1,0:T(8,128)S(1)}, f32[1,3,16,16]{3,2,1,0:T(8,128)S(1)}, u32[]{:S(2)}, u32[]{:S(2)}) collective-permute-start(f32[1,3,16,16]{3,2,1,0:T(8,128)S(1)} %constant_dynamic-slice_fusion.6), channel_id=1, source_target_pairs={{0,1},{1,2},{2,3},{3,4},{4,5},{5,6},{6,7},{7,8},{8,9},{9,10},{10,1... | collective-permute-start | bytes 9224 | tf_op jit(solution)/shard_map/ppermute | solution.py:19
  207.2 14.7 %collective-permute-start.48 = (f32[1,3,16,16]{3,2,1,0:T(8,128)S(1)}, f32[1,3,16,16]{3,2,1,0:T(8,128)S(1)}, u32[]{:S(2)}, u32[]{:S(2)}) collective-permute-start(f32[1,3,16,16]{3,2,1,0:T(8,128)S(1)} %get-tuple-element.89), channel_id=1, source_target_pairs={{1,0},{2,1},{3,2},{4,3},{5,4},{6,5},{7,6},{8,7},{9,8},{10,9},{11,1... | collective-permute-start | bytes 9224 | tf_op jit(solution)/shard_map/ppermute | solution.py:21
  213.0 9.1 %collective-permute-start.47 = (f32[1,3,16,16]{3,2,1,0:T(8,128)S(1)}, f32[1,3,16,16]{3,2,1,0:T(8,128)S(1)}, u32[]{:S(2)}, u32[]{:S(2)}) collective-permute-start(f32[1,3,16,16]{3,2,1,0:T(8,128)S(1)} %constant_dynamic-slice_fusion.5), channel_id=1, source_target_pairs={{0,1},{1,2},{2,3},{3,4},{4,5},{5,6},{6,7},{7,8},{8,9},{9,10},{10,1... | collective-permute-start | bytes 9224 | tf_op jit(solution)/shard_map/ppermute | solution.py:19
  214.9 7.1 %collective-permute-start.45 = (f32[2,3,1,256]{3,2,1,0:T(1,128)S(1)}, f32[2,3,1,256]{3,2,1,0:T(1,128)S(1)}, u32[]{:S(2)}, u32[]{:S(2)}) collective-permute-start(f32[2,3,1,256]{3,2,1,0:T(1,128)S(1)} %get-tuple-element.92), channel_id=1, source_target_pairs={{32,0},{64,32},{96,64},{128,96},{160,128},{192,160},{224,192},{256... | collective-permute-start | bytes 18440 | tf_op jit(solution)/shard_map/ppermute | solution.py:21
  223.2 14.7 %collective-permute-start.52 = (f32[1,3,16,16]{3,2,1,0:T(8,128)S(1)}, f32[1,3,16,16]{3,2,1,0:T(8,128)S(1)}, u32[]{:S(2)}, u32[]{:S(2)}) collective-permute-start(f32[1,3,16,16]{3,2,1,0:T(8,128)S(1)} %get-tuple-element.80), channel_id=1, source_target_pairs={{1,0},{2,1},{3,2},{4,3},{5,4},{6,5},{7,6},{8,7},{9,8},{10,9},{11,1... | collective-permute-start | bytes 9224 | tf_op jit(solution)/shard_map/ppermute | solution.py:21
  229.0 9.1 %collective-permute-start.51 = (f32[1,3,16,16]{3,2,1,0:T(8,128)S(1)}, f32[1,3,16,16]{3,2,1,0:T(8,128)S(1)}, u32[]{:S(2)}, u32[]{:S(2)}) collective-permute-start(f32[1,3,16,16]{3,2,1,0:T(8,128)S(1)} %constant_dynamic-slice_fusion.4), channel_id=1, source_target_pairs={{0,1},{1,2},{2,3},{3,4},{4,5},{5,6},{6,7},{7,8},{8,9},{9,10},{10,1... | collective-permute-start | bytes 9224 | tf_op jit(solution)/shard_map/ppermute | solution.py:19
  238.9 7.2 %collective-permute-start.53 = (f32[3,16,128]{2,1,0:T(8,128)S(1)}, f32[3,16,128]{2,1,0:T(8,128)S(1)}, u32[]{:S(2)}, u32[]{:S(2)}) collective-permute-start(f32[3,16,128]{2,1,0:T(8,128)S(1)} %slice.982), channel_id=1, source_target_pairs={{0,1},{1,2},{2,3},{3,4},{4,5},{5,6},{6,7},{7,8},{8,9},{9,10},{10,1... | collective-permute-start | bytes 73736 | tf_op jit(solution)/shard_map/ppermute | solution.py:31
  249.3 13.2 %collective-permute-start.57 = (f32[1,3,32,32]{3,2,1,0:T(8,128)S(1)}, f32[1,3,32,32]{3,2,1,0:T(8,128)S(1)}, u32[]{:S(2)}, u32[]{:S(2)}) collective-permute-start(f32[1,3,32,32]{3,2,1,0:T(8,128)S(1)} %slice.991), channel_id=1, source_target_pairs={{1,0},{2,1},{3,2},{4,3},{5,4},{6,5},{7,6},{8,7},{9,8},{10,9},{11,1... | collective-permute-start | bytes 36872 | tf_op jit(solution)/shard_map/ppermute | solution.py:21
  253.6 9.7 %collective-permute-start.56 = (f32[1,3,32,32]{3,2,1,0:T(8,128)S(1)}, f32[1,3,32,32]{3,2,1,0:T(8,128)S(1)}, u32[]{:S(2)}, u32[]{:S(2)}) collective-permute-start(f32[1,3,32,32]{3,2,1,0:T(8,128)S(1)} %constant_dynamic-slice_fusion.3), channel_id=1, source_target_pairs={{0,1},{1,2},{2,3},{3,4},{4,5},{5,6},{6,7},{7,8},{8,9},{9,10},{10,1... | collective-permute-start | bytes 36872 | tf_op jit(solution)/shard_map/ppermute | solution.py:19
  255.5 7.8 %collective-permute-start.54 = (f32[4,3,1,512]{3,2,1,0:T(1,128)S(1)}, f32[4,3,1,512]{3,2,1,0:T(1,128)S(1)}, u32[]{:S(2)}, u32[]{:S(2)}) collective-permute-start(f32[4,3,1,512]{3,2,1,0:T(1,128)S(1)} %get-tuple-element.42), channel_id=1, source_target_pairs={{32,0},{64,32},{96,64},{128,96},{160,128},{192,160},{224,192},{256... | collective-permute-start | bytes 73736 | tf_op jit(solution)/shard_map/ppermute | solution.py:21
  265.9 14.7 %collective-permute-start.61 = (f32[1,3,32,32]{3,2,1,0:T(8,128)S(1)}, f32[1,3,32,32]{3,2,1,0:T(8,128)S(1)}, u32[]{:S(2)}, u32[]{:S(2)}) collective-permute-start(f32[1,3,32,32]{3,2,1,0:T(8,128)S(1)} %slice.1001), channel_id=1, source_target_pairs={{1,0},{2,1},{3,2},{4,3},{5,4},{6,5},{7,6},{8,7},{9,8},{10,9},{11,1... | collective-permute-start | bytes 36872 | tf_op jit(solution)/shard_map/ppermute | solution.py:21
  271.7 9.1 %collective-permute-start.60 = (f32[1,3,32,32]{3,2,1,0:T(8,128)S(1)}, f32[1,3,32,32]{3,2,1,0:T(8,128)S(1)}, u32[]{:S(2)}, u32[]{:S(2)}) collective-permute-start(f32[1,3,32,32]{3,2,1,0:T(8,128)S(1)} %constant_dynamic-slice_fusion.2), channel_id=1, source_target_pairs={{0,1},{1,2},{2,3},{3,4},{4,5},{5,6},{6,7},{7,8},{8,9},{9,10},{10,1... | collective-permute-start | bytes 36872 | tf_op jit(solution)/shard_map/ppermute | solution.py:19
  273.6 7.2 %collective-permute-start.58 = (f32[4,3,1,512]{3,2,1,0:T(1,128)S(1)}, f32[4,3,1,512]{3,2,1,0:T(1,128)S(1)}, u32[]{:S(2)}, u32[]{:S(2)}) collective-permute-start(f32[4,3,1,512]{3,2,1,0:T(1,128)S(1)} %get-tuple-element.34), channel_id=1, source_target_pairs={{32,0},{64,32},{96,64},{128,96},{160,128},{192,160},{224,192},{256... | collective-permute-start | bytes 73736 | tf_op jit(solution)/shard_map/ppermute | solution.py:21
  283.4 14.7 %collective-permute-start.65 = (f32[1,3,32,32]{3,2,1,0:T(8,128)S(1)}, f32[1,3,32,32]{3,2,1,0:T(8,128)S(1)}, u32[]{:S(2)}, u32[]{:S(2)}) collective-permute-start(f32[1,3,32,32]{3,2,1,0:T(8,128)S(1)} %slice.1011), channel_id=1, source_target_pairs={{1,0},{2,1},{3,2},{4,3},{5,4},{6,5},{7,6},{8,7},{9,8},{10,9},{11,1... | collective-permute-start | bytes 36872 | tf_op jit(solution)/shard_map/ppermute | solution.py:21
  289.1 9.1 %collective-permute-start.64 = (f32[1,3,32,32]{3,2,1,0:T(8,128)S(1)}, f32[1,3,32,32]{3,2,1,0:T(8,128)S(1)}, u32[]{:S(2)}, u32[]{:S(2)}) collective-permute-start(f32[1,3,32,32]{3,2,1,0:T(8,128)S(1)} %constant_dynamic-slice_fusion.1), channel_id=1, source_target_pairs={{0,1},{1,2},{2,3},{3,4},{4,5},{5,6},{6,7},{7,8},{8,9},{9,10},{10,1... | collective-permute-start | bytes 36872 | tf_op jit(solution)/shard_map/ppermute | solution.py:19
  291.1 7.2 %collective-permute-start.62 = (f32[4,3,1,512]{3,2,1,0:T(1,128)S(1)}, f32[4,3,1,512]{3,2,1,0:T(1,128)S(1)}, u32[]{:S(2)}, u32[]{:S(2)}) collective-permute-start(f32[4,3,1,512]{3,2,1,0:T(1,128)S(1)} %get-tuple-element.26), channel_id=1, source_target_pairs={{32,0},{64,32},{96,64},{128,96},{160,128},{192,160},{224,192},{256... | collective-permute-start | bytes 73736 | tf_op jit(solution)/shard_map/ppermute | solution.py:21
  300.9 14.7 %collective-permute-start.69 = (f32[1,3,32,32]{3,2,1,0:T(8,128)S(1)}, f32[1,3,32,32]{3,2,1,0:T(8,128)S(1)}, u32[]{:S(2)}, u32[]{:S(2)}) collective-permute-start(f32[1,3,32,32]{3,2,1,0:T(8,128)S(1)} %slice.1021), channel_id=1, source_target_pairs={{1,0},{2,1},{3,2},{4,3},{5,4},{6,5},{7,6},{8,7},{9,8},{10,9},{11,1... | collective-permute-start | bytes 36872 | tf_op jit(solution)/shard_map/ppermute | solution.py:21
  306.6 9.1 %collective-permute-start.68 = (f32[1,3,32,32]{3,2,1,0:T(8,128)S(1)}, f32[1,3,32,32]{3,2,1,0:T(8,128)S(1)}, u32[]{:S(2)}, u32[]{:S(2)}) collective-permute-start(f32[1,3,32,32]{3,2,1,0:T(8,128)S(1)} %constant_dynamic-slice_fusion), channel_id=1, source_target_pairs={{0,1},{1,2},{2,3},{3,4},{4,5},{5,6},{6,7},{7,8},{8,9},{9,10},{10,1... | collective-permute-start | bytes 36872 | tf_op jit(solution)/shard_map/ppermute | solution.py:19
  308.5 7.2 %collective-permute-start.66 = (f32[4,3,1,512]{3,2,1,0:T(1,128)S(1)}, f32[4,3,1,512]{3,2,1,0:T(1,128)S(1)}, u32[]{:S(2)}, u32[]{:S(2)}) collective-permute-start(f32[4,3,1,512]{3,2,1,0:T(1,128)S(1)} %get-tuple-element.12), channel_id=1, source_target_pairs={{32,0},{64,32},{96,64},{128,96},{160,128},{192,160},{224,192},{256... | collective-permute-start | bytes 73736 | tf_op jit(solution)/shard_map/ppermute | solution.py:21
  (55 other events, 901.1 us)
where the time goes:
time: 439 us; the launch traced here: 436 us
  starting transfers between devices  247 us (56%)
  blocking collectives  116 us (26%)
  other arithmetic  26.9 us (6%)
  local copies, waits for them, and re-layouts  22.6 us (5%)
  waiting for transfers between devices  13.9 us (3%)
  between operations  7.82 us (2%)
    ppermute x34, starting transfers between devices, padded_2(): lax.ppermute(tail, axis, [(i, (i + 1) % count) for i in range(ends)])  124 us
    ppermute x34, starting transfers between devices, padded_2(): lax.ppermute(head, axis, [((i + 1) % count, i) for i in range(ends)])  116 us
    psum x1, blocking collectives, per_device(): dot_total = lax.psum(local_dot, ('gx', 'gy', 'gz'))  116 us
    ppermute x34, waiting for transfers between devices, padded_2(): lax.ppermute(tail, axis, [(i, (i + 1) % count) for i in range(ends)])  9.14 us
  transfers between devices with their start and end apart: 70, of which 15 were waited for; matrix products, arithmetic and copies ran while one was open for 7% of the time, Pallas kernels for 0%

commit v1 on v0

v1 whole, which is shorter than its diff:
```python
import functools

import jax
import jax.numpy as jnp
from jax import lax
from jax.experimental import pallas as pl
from jax.experimental.pallas import tpu as pltpu
from jax.sharding import PartitionSpec as P

GROUP_AXES = ("gy", "gz")
F32 = jnp.float32
BF16 = jnp.bfloat16
VMEM_BYTES = 48 * 1024 * 1024

SLOTS = 4
TILES = 2 * SLOTS
ROWS = 48
WIDE = TILES + 4
COWN = 16
CHALO = 10
CROWS = COWN + 2 * CHALO
CWIDE = SLOTS + 6


def iota(shape, dim):
    return lax.broadcasted_iota(jnp.int32, shape, dim)


def exact_dot(values, ones):
    high = values.astype(BF16)
    rest = values - high.astype(F32)
    mid = rest.astype(BF16)
    low = (rest - mid.astype(F32)).astype(BF16)
    total = jnp.dot(low, ones, preferred_element_type=F32)
    total = total + jnp.dot(mid, ones, preferred_element_type=F32)
    return total + jnp.dot(high, ones, preferred_element_type=F32)


def split_matrix():
    source, target = iota((256, 256), 0), iota((256, 256), 1)
    y = source % 32
    wanted = (y % 2) * 128 + source // 32 * 16 + y // 2
    return (target == wanted).astype(F32).astype(BF16)


def merge_matrix():
    source, target = iota((256, 256), 0), iota((256, 256), 1)
    y = target % 32
    wanted = (y % 2) * 128 + target // 32 * 16 + y // 2
    return (source == wanted).astype(F32).astype(BF16)


def pool_matrix():
    source, target = iota((256, 128), 0), iota((256, 128), 1)
    wanted = source // 32 * 16 + source % 16
    return (target == wanted).astype(F32).astype(BF16)


def spread_matrix():
    source, target = iota((128, 256), 0), iota((128, 256), 1)
    wanted = target // 32 * 16 + target % 16
    return (source == wanted).astype(F32).astype(BF16)


def even_cells(rows):
    shape = (rows, 128)
    return (iota(shape, 0) + iota(shape, 1) // 16) % 2 == 0


def pack_kernel(count, right, coef, above, below, packed, left_edge, right_edge):
    slot = pl.program_id(0)
    live = slot < count[0]
    split = split_matrix()
    even = even_cells(4 * ROWS)
    for half in range(2):
        lanes = slice(256 * half, 256 * half + 256)
        parts = []
        for m in range(4):
            own = right[0, m, :, lanes] if m < 3 else coef[0, :, lanes]
            parts += [above[0, m, :, lanes], own, below[0, m, :, lanes]]
        cells = jnp.where(live, jnp.concatenate(parts, axis=0), 0.0)
        both = exact_dot(cells, split)
        first, second = both[:, :128], both[:, 128:]
        red = jnp.where(even, first, second)
        black = jnp.where(even, second, first)
        for m in range(4):
            rows = slice(ROWS * m, ROWS * m + ROWS)
            packed[m, 0, half] = red[rows]
            packed[m, 1, half] = black[rows]

    @pl.when(slot == 0)
    def _():
        left_edge[...] = packed[:, :, 0]

    @pl.when(slot == count[0] - 1)
    def _():
        right_edge[...] = packed[:, :, 1]


def load_fine(count, factor, packed, from_left, from_right, scaled, ratio):
    def put(tile, take):
        out = []
        for colour in range(2):
            coef = take(3, colour)
            inside = coef > 0.0
            for m in range(3):
                inverse = jnp.where(inside, 1.0 / (coef + 6.0 * factor[m]), 0.0)
                out.append((m, colour, take(m, colour) * inverse, factor[m] * inverse))
        for m, colour, first, second in out:
            scaled[m, colour, tile] = first
            ratio[m, colour, tile] = second

    def own(tile, carry):
        put(tile + 2, lambda m, colour: packed[m, colour, tile])
        return carry

    lax.fori_loop(0, TILES, own, 0)
    put(1, lambda m, colour: from_left[m, colour])
    none = jnp.zeros((3, 2, ROWS, 128), F32)
    for tile in (0, WIDE - 2, WIDE - 1):
        scaled[:, :, tile] = none
        ratio[:, :, tile] = none
    put(2 * count + 2, lambda m, colour: from_right[m, colour])


def fine_update(other, scaled, ratio, m, colour, tile, chunk, masks):
    lane_low, lane_high, even, edges = masks
    row = 8 + 8 * chunk
    here = other[m, tile, row : row + 8]
    total = here + other[m, tile, row - 1 : row + 7]
    total = total + other[m, tile, row + 1 : row + 9]
    before = other[m, tile - 1, row : row + 8]
    after = other[m, tile + 1, row : row + 8]
    total = total + pltpu.roll(jnp.where(lane_high, before, here), 16, 1)
    total = total + pltpu.roll(jnp.where(lane_low, after, here), 112, 1)
    up, down = pltpu.roll(here, 1, 1), pltpu.roll(here, 127, 1)
    beside = jnp.where(even, up, down) if colour == 0 else jnp.where(even, down, up)
    total = total + jnp.where(edges[colour], 0.0, beside)
    rows = slice(8 * chunk, 8 * chunk + 8)
    return scaled[m, colour, tile, rows] + ratio[m, colour, tile, rows] * total


def fine_masks():
    lane = iota((8, 128), 1)
    even = even_cells(8)
    first, last = lane % 16 == 0, lane % 16 == 15
    edges = (
        (even & first) | (jnp.logical_not(even) & last),
        (even & last) | (jnp.logical_not(even) & first),
    )
    return lane < 16, lane >= 112, even, edges


def fine_sweep(values, scaled, ratio, colour, masks):
    def body(tile, carry):
        found = [
            (m, chunk, fine_update(values[1 - colour], scaled, ratio, m, colour, tile, chunk, masks))
            for m in range(3)
            for chunk in range(ROWS // 8)
        ]
        for m, chunk, new in found:
            values[colour][m, tile, 8 + 8 * chunk : 16 + 8 * chunk] = new
        return carry

    lax.fori_loop(1, WIDE - 1, body, 0, unroll=2)


def down_kernel(
    count, factor, packed, from_left, from_right, red, black, coarse, to_above, to_below, partial,
    scaled, ratio, remain
):
    held = count[0]
    load_fine(held, factor, packed, from_left, from_right, scaled, ratio)
    masks = fine_masks()
    pre = (red, black)
    red[...] = jnp.zeros(red.shape, F32)
    black[...] = jnp.zeros(black.shape, F32)
    red[:, :, 8 : 8 + ROWS] = scaled[:, 0]
    fine_sweep(pre, scaled, ratio, 1, masks)
    fine_sweep(pre, scaled, ratio, 0, masks)
    fine_sweep(pre, scaled, ratio, 1, masks)

    def residual(tile, total):
        found = []
        for chunk in range(1, 5):
            rows = slice(8 * chunk, 8 * chunk + 8)
            row = 8 + 8 * chunk
            coef = packed[3, 0, tile - 2, rows]
            out = slice(8 * chunk - 8, 8 * chunk)
            for m in range(3):
                reds = red[m, tile, row : row + 8]
                blacks = black[m, tile, row : row + 8]
                update = fine_update(black, scaled, ratio, m, 0, tile, chunk, masks)
                left = (coef + 6.0 * factor[m]) * (update - reds)
                left = jnp.where(tile < 2 * held + 2, left, 0.0)
                found.append((m, out, left))
                term = (packed[m, 0, tile - 2, rows] + left) * reds
                total = total + term + packed[m, 1, tile - 2, rows] * blacks
            found.append((3, out, coef + packed[3, 1, tile - 2, rows]))
        for m, out, left in found:
            remain[m, tile - 2, out] = left
        return total

    total = lax.fori_loop(2, 2 + TILES, residual, jnp.zeros((8, 128), F32))
    partial[...] = total
    pool = pool_matrix()
    for slot in range(SLOTS):
        sides = []
        for tile in (2 * slot, 2 * slot + 1):
            sides.append(
                jnp.concatenate(
                    [
                        remain[m, tile, pl.ds(0, COWN, stride=2)]
                        + remain[m, tile, pl.ds(1, COWN, stride=2)]
                        for m in range(4)
                    ],
                    axis=0,
                )
            )
        pooled = exact_dot(jnp.concatenate(sides, axis=1), pool) * 0.125
        for m in range(4):
            box = pooled[COWN * m : COWN * m + COWN]
            coarse[m, slot] = box
            to_above[m, CHALO * slot : CHALO * slot + CHALO] = box[:CHALO]
            to_below[m, CHALO * slot : CHALO * slot + CHALO] = box[COWN - CHALO :]


def up_kernel(
    count, factor, packed, from_left, from_right, pre_red, pre_black, coarse, above, below,
    coarse_left, coarse_right, partial, smoothed, share, scaled, ratio, red, black, cscaled,
    cratio, cred, cblack, spread
):
    held = count[0]
    cscaled[...] = jnp.zeros(cscaled.shape, F32)
    cratio[...] = jnp.zeros(cratio.shape, F32)

    def put(tile, row, pieces):
        coef = pieces[3]
        size = coef.shape[0]
        for m in range(3):
            b = 0.25 * factor[m]
            inverse = jnp.where(coef > 0.0, 1.0 / (coef + 6.0 * b), 0.0)
            cscaled[m, tile, row : row + size] = pieces[m] * inverse
            cratio[m, tile, row : row + size] = b * inverse

    for slot in range(SLOTS):
        rows = slice(CHALO * slot, CHALO * slot + CHALO)
        put(slot + 3, 0, [above[m, rows] for m in range(4)])
        put(slot + 3, CHALO, [coarse[m, slot] for m in range(4)])
        put(slot + 3, CHALO + COWN, [below[m, rows] for m in range(4)])
    for side in range(2):
        rows = slice(CROWS * side, CROWS * side + CROWS)
        put(1 + side, 0, [coarse_left[m, rows] for m in range(4)])
        put(held + 3 + side, 0, [coarse_right[m, rows] for m in range(4)])

    lane = iota((8, 128), 1)
    lane_low, lane_high = lane < 16, lane >= 112
    first, last = lane % 16 == 0, lane % 16 == 15
    is_red = (iota((8, 128), 0) + lane // 16 + lane % 16) % 2 == 0
    chosen = (is_red, jnp.logical_not(is_red))
    corr = (cred, cblack)
    cred[...] = jnp.zeros(cred.shape, F32)
    cblack[...] = jnp.zeros(cblack.shape, F32)

    def start(tile, carry):
        found = [
            (m, chunk, jnp.where(is_red, cscaled[m, tile, 8 * chunk : 8 * chunk + 8], 0.0))
            for m in range(3)
            for chunk in range(5)
        ]
        for m, chunk, new in found:
            cred[m, tile, 8 + 8 * chunk : 16 + 8 * chunk] = new
        return carry

    lax.fori_loop(1, CWIDE - 1, start, 0)

    def coarse_sweep(colour):
        other = corr[1 - colour]

        def body(tile, carry):
            found = []
            for m in range(3):
                for chunk in range(5):
                    row = 8 + 8 * chunk
                    here = other[m, tile, row : row + 8]
                    total = other[m, tile, row - 1 : row + 7] + other[m, tile, row + 1 : row + 9]
                    before = other[m, tile - 1, row : row + 8]
                    after = other[m, tile + 1, row : row + 8]
                    total = total + pltpu.roll(jnp.where(lane_high, before, here), 16, 1)
                    total = total + pltpu.roll(jnp.where(lane_low, after, here), 112, 1)
                    total = total + jnp.where(first, 0.0, pltpu.roll(here, 1, 1))
                    total = total + jnp.where(last, 0.0, pltpu.roll(here, 127, 1))
                    rows = slice(8 * chunk, 8 * chunk + 8)
                    new = cscaled[m, tile, rows] + cratio[m, tile, rows] * total
                    found.append((m, row, jnp.where(chosen[colour], new, 0.0)))
            for m, row, new in found:
                corr[colour][m, tile, row : row + 8] = new
            return carry

        lax.fori_loop(1, CWIDE - 1, body, 0, unroll=2)

    coarse_sweep(1)
    for _ in range(3):
        coarse_sweep(0)
        coarse_sweep(1)

    total = partial[...]
    for slot in range(SLOTS):
        for m in range(3):
            for chunk in range(2):
                row = 8 + CHALO + 8 * chunk
                both = cred[m, slot + 3, row : row + 8] + cblack[m, slot + 3, row : row + 8]
                total = total + 8.0 * (coarse[m, slot, 8 * chunk : 8 * chunk + 8] * both)
    share[...] = jnp.broadcast_to(jnp.sum(total, axis=0, keepdims=True), share.shape)

    load_fine(held, factor, packed, from_left, from_right, scaled, ratio)
    masks = fine_masks()
    values = (red, black)
    for value in values:
        value[...] = jnp.zeros(value.shape, F32)
    widen = spread_matrix()
    half_rows = ROWS // 2
    for ctile in range(2, CWIDE - 2):
        low = 8 + CHALO - 4
        cells = jnp.concatenate(
            [
                cred[m, ctile, low : low + half_rows] + cblack[m, ctile, low : low + half_rows]
                for m in range(3)
            ],
            axis=0,
        )
        wide = exact_dot(cells, widen)
        for half in range(2):
            tile = 2 * (ctile - 3) + half + 2
            if not 1 <= tile <= WIDE - 2:
                continue
            for m in range(3):
                piece = wide[half_rows * m : half_rows * m + half_rows, 128 * half : 128 * half + 128]
                spread[m, tile, pl.ds(0, half_rows, stride=2)] = piece
                spread[m, tile, pl.ds(1, half_rows, stride=2)] = piece

    def add(tile, carry):
        found = [
            (value, m, old[m, tile, 8 : 8 + ROWS] + spread[m, tile])
            for value, old in ((red, pre_red), (black, pre_black))
            for m in range(3)
        ]
        for value, m, new in found:
            value[m, tile, 8 : 8 + ROWS] = new
        return carry

    lax.fori_loop(1, WIDE - 1, add, 0)
    for _ in range(2):
        fine_sweep(values, scaled, ratio, 1, masks)
        fine_sweep(values, scaled, ratio, 0, masks)

    merge = merge_matrix()
    even = even_cells(3 * 32)
    for slot in range(SLOTS):
        live = slot < held
        for half in range(2):
            tile = 2 + 2 * slot + half
            reds = jnp.concatenate([red[m, tile, 16:48] for m in range(3)], axis=0)
            blacks = jnp.concatenate([black[m, tile, 16:48] for m in range(3)], axis=0)
            both = jnp.concatenate(
                [jnp.where(even, reds, blacks), jnp.where(even, blacks, reds)], axis=1
            )
            cells = exact_dot(jnp.where(live, both, 0.0), merge)
            for m in range(3):
                smoothed[slot, m, :, 256 * half : 256 * half + 256] = cells[32 * m : 32 * m + 32]


def shape(*dims):
    return jax.ShapeDtypeStruct(dims, F32)


SMEM = pl.BlockSpec(memory_space=pltpu.SMEM)
WHOLE = pl.BlockSpec(memory_space=pltpu.VMEM)


def shift(value, axis, step):
    size = lax.axis_size(axis)
    pairs = [(i, i + step) for i in range(size) if 0 <= i + step < size]
    return lax.ppermute(value, axis, pairs)


def total_over(rows, axis):
    return jnp.sum(lax.all_to_all(rows, axis, 0, 0), axis=0)


def per_device(box_counts, viscosity, implicit_coef, right_side, old_direction, previous_dot):
    group_n = lax.axis_size(GROUP_AXES)
    slab_n = lax.axis_size("gx")
    my_index = lax.axis_index(GROUP_AXES)
    held = lax.dynamic_index_in_dim(box_counts, my_index, 0, keepdims=False)
    count = held[None]
    right, coef = right_side[0], implicit_coef[0]
    params = pltpu.CompilerParams(vmem_limit_bytes=VMEM_BYTES)

    top = jnp.concatenate([right[:, :, :8], coef[:, None, :8]], axis=1)
    bottom = jnp.concatenate([right[:, :, 24:], coef[:, None, 24:]], axis=1)
    above = shift(bottom, "gx", 1)
    below = shift(top, "gx", -1)

    slot_block = lambda *dims: pl.BlockSpec((1,) + dims, lambda q: (q,) + (0,) * len(dims))
    edge_block = pl.BlockSpec((4, 2, ROWS, 128), lambda q: (0, 0, 0, 0))
    packed, left_edge, right_edge = pl.pallas_call(
        pack_kernel,
        grid=(SLOTS,),
        in_specs=[
            SMEM,
            slot_block(3, 32, 512),
            slot_block(32, 512),
            slot_block(4, 8, 512),
            slot_block(4, 8, 512),
        ],
        out_specs=[
            pl.BlockSpec((4, 2, 2, ROWS, 128), lambda q: (0, 0, q, 0, 0)),
            edge_block,
            edge_block,
        ],
        out_shape=[
            shape(4, 2, TILES, ROWS, 128),
            shape(4, 2, ROWS, 128),
            shape(4, 2, ROWS, 128),
        ],
        compiler_params=params,
        name="pack",
    )(count, right, coef, above, below)

    from_left = shift(right_edge, GROUP_AXES, 1)
    from_right = shift(left_edge, GROUP_AXES, -1)

    padded = (3, WIDE, ROWS + 16, 128)
    fine = pltpu.VMEM((3, 2, WIDE, ROWS, 128), F32)
    pre_red, pre_black, coarse, to_above, to_below, partial = pl.pallas_call(
        down_kernel,
        in_specs=[SMEM, SMEM, WHOLE, WHOLE, WHOLE],
        out_specs=[WHOLE] * 6,
        out_shape=[
            shape(*padded),
            shape(*padded),
            shape(4, SLOTS, COWN, 128),
            shape(4, SLOTS * CHALO, 128),
            shape(4, SLOTS * CHALO, 128),
            shape(8, 128),
        ],
        scratch_shapes=[fine, fine, pltpu.VMEM((4, TILES, 32, 128), F32)],
        compiler_params=params,
        name="down",
    )(count, viscosity, packed, from_left, from_right)

    coarse_above = shift(to_below, "gx", 1)
    coarse_below = shift(to_above, "gx", -1)
    tall = jnp.concatenate(
        [
            coarse_above.reshape(4, SLOTS, CHALO, 128),
            coarse,
            coarse_below.reshape(4, SLOTS, CHALO, 128),
        ],
        axis=2,
    )
    edge_shape = (4, 2 * CROWS, 128)
    coarse_first = tall[:, :2].reshape(edge_shape)
    coarse_last = lax.dynamic_slice_in_dim(tall, held - 2, 2, axis=1).reshape(edge_shape)
    coarse_left = shift(coarse_last, GROUP_AXES, 1)
    coarse_right = shift(coarse_first, GROUP_AXES, -1)

    cfine = pltpu.VMEM((3, CWIDE, 40, 128), F32)
    smoothed, share = pl.pallas_call(
        up_kernel,
        in_specs=[SMEM, SMEM] + [WHOLE] * 11,
        out_specs=[WHOLE] * 2,
        out_shape=[shape(SLOTS, 3, 32, 512), shape(group_n, 128)],
        scratch_shapes=[
            fine,
            fine,
            pltpu.VMEM(padded, F32),
            pltpu.VMEM(padded, F32),
            cfine,
            cfine,
            pltpu.VMEM((3, CWIDE, 56, 128), F32),
            pltpu.VMEM((3, CWIDE, 56, 128), F32),
            pltpu.VMEM((3, WIDE, ROWS, 128), F32),
        ],
        compiler_params=params,
        name="up",
    )(
        count, viscosity, packed, from_left, from_right, pre_red, pre_black, coarse, coarse_above,
        coarse_below, coarse_left, coarse_right, partial
    )

    row = total_over(share, GROUP_AXES)
    row = total_over(jnp.broadcast_to(row[None], (slab_n, 128)), "gx")
    dot_total = jnp.sum(row)
    cell_total = jnp.sum(box_counts).astype(F32) * (3.0 * slab_n * 32 * 512)
    ratio = dot_total / cell_total / previous_dot[0]
    usable = (jnp.arange(SLOTS, dtype=jnp.int32) < held)[:, None, None, None]
    direction = jnp.where(usable, smoothed + ratio * old_direction[0], 0.0)
    return smoothed[None], direction[None]


def solution(mesh):
    wide = P("gx", GROUP_AXES, None, None, None)
    placed = (P(), P(), P("gx", GROUP_AXES, None, None), wide, wide, P())
    return jax.shard_map(
        per_device, mesh=mesh, in_specs=placed, out_specs=(wide, wide), check_vma=False
    )
```

time: 439 us -> 119 us (0.27)
  starting transfers between devices: 247 us -> 42 us
  blocking collectives: 116 us -> 17.1 us
  Pallas kernels: 0 us -> 23.5 us
  other arithmetic: 26.9 us -> 4.44 us
  local copies, waits for them, and re-layouts: 22.6 us -> 4.48 us
  waiting for transfers between devices: 13.9 us -> 23 us
    ppermute x70 -> x8, starting transfers between devices: 247 us -> 29.2 us  [shift(): return lax.ppermute(value, axis, pairs)]
    psum x1 -> x0, blocking collectives: 116 us -> none  [per_device(): dot_total = lax.psum(local_dot, ('gx', 'gy', 'gz'))]
    pallas_call x0 -> x3, Pallas kernels: none -> 23.5 us  [the longest x1 14.3 us: per_device(): pl.pallas_call(up_kernel, in_specs=[SMEM, SMEM] + [WHOLE] * 11, out_specs...]
    all_to_all x0 -> x1, blocking collectives: none -> 17.1 us  [total_over(): return jnp.sum(lax.all_to_all(rows, axis, 0, 0), axis=0)]
    all_to_all x0 -> x1, starting transfers between devices: none -> 12.8 us  [total_over(): return jnp.sum(lax.all_to_all(rows, axis, 0, 0), axis=0)]
    select_n x40 -> x0, other arithmetic: 12.1 us -> none  [the longest x15 8.39 us: sweep_colour(): return jnp.where(chosen, updated, values)]
    slice x86 -> x3, local copies, waits for them, and re-layouts: 11 us -> 1.22 us  [the longest x1 1.14 us: per_device(): top = jnp.concatenate([right[:, :, :8], coef[:, None, :8]], axis=1)]
    all_to_all x0 -> x1, waiting for transfers between devices: none -> 8.82 us  [total_over(): return jnp.sum(lax.all_to_all(rows, axis, 0, 0), axis=0)]
  transfers between devices with their start and end apart: 70 -> 9, of which waited for: 15 -> 8; matrix products, arithmetic and copies ran while one was open for 7% -> 2% of each run, Pallas kernels for 0% -> 0%
where the time goes in v1:
time: 119 us; the launch traced here: 118 us
  starting transfers between devices  42 us (35%)
  Pallas kernels  23.5 us (20%)
  waiting for transfers between devices  23 us (19%)
  blocking collectives  17.1 us (14%)
  local copies, waits for them, and re-layouts  4.48 us (4%)
  other arithmetic  4.44 us (4%)
  between operations  3.85 us (3%)
    ppermute x8, starting transfers between devices, shift(): return lax.ppermute(value, axis, pairs)  29.2 us
    all_to_all x1, blocking collectives, total_over(): return jnp.sum(lax.all_to_all(rows, axis, 0, 0), axis=0)  17.1 us
    pallas_call x1, Pallas kernels, per_device(): pl.pallas_call(up_kernel, in_specs=[SMEM, SMEM] + [WHOLE] * 11, out_specs...  14.3 us
    ppermute x8, waiting for transfers between devices, shift(): return lax.ppermute(value, axis, pairs)  14.2 us
    all_to_all x1, starting transfers between devices, total_over(): return jnp.sum(lax.all_to_all(rows, axis, 0, 0), axis=0)  12.8 us
    all_to_all x1, waiting for transfers between devices, total_over(): return jnp.sum(lax.all_to_all(rows, axis, 0, 0), axis=0)  8.82 us
    pallas_call x1, Pallas kernels, per_device(): pl.pallas_call(down_kernel, in_specs=[SMEM, SMEM, WHOLE, WHOLE, WHOLE], o...  7.04 us
    broadcast_in_dim x1, other arithmetic, per_device(): return (smoothed[None], direction[None])  2.52 us
  transfers between devices with their start and end apart: 9, of which 8 were waited for; matrix products, arithmetic and copies ran while one was open for 2% of the time, Pallas kernels for 0%

profile of v1, /device:TPU:1, one launch (start us, length us, event | category | flops | bytes accessed | tf_op | source)
XLA Modules:
  0.0 118.4 jit_solution(5363111438122669104)
XLA Ops:
  0.6 0.0 copy-start
  0.6 0.0 copy-start.3
  0.7 0.0 copy-start.5
  0.7 1.1 fusion.2
  1.8 0.9 slice_bitcast_fusion
  2.7 0.0 copy-start.4
  2.7 4.4 %collective-permute-start = (f32[4,4,8,512]{3,2,1,0:T(8,128)S(1)}, f32[4,4,8,512]{3,2,1,0:T(8,128)S(1)}, u32[]{:S(2)}, u32[]{:S(2)}) collective-permute-start(f32[4,4,8,512]{3,2,1,0:T(8,128)S(1)} %pad_maximum_fusion.1), channel_id=1, source_target_pairs={{0,32},{32,64},{64,96},{96,128},{128,160},{160,192},{192,224},{224... | collective-permute-start | bytes 786440 | tf_op jit(solution)/shard_map/ppermute | solution.py:384
  7.2 1.3 %collective-permute-start.1 = (f32[4,4,8,512]{3,2,1,0:T(8,128)S(1)}, f32[4,4,8,512]{3,2,1,0:T(8,128)S(1)}, u32[]{:S(2)}, u32[]{:S(2)}) collective-permute-start(f32[4,4,8,512]{3,2,1,0:T(8,128)S(1)} %pad_maximum_fusion.2), channel_id=1, source_target_pairs={{32,0},{64,32},{96,64},{128,96},{160,128},{192,160},{224,192},{256... | collective-permute-start | bytes 786440 | tf_op jit(solution)/shard_map/ppermute | solution.py:384
  8.5 0.0 copy-done.5
  8.5 0.6 dynamic_slice.7.count
  9.0 1.4 %collective-permute-done.above = f32[4,4,8,512]{3,2,1,0:T(8,128)S(1)} collective-permute-done((f32[4,4,8,512]{3,2,1,0:T(8,128)S(1)}, f32[4,4,8,512]{3,2,1,0:T(8,128)S(1)}, u32[]{:S(2)}, u32[]{:S(2)}) %collective-permute-start) | collective-permute-done | bytes 262176 | tf_op jit(solution)/shard_map/ppermute | solution.py:384
  10.4 4.0 %collective-permute-done.1.below = f32[4,4,8,512]{3,2,1,0:T(8,128)S(1)} collective-permute-done((f32[4,4,8,512]{3,2,1,0:T(8,128)S(1)}, f32[4,4,8,512]{3,2,1,0:T(8,128)S(1)}, u32[]{:S(2)}, u32[]{:S(2)}) %collective-permute-start.1) | collective-permute-done | bytes 262176 | tf_op jit(solution)/shard_map/ppermute | solution.py:384
  14.4 0.0 copy-done
  14.4 0.0 copy-done.3
  14.4 2.2 %pack.1 = (f32[4,2,8,48,128]{4,3,2,1,0:T(8,128)S(1)}, f32[4,2,48,128]{3,2,1,0:T(8,128)S(1)}, f32[4,2,48,128]{3,2,1,0:T(8,128)S(1)}) custom-call(s32[1]{0:T(128)} %dynamic_slice.7.count, f32[4,3,32,512]{3,2,1,0:T(8,128)S(1)} %bitcast.29, f32[4,32,512]{2,1,0:T(8,128)S(1)} %bitcast.31, f32[4,4,8,512]{3,2,1,0:T(8,128)S(1)} %collective-permute-done.above, ...), custom_call_target="tpu_custom_call" | custom-call | tf_op jit(solution)/shard_map/pack/pallas_call | solution.py:407
  16.6 5.0 %collective-permute-start.2 = (f32[4,2,48,128]{3,2,1,0:T(8,128)S(1)}, f32[4,2,48,128]{3,2,1,0:T(8,128)S(1)}, u32[]{:S(2)}, u32[]{:S(2)}) collective-permute-start(f32[4,2,48,128]{3,2,1,0:T(8,128)S(1)} %get-tuple-element.14), channel_id=1, source_target_pairs={{0,1},{1,2},{2,3},{3,4},{4,5},{5,6},{6,7},{7,8},{8,9},{9,10},{10,1... | collective-permute-start | bytes 589832 | tf_op jit(solution)/shard_map/ppermute | solution.py:384
  21.7 4.9 %collective-permute-start.3 = (f32[4,2,48,128]{3,2,1,0:T(8,128)S(1)}, f32[4,2,48,128]{3,2,1,0:T(8,128)S(1)}, u32[]{:S(2)}, u32[]{:S(2)}) collective-permute-start(f32[4,2,48,128]{3,2,1,0:T(8,128)S(1)} %get-tuple-element.15), channel_id=1, source_target_pairs={{1,0},{2,1},{3,2},{4,3},{5,4},{6,5},{7,6},{8,7},{9,8},{10,9},{11,1... | collective-permute-start | bytes 589832 | tf_op jit(solution)/shard_map/ppermute | solution.py:384
  26.6 1.4 %collective-permute-done.2.from_left = f32[4,2,48,128]{3,2,1,0:T(8,128)S(1)} collective-permute-done((f32[4,2,48,128]{3,2,1,0:T(8,128)S(1)}, f32[4,2,48,128]{3,2,1,0:T(8,128)S(1)}, u32[]{:S(2)}, u32[]{:S(2)}) %collective-permute-start.2) | collective-permute-done | bytes 196640 | tf_op jit(solution)/shard_map/ppermute | solution.py:384
  28.0 1.2 collective-permute-done.3.from_right
  29.2 0.0 copy-done.4
  29.2 7.0 %down.1 = (f32[3,12,64,128]{3,2,1,0:T(8,128)S(1)}, f32[3,12,64,128]{3,2,1,0:T(8,128)S(1)}, f32[4,4,16,128]{3,2,1,0:T(8,128)S(1)}, f32[4,40,128]{2,1,0:T(8,128)S(...) custom-call(s32[1]{0:T(128)} %dynamic_slice.7.count, f32[3]{0:T(128)S(1)} %copy-done.4, ...), custom_call_target="tpu_custom_call" | custom-call | tf_op jit(solution)/shard_map/down/pallas_call | solution.py:436
  36.2 0.0 copy-start.1
  36.2 1.0 copy-done.1
  37.3 3.5 %collective-permute-start.4 = (f32[4,40,128]{2,1,0:T(8,128)}, f32[4,40,128]{2,1,0:T(8,128)S(1)}, u32[]{:S(2)}, u32[]{:S(2)}) collective-permute-start(f32[4,40,128]{2,1,0:T(8,128)} %get-tuple-element.19), channel_id=1, source_target_pairs={{0,32},{32,64},{64,96},{96,128},{128,160},{160,192},{192,224},{224... | collective-permute-start | bytes 245768 | tf_op jit(solution)/shard_map/ppermute | solution.py:384
  40.8 1.3 %collective-permute-start.5 = (f32[4,40,128]{2,1,0:T(8,128)S(1)}, f32[4,40,128]{2,1,0:T(8,128)S(1)}, u32[]{:S(2)}, u32[]{:S(2)}) collective-permute-start(f32[4,40,128]{2,1,0:T(8,128)S(1)} %get-tuple-element.20), channel_id=1, source_target_pairs={{32,0},{64,32},{96,64},{128,96},{160,128},{192,160},{224,192},{256... | collective-permute-start | bytes 245768 | tf_op jit(solution)/shard_map/ppermute | solution.py:384
  43.2 0.0 collective-permute-done.4.above
  43.3 4.1 %collective-permute-done.5.below = f32[4,40,128]{2,1,0:T(8,128)S(1)} collective-permute-done((f32[4,40,128]{2,1,0:T(8,128)S(1)}, f32[4,40,128]{2,1,0:T(8,128)S(1)}, u32[]{:S(2)}, u32[]{:S(2)}) %collective-permute-start.5) | collective-permute-done | bytes 81952 | tf_op jit(solution)/shard_map/ppermute | solution.py:384
  47.4 0.0 copy-start.2
  47.5 0.1 copy.43
  47.6 2.4 %collective-permute-start.6 = (f32[4,72,128]{2,1,0:T(8,128)S(1)}, f32[4,72,128]{2,1,0:T(8,128)S(1)}, u32[]{:S(2)}, u32[]{:S(2)}) collective-permute-start(f32[4,72,128]{2,1,0:T(8,128)S(1)} %copy.44), channel_id=1, source_target_pairs={{0,1},{1,2},{2,3},{3,4},{4,5},{5,6},{6,7},{7,8},{8,9},{9,10},{10,1... | collective-permute-start | bytes 442376 | tf_op jit(solution)/shard_map/ppermute | solution.py:384
  50.0 0.1 copy.45
  50.1 6.4 %collective-permute-start.7 = (f32[4,72,128]{2,1,0:T(8,128)S(1)}, f32[4,72,128]{2,1,0:T(8,128)S(1)}, u32[]{:S(2)}, u32[]{:S(2)}) collective-permute-start(f32[4,72,128]{2,1,0:T(8,128)S(1)} %copy.46), channel_id=1, source_target_pairs={{1,0},{2,1},{3,2},{4,3},{5,4},{6,5},{7,6},{8,7},{9,8},{10,9},{11,1... | collective-permute-start | bytes 442376 | tf_op jit(solution)/shard_map/ppermute | solution.py:384
  56.5 0.8 collective-permute-done.6.coarse_left
  57.3 1.3 %collective-permute-done.7.coarse_right = f32[4,72,128]{2,1,0:T(8,128)S(1)} collective-permute-done((f32[4,72,128]{2,1,0:T(8,128)S(1)}, f32[4,72,128]{2,1,0:T(8,128)S(1)}, u32[]{:S(2)}, u32[]{:S(2)}) %collective-permute-start.7) | collective-permute-done | bytes 147488 | tf_op jit(solution)/shard_map/ppermute | solution.py:384
  58.6 0.0 copy-done.2
  58.6 14.3 %up.1 = (f32[4,3,32,512]{3,2,1,0:T(8,128)}, f32[32,128]{1,0:T(8,128)S(1)}) custom-call(s32[1]{0:T(128)} %dynamic_slice.7.count, f32[3]{0:T(128)S(1)} %copy-done.4, f32[4,2,8,48,128]{4,3,2,1,0:T(8,128)S(1)} %get-tuple-element.13.packed, f32[4,2,48,128]{3,2,1,0:T(8,128)S(1)} %collective-permute-done.2.from_left, ...), custom_call_target="tpu_custom_call" | custom-call | tf_op jit(solution)/shard_map/up/pallas_call | solution.py:470
  72.9 17.1 %all_to_all.15 = f32[32,1,128]{2,1,0:T(1,128)S(1)} all-to-all(f32[32,1,128]{2,1,0:T(1,128)S(1)} %bitcast.32), channel_id=1, replica_groups=mesh['gx'=16,'gy'=8,'gz'=4] {'gy','gz'}, dimensions={0} | all-to-all | bytes 32768 | tf_op jit(solution)/shard_map/all_to_all | solution.py:388
  90.0 0.1 reduce_sum.27
  90.0 0.6 broadcast_in_dim.36
  90.6 12.8 %all-to-all-start.1 = ((f32[16,1,128]{2,1,0:T(1,128)}), f32[16,1,128]{2,1,0:T(1,128)S(1)}, u32[]{:S(2)}, u32[]{:S(2)}) async-start(f32[16,1,128]{2,1,0:T(1,128)} %broadcast_in_dim.36), calls=%async_computation.1 | async-start | bytes 16384 | tf_op jit(solution)/shard_map/all_to_all | solution.py:388
  103.4 0.6 iota_compare_fusion
  104.0 0.6 reduce_sum.33
  105.8 8.8 %all-to-all-done.1 = f32[16,1,128]{2,1,0:T(1,128)S(1)} async-done(((f32[16,1,128]{2,1,0:T(1,128)}), f32[16,1,128]{2,1,0:T(1,128)S(1)}, u32[]{:S(2)}, u32[]{:S(2)}) %all-to-all-start.1) | async-done | bytes 8224 | tf_op jit(solution)/shard_map/all_to_all | solution.py:388
  114.6 0.6 reduce_sum.32
  115.9 2.5 %fusion.1 = f32[1,4,3,32,512]{4,3,2,1,0:T(8,128)} fusion(f32[4,3,32,512]{3,2,1,0:T(8,128)} %get-tuple-element.22, f32[1,4,3,32,512]{4,3,2,1,0:T(8,128)} %param.10, f32[]{:T(128)S(6)} %div.4, pred[4]{0:T(512)(128)(4,1)S(1)} %iota_compare_fusion), kind=kLoop, calls=%fused_computation.2 | loop fusion | flops 589824 | bytes 2359304 | tf_op jit(solution)/shard_map/broadcast_in_dim | solution.py:500
  (10 shorter events, 0.2 us)
Async XLA Ops:
  0.6 13.8 %copy-start = (f32[1,4,3,32,512]{4,3,2,1,0:T(8,128)S(1)}, f32[1,4,3,32,512]{4,3,2,1,0:T(8,128)}, u32[]{:S(2)}) copy-start(f32[1,4,3,32,512]{4,3,2,1,0:T(8,128)} %param.9) | copy-start | bytes 2359300
  0.6 13.8 %copy-start.3 = (f32[1,4,32,512]{3,2,1,0:T(8,128)S(1)}, f32[1,4,32,512]{3,2,1,0:T(8,128)}, u32[]{:S(2)}) copy-start(f32[1,4,32,512]{3,2,1,0:T(8,128)} %param.8) | copy-start | bytes 786436
  0.7 7.8 %copy-start.5 = (s32[32]{0:T(128)S(1)}, s32[32]{0:T(128)}, u32[]{:S(2)}) copy-start(s32[32]{0:T(128)} %param.6) | copy-start | bytes 388
  2.7 26.5 %copy-start.4 = (f32[3]{0:T(128)S(1)}, f32[3]{0:T(128)}, u32[]{:S(2)}) copy-start(f32[3]{0:T(128)} %factor.3) | copy-start | bytes 40
  2.7 7.7 %collective-permute-start = (f32[4,4,8,512]{3,2,1,0:T(8,128)S(1)}, f32[4,4,8,512]{3,2,1,0:T(8,128)S(1)}, u32[]{:S(2)}, u32[]{:S(2)}) collective-permute-start(f32[4,4,8,512]{3,2,1,0:T(8,128)S(1)} %pad_maximum_fusion.1), channel_id=1, source_target_pairs={{0,32},{32,64},{64,96},{96,128},{128,160},{160,192},{192,224},{224... | collective-permute-start | bytes 786440 | tf_op jit(solution)/shard_map/ppermute | solution.py:384
  7.2 7.3 %collective-permute-start.1 = (f32[4,4,8,512]{3,2,1,0:T(8,128)S(1)}, f32[4,4,8,512]{3,2,1,0:T(8,128)S(1)}, u32[]{:S(2)}, u32[]{:S(2)}) collective-permute-start(f32[4,4,8,512]{3,2,1,0:T(8,128)S(1)} %pad_maximum_fusion.2), channel_id=1, source_target_pairs={{32,0},{64,32},{96,64},{128,96},{160,128},{192,160},{224,192},{256... | collective-permute-start | bytes 786440 | tf_op jit(solution)/shard_map/ppermute | solution.py:384
  16.6 11.4 %collective-permute-start.2 = (f32[4,2,48,128]{3,2,1,0:T(8,128)S(1)}, f32[4,2,48,128]{3,2,1,0:T(8,128)S(1)}, u32[]{:S(2)}, u32[]{:S(2)}) collective-permute-start(f32[4,2,48,128]{3,2,1,0:T(8,128)S(1)} %get-tuple-element.14), channel_id=1, source_target_pairs={{0,1},{1,2},{2,3},{3,4},{4,5},{5,6},{6,7},{7,8},{8,9},{9,10},{10,1... | collective-permute-start | bytes 589832 | tf_op jit(solution)/shard_map/ppermute | solution.py:384
  21.7 7.5 %collective-permute-start.3 = (f32[4,2,48,128]{3,2,1,0:T(8,128)S(1)}, f32[4,2,48,128]{3,2,1,0:T(8,128)S(1)}, u32[]{:S(2)}, u32[]{:S(2)}) collective-permute-start(f32[4,2,48,128]{3,2,1,0:T(8,128)S(1)} %get-tuple-element.15), channel_id=1, source_target_pairs={{1,0},{2,1},{3,2},{4,3},{5,4},{6,5},{7,6},{8,7},{9,8},{10,9},{11,1... | collective-permute-start | bytes 589832 | tf_op jit(solution)/shard_map/ppermute | solution.py:384
  36.2 1.0 copy-start.1
  37.3 5.9 %collective-permute-start.4 = (f32[4,40,128]{2,1,0:T(8,128)}, f32[4,40,128]{2,1,0:T(8,128)S(1)}, u32[]{:S(2)}, u32[]{:S(2)}) collective-permute-start(f32[4,40,128]{2,1,0:T(8,128)} %get-tuple-element.19), channel_id=1, source_target_pairs={{0,32},{32,64},{64,96},{96,128},{128,160},{160,192},{192,224},{224... | collective-permute-start | bytes 245768 | tf_op jit(solution)/shard_map/ppermute | solution.py:384
  40.8 6.6 %collective-permute-start.5 = (f32[4,40,128]{2,1,0:T(8,128)S(1)}, f32[4,40,128]{2,1,0:T(8,128)S(1)}, u32[]{:S(2)}, u32[]{:S(2)}) collective-permute-start(f32[4,40,128]{2,1,0:T(8,128)S(1)} %get-tuple-element.20), channel_id=1, source_target_pairs={{32,0},{64,32},{96,64},{128,96},{160,128},{192,160},{224,192},{256... | collective-permute-start | bytes 245768 | tf_op jit(solution)/shard_map/ppermute | solution.py:384
  47.4 11.2 %copy-start.2 = (f32[3,12,64,128]{3,2,1,0:T(8,128)S(1)}, f32[3,12,64,128]{3,2,1,0:T(8,128)}, u32[]{:S(2)}) copy-start(f32[3,12,64,128]{3,2,1,0:T(8,128)} %copy-done.1) | copy-start | bytes 3538948
  47.6 9.7 %collective-permute-start.6 = (f32[4,72,128]{2,1,0:T(8,128)S(1)}, f32[4,72,128]{2,1,0:T(8,128)S(1)}, u32[]{:S(2)}, u32[]{:S(2)}) collective-permute-start(f32[4,72,128]{2,1,0:T(8,128)S(1)} %copy.44), channel_id=1, source_target_pairs={{0,1},{1,2},{2,3},{3,4},{4,5},{5,6},{6,7},{7,8},{8,9},{9,10},{10,1... | collective-permute-start | bytes 442376 | tf_op jit(solution)/shard_map/ppermute | solution.py:384
  50.1 8.5 %collective-permute-start.7 = (f32[4,72,128]{2,1,0:T(8,128)S(1)}, f32[4,72,128]{2,1,0:T(8,128)S(1)}, u32[]{:S(2)}, u32[]{:S(2)}) collective-permute-start(f32[4,72,128]{2,1,0:T(8,128)S(1)} %copy.46), channel_id=1, source_target_pairs={{1,0},{2,1},{3,2},{4,3},{5,4},{6,5},{7,6},{8,7},{9,8},{10,9},{11,1... | collective-permute-start | bytes 442376 | tf_op jit(solution)/shard_map/ppermute | solution.py:384
  90.6 24.0 %all-to-all-start.1 = ((f32[16,1,128]{2,1,0:T(1,128)}), f32[16,1,128]{2,1,0:T(1,128)S(1)}, u32[]{:S(2)}, u32[]{:S(2)}) async-start(f32[16,1,128]{2,1,0:T(1,128)} %broadcast_in_dim.36), calls=%async_computation.1 | async-start | bytes 16384 | tf_op jit(solution)/shard_map/all_to_all | solution.py:388

commit v2 on v1

v2 whole, which is shorter than its diff:
```python
import functools

import jax
import jax.numpy as jnp
from jax import lax
from jax.experimental import pallas as pl
from jax.experimental.pallas import tpu as pltpu
from jax.sharding import PartitionSpec as P

GROUP_AXES = ("gy", "gz")
SLAB_AXIS = "gx"
F32 = jnp.float32
BF16 = jnp.bfloat16
VMEM_BYTES = 12 * 1024 * 1024

SLOTS = 4
TILES = 2 * SLOTS
ROWS = 48
NARROW = 40
WIDE = TILES + 4
COWN = 16
CHALO = 10
CROWS = COWN + 2 * CHALO
CWIDE = SLOTS + 6


def iota(shape, dim):
    return lax.broadcasted_iota(jnp.int32, shape, dim)


def exact_dot(values, ones):
    high = values.astype(BF16)
    rest = values - high.astype(F32)
    mid = rest.astype(BF16)
    low = (rest - mid.astype(F32)).astype(BF16)
    total = jnp.dot(low, ones, preferred_element_type=F32)
    total = total + jnp.dot(mid, ones, preferred_element_type=F32)
    return total + jnp.dot(high, ones, preferred_element_type=F32)


def split_matrix():
    source, target = iota((256, 256), 0), iota((256, 256), 1)
    y = source % 32
    wanted = (y % 2) * 128 + source // 32 * 16 + y // 2
    return (target == wanted).astype(F32).astype(BF16)


def merge_matrix():
    source, target = iota((256, 256), 0), iota((256, 256), 1)
    y = target % 32
    wanted = (y % 2) * 128 + target // 32 * 16 + y // 2
    return (source == wanted).astype(F32).astype(BF16)


def pool_matrix():
    source, target = iota((256, 128), 0), iota((256, 128), 1)
    wanted = source // 32 * 16 + source % 16
    return (target == wanted).astype(F32).astype(BF16)


def spread_matrix():
    source, target = iota((128, 256), 0), iota((128, 256), 1)
    wanted = target // 32 * 16 + target % 16
    return (source == wanted).astype(F32).astype(BF16)


def even_cells(rows):
    shape = (rows, 128)
    return (iota(shape, 0) + iota(shape, 1) // 16) % 2 == 0


def swap(value, axis, offset):
    size = lax.axis_size(axis)
    pairs = []
    for i in range(offset, size - 1, 2):
        pairs += [(i, i + 1), (i + 1, i)]
    return lax.ppermute(value, axis, pairs)


def exchange(first, second, axis):
    return swap(first, axis, 0), swap(second, axis, 1)


def split_cells(cells, rows, packed, put):
    even = even_cells(4 * rows)
    both = exact_dot(cells, packed)
    first, second = both[:, :128], both[:, 128:]
    red = jnp.where(even, first, second)
    black = jnp.where(even, second, first)
    for m in range(4):
        put(m, 0, red[rows * m : rows * m + rows])
        put(m, 1, black[rows * m : rows * m + rows])


def pack_kernel(info, right, coef, packed):
    live = pl.program_id(0) < info[0]
    split = split_matrix()
    for half in range(2):
        lanes = slice(256 * half, 256 * half + 256)
        parts = [right[0, m, :, lanes] for m in range(3)] + [coef[0, :, lanes]]
        cells = jnp.where(live, jnp.concatenate(parts, axis=0), 0.0)

        def put(m, colour, value, half=half):
            packed[m, colour, half] = value

        split_cells(cells, 32, split, put)


def pack_rim_kernel(info, above, below, rim):
    held = info[0]
    split = split_matrix()
    for slot in range(SLOTS):
        for half in range(2):
            lanes = slice(256 * half, 256 * half + 256)
            parts = []
            for m in range(4):
                parts += [above[slot, m, :, lanes], below[slot, m, :, lanes]]
            cells = jnp.where(slot < held, jnp.concatenate(parts, axis=0), 0.0)

            def put(m, colour, value, tile=2 * slot + half):
                rim[m, colour, tile] = value

            split_cells(cells, 16, split, put)


def pack_edges_kernel(info, above, below, packed, edge_a, edge_b):
    held, odd = info[0], info[2] == 1
    split = split_matrix()
    for slot, half in ((0, 0), (held - 1, 1)):
        lanes = slice(256 * half, 256 * half + 256)
        parts = []
        for m in range(4):
            parts += [above[slot, m, :, lanes], below[slot, m, :, lanes]]
        found = {}

        def put(m, colour, value):
            found[m, colour] = value

        split_cells(jnp.concatenate(parts, axis=0), 16, split, put)
        tile = 2 * slot + half
        for out, when in ((edge_a, odd), (edge_b, jnp.logical_not(odd))):

            @pl.when(when if half == 0 else jnp.logical_not(when))
            def _(out=out):
                for (m, colour), value in found.items():
                    out[m, colour, 0:8] = value[:8]
                    out[m, colour, 8:40] = packed[m, colour, tile]
                    out[m, colour, 40:48] = value[8:]


def load_fine(count, odd, factor, packed, rim, edge_a, edge_b, scaled, ratio, skip, rows):
    used = slice(skip, skip + rows)

    def put(tile, take):
        out = []
        for colour in range(2):
            coef = take(3, colour)
            inside = coef > 0.0
            for m in range(3):
                inverse = jnp.where(inside, 1.0 / (coef + 6.0 * factor[m]), 0.0)
                out.append((m, colour, take(m, colour) * inverse, factor[m] * inverse))
        for m, colour, first, second in out:
            scaled[m, colour, tile] = first
            ratio[m, colour, tile] = second

    def own(m, colour, tile):
        start, end = rim[m, colour, tile, skip:8], rim[m, colour, tile, 8 : 16 - skip]
        return jnp.concatenate([start, packed[m, colour, tile], end], axis=0)

    for tile in range(TILES):
        put(tile + 2, lambda m, colour: own(m, colour, tile))
    none = jnp.zeros((3, 2, rows, 128), F32)
    tile = WIDE - 2
    scaled[:, :, tile] = none
    ratio[:, :, tile] = none
    end = 2 * count + 2
    put(jnp.where(odd, 1, end), lambda m, colour: edge_a[m, colour, used])
    put(jnp.where(odd, end, 1), lambda m, colour: edge_b[m, colour, used])


def clear_rim(values, rows):
    rim = jnp.zeros((3, WIDE, 8, 128), F32)
    values[:, :, 0:8] = rim
    values[:, :, 8 + rows : 16 + rows] = rim
    side = jnp.zeros((3, rows, 128), F32)
    for tile in (0, WIDE - 1):
        values[:, tile, 8 : 8 + rows] = side


def fine_update(other, scaled, ratio, m, colour, tile, chunk, masks):
    lane_low, lane_high, even, edges = masks
    row = 8 + 8 * chunk
    here = other[m, tile, row : row + 8]
    total = here + other[m, tile, row - 1 : row + 7]
    total = total + other[m, tile, row + 1 : row + 9]
    before = other[m, tile - 1, row : row + 8]
    after = other[m, tile + 1, row : row + 8]
    total = total + pltpu.roll(jnp.where(lane_high, before, here), 16, 1)
    total = total + pltpu.roll(jnp.where(lane_low, after, here), 112, 1)
    up, down = pltpu.roll(here, 1, 1), pltpu.roll(here, 127, 1)
    beside = jnp.where(even, up, down) if colour == 0 else jnp.where(even, down, up)
    total = total + jnp.where(edges[colour], 0.0, beside)
    rows = slice(8 * chunk, 8 * chunk + 8)
    return scaled[m, colour, tile, rows] + ratio[m, colour, tile, rows] * total


def fine_masks():
    lane = iota((8, 128), 1)
    even = even_cells(8)
    first, last = lane % 16 == 0, lane % 16 == 15
    edges = (
        (even & first) | (jnp.logical_not(even) & last),
        (even & last) | (jnp.logical_not(even) & first),
    )
    return lane < 16, lane >= 112, even, edges


def fine_sweep(values, scaled, ratio, colour, masks, chunks, tiles=range(1, WIDE - 1)):
    for tile in tiles:
        for m in range(3):
            for chunk in chunks:
                values[colour][m, tile, 8 + 8 * chunk : 16 + 8 * chunk] = fine_update(
                    values[1 - colour], scaled, ratio, m, colour, tile, chunk, masks
                )


def down_kernel(
    info, factor, packed, rim, edge_a, edge_b, pre_red, pre_black, coarse, layers_a, layers_b,
    partial, scaled, ratio, red, black, remain
):
    held, odd, odd_slab = info[0], info[2] == 1, info[3] == 1
    load_fine(held, odd, factor, packed, rim, edge_a, edge_b, scaled, ratio, 0, ROWS)
    masks = fine_masks()
    pre = (red, black)
    clear_rim(red, ROWS)
    clear_rim(black, ROWS)
    chunks = range(ROWS // 8)
    red[:, 1 : WIDE - 1, 8 : 8 + ROWS] = scaled[:, 0, 1 : WIDE - 1]
    fine_sweep(pre, scaled, ratio, 1, masks, chunks)
    fine_sweep(pre, scaled, ratio, 0, masks, chunks)
    fine_sweep(pre, scaled, ratio, 1, masks, chunks)

    skip = (ROWS - NARROW) // 2
    pre_red[...] = red[:, 1 : WIDE - 1, 8 + skip : 8 + skip + NARROW]
    pre_black[...] = black[:, 1 : WIDE - 1, 8 + skip : 8 + skip + NARROW]

    totals = [jnp.zeros((8, 128), F32) for _ in range(4)]
    for tile in range(2, 2 + TILES):
        for chunk in range(1, 5):
            row = 8 + 8 * chunk
            out = slice(8 * chunk - 8, 8 * chunk)
            coef = packed[3, 0, tile - 2, out]
            for m in range(3):
                reds = red[m, tile, row : row + 8]
                blacks = black[m, tile, row : row + 8]
                update = fine_update(black, scaled, ratio, m, 0, tile, chunk, masks)
                left = (coef + 6.0 * factor[m]) * (update - reds)
                left = jnp.where(tile < 2 * held + 2, left, 0.0)
                remain[m, tile - 2, out] = left
                term = (packed[m, 0, tile - 2, out] + left) * reds
                totals[m] = totals[m] + term
                totals[3] = totals[3] + packed[m, 1, tile - 2, out] * blacks
            remain[3, tile - 2, out] = coef + packed[3, 1, tile - 2, out]
    partial[...] = (totals[0] + totals[1]) + (totals[2] + totals[3])
    pool = pool_matrix()
    for slot in range(SLOTS):
        sides = []
        for tile in (2 * slot, 2 * slot + 1):
            sides.append(
                jnp.concatenate(
                    [
                        remain[m, tile, pl.ds(0, COWN, stride=2)]
                        + remain[m, tile, pl.ds(1, COWN, stride=2)]
                        for m in range(4)
                    ],
                    axis=0,
                )
            )
        pooled = exact_dot(jnp.concatenate(sides, axis=1), pool) * 0.125
        for m in range(4):
            box = pooled[COWN * m : COWN * m + COWN]
            coarse[m, slot] = box
            start, end = box[:CHALO], box[COWN - CHALO :]
            rows = slice(CHALO * slot, CHALO * slot + CHALO)
            layers_a[m, rows] = jnp.where(odd_slab, start, end)
            layers_b[m, rows] = jnp.where(odd_slab, end, start)


def edges_kernel(info, coarse, layers_a, layers_b, kept_red, kept_black, edge_a, edge_b):
    held, odd, odd_slab = info[0], info[2] == 1, info[3] == 1

    def fill(out, slots):
        for n, slot in enumerate(slots):
            rows = slice(CHALO * slot, CHALO * slot + CHALO)
            base = CROWS * n
            for m in range(4):
                one, other = layers_a[m, rows], layers_b[m, rows]
                out[m, base : base + CHALO] = jnp.where(odd_slab, one, other)
                out[m, base + CHALO : base + CHALO + COWN] = coarse[m, slot]
                out[m, base + CHALO + COWN : base + CROWS] = jnp.where(odd_slab, other, one)

    for is_odd in (False, True):
        for count in range(2, SLOTS + 1):

            @pl.when((odd == is_odd) & (held == count))
            def _(is_odd=is_odd, count=count):
                start, end = (0, 1), (count - 2, count - 1)
                fill(edge_a, start if is_odd else end)
                fill(edge_b, end if is_odd else start)


def solve_kernel(
    info, factor, previous, coarse, layers_a, layers_b, coarse_a, coarse_b, partial, kept_red,
    kept_black, wanted, share, cscaled, cratio, cred, cblack
):
    held, odd, odd_slab = info[0], info[2] == 1, info[3] == 1

    def put(tile, row, pieces):
        coef = pieces[3]
        size = coef.shape[0]
        for m in range(3):
            b = 0.25 * factor[m]
            inverse = jnp.where(coef > 0.0, 1.0 / (coef + 6.0 * b), 0.0)
            cscaled[m, tile, row : row + size] = pieces[m] * inverse
            cratio[m, tile, row : row + size] = b * inverse

    rest = jnp.zeros((3, CWIDE, 40 - CROWS, 128), F32)
    cscaled[:, :, CROWS:] = rest
    cratio[:, :, CROWS:] = rest
    none = jnp.zeros((3, CROWS, 128), F32)
    for tile in (0, CWIDE - 3, CWIDE - 2, CWIDE - 1):
        cscaled[:, tile, :CROWS] = none
        cratio[:, tile, :CROWS] = none
    for slot in range(SLOTS):
        rows = slice(CHALO * slot, CHALO * slot + CHALO)
        ones = [layers_a[m, rows] for m in range(4)]
        others = [layers_b[m, rows] for m in range(4)]
        above = [jnp.where(odd_slab, ones[m], others[m]) for m in range(4)]
        below = [jnp.where(odd_slab, others[m], ones[m]) for m in range(4)]
        put(slot + 3, 0, above)
        put(slot + 3, CHALO, [coarse[m, slot] for m in range(4)])
        put(slot + 3, CHALO + COWN, below)
    for side in range(2):
        rows = slice(CROWS * side, CROWS * side + CROWS)
        put(jnp.where(odd, 1, held + 3) + side, 0, [coarse_a[m, rows] for m in range(4)])
        put(jnp.where(odd, held + 3, 1) + side, 0, [coarse_b[m, rows] for m in range(4)])

    lane = iota((8, 128), 1)
    lane_low, lane_high = lane < 16, lane >= 112
    first, last = lane % 16 == 0, lane % 16 == 15
    is_red = (iota((8, 128), 0) + lane // 16 + lane % 16) % 2 == 0
    chosen = (is_red, jnp.logical_not(is_red))
    corr = (cred, cblack)
    rim = jnp.zeros((3, CWIDE, 8, 128), F32)
    side = jnp.zeros((3, 40, 128), F32)
    for value in corr:
        value[:, :, 0:8] = rim
        value[:, :, 48:56] = rim
    for tile in (0, CWIDE - 1):
        cred[:, tile, 8:48] = side
    for tile in (0, 1, CWIDE - 2, CWIDE - 1):
        cblack[:, tile, 8:48] = side
    for tile in range(1, CWIDE - 1):
        for m in range(3):
            for chunk in range(5):
                cred[m, tile, 8 + 8 * chunk : 16 + 8 * chunk] = jnp.where(
                    is_red, cscaled[m, tile, 8 * chunk : 8 * chunk + 8], 0.0
                )

    def coarse_sweep(colour, chunks):
        other = corr[1 - colour]
        for tile in range(2, CWIDE - 2):
            for m in range(3):
                for chunk in chunks:
                    row = 8 + 8 * chunk
                    here = other[m, tile, row : row + 8]
                    total = other[m, tile, row - 1 : row + 7] + other[m, tile, row + 1 : row + 9]
                    before = other[m, tile - 1, row : row + 8]
                    after = other[m, tile + 1, row : row + 8]
                    total = total + pltpu.roll(jnp.where(lane_high, before, here), 16, 1)
                    total = total + pltpu.roll(jnp.where(lane_low, after, here), 112, 1)
                    total = total + jnp.where(first, 0.0, pltpu.roll(here, 1, 1))
                    total = total + jnp.where(last, 0.0, pltpu.roll(here, 127, 1))
                    rows = slice(8 * chunk, 8 * chunk + 8)
                    new = cscaled[m, tile, rows] + cratio[m, tile, rows] * total
                    corr[colour][m, tile, row : row + 8] = jnp.where(chosen[colour], new, 0.0)

    for sweep, chunks in enumerate((5, 5, 4, 4, 4, 4)):
        coarse_sweep((sweep + 1) % 2, range(chunks))
    coarse_sweep(1, range(1, 4))

    total = partial[...]
    for slot in range(SLOTS):
        for m in range(3):
            for chunk in range(2):
                row = 8 + CHALO + 8 * chunk
                both = cred[m, slot + 3, row : row + 8] + cblack[m, slot + 3, row : row + 8]
                total = total + 8.0 * (coarse[m, slot, 8 * chunk : 8 * chunk + 8] * both)
    cells = jnp.full((1, 128), info[1], jnp.int32).astype(F32)
    cells = cells * (3.0 * lax.axis_size(SLAB_AXIS) * 32 * 512)
    part = jnp.sum(total, axis=0, keepdims=True) / cells / previous[0]
    share[...] = jnp.broadcast_to(part, share.shape)

    low = 8 + CHALO - 2
    for ctile in range(2, CWIDE - 2):
        for m in range(3):
            wanted[ctile - 2, NARROW // 2 * m : NARROW // 2 * (m + 1)] = (
                cred[m, ctile, low : low + NARROW // 2] + cblack[m, ctile, low : low + NARROW // 2]
            )


def up_kernel(
    info, factor, packed, rim, edge_a, edge_b, pre_red, pre_black, wanted, old, smoothed, carried,
    scaled, ratio, red, black, spread, filled, sem
):
    carry = pltpu.make_async_copy(old, carried, sem.at[SLOTS])
    carry.start()
    held, odd = info[0], info[2] == 1
    skip = (ROWS - NARROW) // 2
    load_fine(held, odd, factor, packed, rim, edge_a, edge_b, scaled, ratio, skip, NARROW)
    masks = fine_masks()
    values = (red, black)
    clear_rim(red, NARROW)
    clear_rim(black, NARROW)
    widen = spread_matrix()
    half_rows = NARROW // 2
    for ctile in range(2, CWIDE - 2):
        wide = exact_dot(wanted[ctile - 2], widen)
        for half in range(2):
            tile = 2 * (ctile - 3) + half + 2
            if not 1 <= tile <= WIDE - 2:
                continue
            for m in range(3):
                piece = wide[half_rows * m : half_rows * m + half_rows, 128 * half : 128 * half + 128]
                spread[m, tile, pl.ds(0, half_rows, stride=2)] = piece
                spread[m, tile, pl.ds(1, half_rows, stride=2)] = piece
    for value, old in ((red, pre_red), (black, pre_black)):
        for tile in range(1, WIDE - 1):
            for m in range(3):
                value[m, tile, 8 : 8 + NARROW] = old[m, tile - 1] + spread[m, tile]
    chunks = range(NARROW // 8)
    for _ in range(2):
        fine_sweep(values, scaled, ratio, 1, masks, chunks)
        fine_sweep(values, scaled, ratio, 0, masks, chunks)

    merge = merge_matrix()
    even = even_cells(3 * 32)
    own = slice(12, 44)
    copies = []
    for slot in range(SLOTS):
        live = slot < held
        for half in range(2):
            tile = 2 + 2 * slot + half
            reds = jnp.concatenate([red[m, tile, own] for m in range(3)], axis=0)
            blacks = jnp.concatenate([black[m, tile, own] for m in range(3)], axis=0)
            both = jnp.concatenate(
                [jnp.where(even, reds, blacks), jnp.where(even, blacks, reds)], axis=1
            )
            cells = exact_dot(jnp.where(live, both, 0.0), merge)
            for m in range(3):
                lanes = slice(256 * half, 256 * half + 256)
                filled[slot, m, :, lanes] = cells[32 * m : 32 * m + 32]
        copies.append(pltpu.make_async_copy(filled.at[slot], smoothed.at[slot], sem.at[slot]))
        copies[-1].start()
    for copy in copies + [carry]:
        copy.wait()


def add_kernel(shares, kept_red, kept_black, kept, total):
    total[...] = jnp.broadcast_to(jnp.sum(shares[...], axis=0, keepdims=True), total.shape)


def direction_kernel(
    info, shares, smoothed, old, same, direction, ready, ready_old, filled, sem
):
    held = info[0]
    fetches = []
    for slot in range(SLOTS):
        fetch = pltpu.make_async_copy(smoothed.at[slot], ready.at[slot], sem.at[slot])
        fetch_old = pltpu.make_async_copy(old.at[slot], ready_old.at[slot], sem.at[SLOTS + slot])
        fetch.start()
        fetch_old.start()
        fetches.append((fetch, fetch_old))
    ratio = jnp.sum(shares[...])
    copies = []
    for slot in range(SLOTS):
        for fetch in fetches[slot]:
            fetch.wait()
        filled[slot] = jnp.where(slot < held, ready[slot] + ratio * ready_old[slot], 0.0)
        target = direction.at[slot]
        copies.append(pltpu.make_async_copy(filled.at[slot], target, sem.at[2 * SLOTS + slot]))
        copies[-1].start()
    for copy in copies:
        copy.wait()


def shape(*dims):
    return jax.ShapeDtypeStruct(dims, F32)


SMEM = pl.BlockSpec(memory_space=pltpu.SMEM)
WHOLE = pl.BlockSpec(memory_space=pltpu.VMEM)
ANYWHERE = pl.BlockSpec(memory_space=pl.ANY)
IN_HBM = pl.BlockSpec(memory_space=pltpu.HBM)


def slot_block(*dims):
    return pl.BlockSpec((1,) + dims, lambda q: (q,) + (0,) * len(dims))


def per_device(box_counts, viscosity, implicit_coef, right_side, old_direction, previous_dot):
    group_n = lax.axis_size(GROUP_AXES)
    slab_n = lax.axis_size(SLAB_AXIS)
    right, coef = right_side[0], implicit_coef[0]
    params = pltpu.CompilerParams(vmem_limit_bytes=VMEM_BYTES)

    place = lax.axis_index(GROUP_AXES)
    info = jnp.stack(
        [
            lax.dynamic_index_in_dim(box_counts, place, 0, keepdims=False),
            jnp.sum(box_counts),
            place % 2,
            lax.axis_index(SLAB_AXIS) % 2,
        ]
    ).astype(jnp.int32)

    top = jnp.concatenate([right[:, :, :8], coef[:, None, :8]], axis=1)
    bottom = jnp.concatenate([right[:, :, 24:], coef[:, None, 24:]], axis=1)
    above = lax.ppermute(bottom, SLAB_AXIS, [(i, i + 1) for i in range(slab_n - 1)])
    below = lax.ppermute(top, SLAB_AXIS, [(i + 1, i) for i in range(slab_n - 1)])

    packed = pl.pallas_call(
        pack_kernel,
        grid=(SLOTS,),
        in_specs=[SMEM, slot_block(3, 32, 512), slot_block(32, 512)],
        out_specs=pl.BlockSpec((4, 2, 2, 32, 128), lambda q: (0, 0, q, 0, 0)),
        out_shape=shape(4, 2, TILES, 32, 128),
        compiler_params=params,
        cost_estimate=pl.CostEstimate(flops=20000000, bytes_accessed=2000000, transcendentals=0),
        name="pack",
    )(info, right, coef)
    edges = pl.pallas_call(
        pack_edges_kernel,
        in_specs=[SMEM] + [WHOLE] * 3,
        out_specs=[WHOLE] * 2,
        out_shape=[shape(4, 2, ROWS, 128)] * 2,
        compiler_params=params,
        name="pack_edges",
    )(info, above, below, packed)
    edges = exchange(*edges, GROUP_AXES)
    rim = pl.pallas_call(
        pack_rim_kernel,
        in_specs=[SMEM] + [WHOLE] * 2,
        out_specs=WHOLE,
        out_shape=shape(4, 2, TILES, 16, 128),
        compiler_params=params,
        cost_estimate=pl.CostEstimate(flops=10000000, bytes_accessed=1000000, transcendentals=0),
        name="pack_rim",
    )(info, above, below)

    padded = pltpu.VMEM((3, WIDE, ROWS + 16, 128), F32)
    pre_shape = shape(3, WIDE - 2, NARROW, 128)
    fine = pltpu.VMEM((3, 2, WIDE, ROWS, 128), F32)
    layer_shape = shape(4, SLOTS * CHALO, 128)
    pre_red, pre_black, coarse, *layers, partial = pl.pallas_call(
        down_kernel,
        in_specs=[SMEM] * 2 + [WHOLE] * 4,
        out_specs=[WHOLE] * 6,
        out_shape=[
            pre_shape,
            pre_shape,
            shape(4, SLOTS, COWN, 128),
            layer_shape,
            layer_shape,
            shape(8, 128),
        ],
        scratch_shapes=[fine, fine, padded, padded, pltpu.VMEM((4, TILES, 32, 128), F32)],
        compiler_params=params,
        name="down",
    )(info, viscosity, packed, rim, *edges)

    layers = exchange(*layers, SLAB_AXIS)
    coarse_edges = pl.pallas_call(
        edges_kernel,
        in_specs=[SMEM] + [WHOLE] * 5,
        out_specs=[WHOLE] * 2,
        out_shape=[shape(4, 2 * CROWS, 128)] * 2,
        compiler_params=params,
        name="edges",
    )(info, coarse, *layers, pre_red, pre_black)
    coarse_edges = exchange(*coarse_edges, GROUP_AXES)

    narrow = pltpu.VMEM((3, 2, WIDE, NARROW, 128), F32)
    value = pltpu.VMEM((3, WIDE, NARROW + 16, 128), F32)
    cfine = pltpu.VMEM((3, CWIDE, 40, 128), F32)
    cvalue = pltpu.VMEM((3, CWIDE, 56, 128), F32)
    wanted, share = pl.pallas_call(
        solve_kernel,
        in_specs=[SMEM] * 3 + [WHOLE] * 8,
        out_specs=[WHOLE] * 2,
        out_shape=[shape(CWIDE - 4, 3 * NARROW // 2, 128), shape(group_n, 128)],
        scratch_shapes=[cfine, cfine, cvalue, cvalue],
        compiler_params=params,
        name="solve",
    )(info, viscosity, previous_dot, coarse, *layers, *coarse_edges, partial, pre_red, pre_black)

    whole = shape(SLOTS, 3, 32, 512)
    held_whole = pltpu.VMEM((SLOTS, 3, 32, 512), F32)
    smoothed, carried = pl.pallas_call(
        up_kernel,
        in_specs=[SMEM] * 2 + [WHOLE] * 7 + [ANYWHERE],
        out_specs=[IN_HBM] * 2,
        out_shape=[whole] * 2,
        scratch_shapes=[
            narrow,
            narrow,
            value,
            value,
            pltpu.VMEM((3, WIDE, NARROW, 128), F32),
            held_whole,
            pltpu.SemaphoreType.DMA((SLOTS + 1,)),
        ],
        compiler_params=params,
        cost_estimate=pl.CostEstimate(flops=40000000, bytes_accessed=8000000, transcendentals=0),
        name="up",
    )(
        info, viscosity, packed, rim, *edges, pre_red, pre_black, wanted, old_direction[0]
    )

    shares = lax.all_to_all(share, GROUP_AXES, 0, 0)
    shares = pl.pallas_call(
        add_kernel,
        in_specs=[WHOLE] * 4,
        out_specs=WHOLE,
        out_shape=shape(slab_n, 128),
        compiler_params=params,
        name="add",
    )(shares, pre_red, pre_black, wanted)
    shares = lax.all_to_all(shares, SLAB_AXIS, 0, 0)
    smoothed, direction = pl.pallas_call(
        direction_kernel,
        in_specs=[SMEM, WHOLE, IN_HBM, IN_HBM],
        out_specs=[IN_HBM] * 2,
        out_shape=[whole] * 2,
        input_output_aliases={2: 0, 3: 1},
        scratch_shapes=[held_whole] * 3 + [pltpu.SemaphoreType.DMA((3 * SLOTS,))],
        compiler_params=params,
        name="direction",
    )(info, shares, smoothed, carried)
    return smoothed[None], direction[None]


def solution(mesh):
    wide = P("gx", GROUP_AXES, None, None, None)
    placed = (P(), P(), P("gx", GROUP_AXES, None, None), wide, wide, P())
    return jax.shard_map(
        per_device, mesh=mesh, in_specs=placed, out_specs=(wide, wide), check_vma=False
    )
```

time: 119 us -> 103 us (0.87)
  waiting for transfers between devices: 23 us -> 12.7 us
  starting transfers between devices: 42 us -> 47 us
  Pallas kernels: 23.5 us -> 20.3 us
  other arithmetic: 4.44 us -> 1.93 us
  blocking collectives: 17.1 us -> 14.8 us
  between operations: 3.85 us -> 1.66 us
    ppermute x8, waiting for transfers between devices: 14.2 us -> 7.29 us  [the longest x6 6.39 us: swap(): return lax.ppermute(value, axis, pairs)]
    all_to_all x1, starting transfers between devices: 12.8 us -> 17.8 us  [per_device(): shares = lax.all_to_all(shares, SLAB_AXIS, 0, 0)]
    all_to_all x1, waiting for transfers between devices: 8.82 us -> 5.36 us  [per_device(): shares = lax.all_to_all(shares, SLAB_AXIS, 0, 0)]
    pallas_call x2 -> x8, Pallas kernels: 21.3 us -> 18.4 us  [the longest x1 4.71 us: per_device(): pl.pallas_call(up_kernel, in_specs=[SMEM] * 2 + [WHOLE] * 7 + [ANYWHERE],...]
    broadcast_in_dim x1 -> x0, other arithmetic: 2.52 us -> none  [per_device(): return (smoothed[None], direction[None])]
    all_to_all x1, blocking collectives: 17.1 us -> 14.8 us  [per_device(): shares = lax.all_to_all(share, GROUP_AXES, 0, 0)]
    another operation x0 -> x1, other arithmetic: none -> 1.26 us  [per_device(): jnp.stack([lax.dynamic_index_in_dim(box_counts, place, 0, keepdims=False)...]
  transfers between devices with their start and end apart: 9 -> 9, of which waited for: 8 -> 5; matrix products, arithmetic and copies ran while one was open for 2% -> 2% of each run, Pallas kernels for 0% -> 8%
where the time goes in v2:
time: 103 us
  starting transfers between devices  47 us (46%)
  Pallas kernels  20.3 us (20%)
  blocking collectives  14.8 us (14%)
  waiting for transfers between devices  12.7 us (12%)
  local copies, waits for them, and re-layouts  4.4 us (4%)
  other arithmetic  1.93 us (2%)
  between operations  1.66 us (2%)
    ppermute x6, starting transfers between devices, swap(): return lax.ppermute(value, axis, pairs)  23.4 us
    all_to_all x1, starting transfers between devices, per_device(): shares = lax.all_to_all(shares, SLAB_AXIS, 0, 0)  17.8 us
    all_to_all x1, blocking collectives, per_device(): shares = lax.all_to_all(share, GROUP_AXES, 0, 0)  14.8 us
    ppermute x6, waiting for transfers between devices, swap(): return lax.ppermute(value, axis, pairs)  6.39 us
    all_to_all x1, waiting for transfers between devices, per_device(): shares = lax.all_to_all(shares, SLAB_AXIS, 0, 0)  5.36 us
    pallas_call x1, Pallas kernels, per_device(): pl.pallas_call(up_kernel, in_specs=[SMEM] * 2 + [WHOLE] * 7 + [ANYWHERE],...  4.71 us
    ppermute x1, starting transfers between devices, per_device(): lax.ppermute(bottom, SLAB_AXIS, [(i, i + 1) for i in range(slab_n - 1)])  4.39 us
    pallas_call x1, Pallas kernels, per_device(): pl.pallas_call(down_kernel, in_specs=[SMEM] * 2 + [WHOLE] * 4, out_specs=...  4.35 us
  transfers between devices with their start and end apart: 9, of which 5 were waited for; matrix products, arithmetic and copies ran while one was open for 2% of the time, Pallas kernels for 8%

profile of v2, /device:TPU:1, one launch (start us, length us, event | category | flops | bytes accessed | tf_op | source)
XLA Modules:
  0.0 102.7 jit_solution(16180778005588855353)
XLA Ops:
  0.6 0.9 slice_bitcast_fusion
  1.5 0.0 copy-start
  1.5 1.1 %fusion = (f32[4,3,8,512]{3,2,1,0:T(8,128)S(1)}, f32[4,3,8,512]{3,2,1,0:T(8,128)S(1)}) fusion(f32[4,3,32,512]{3,2,1,0:T(8,128)} %bitcast.22), kind=kLoop, calls=%fused_computation.5 | loop fusion | bytes 786432 | tf_op jit(solution)/shard_map/slice | solution.py:527
  2.7 4.4 %collective-permute-start = (f32[4,4,8,512]{3,2,1,0:T(8,128)S(1)}, f32[4,4,8,512]{3,2,1,0:T(8,128)S(1)}, u32[]{:S(2)}, u32[]{:S(2)}) collective-permute-start(f32[4,4,8,512]{3,2,1,0:T(8,128)S(1)} %pad_maximum_fusion), channel_id=1, source_target_pairs={{0,32},{32,64},{64,96},{96,128},{128,160},{160,192},{192,224},{224... | collective-permute-start | bytes 786440 | tf_op jit(solution)/shard_map/ppermute | solution.py:529
  7.1 0.0 copy-start.2
  7.1 1.4 %collective-permute-start.1 = (f32[4,4,8,512]{3,2,1,0:T(8,128)S(1)}, f32[4,4,8,512]{3,2,1,0:T(8,128)S(1)}, u32[]{:S(2)}, u32[]{:S(2)}) collective-permute-start(f32[4,4,8,512]{3,2,1,0:T(8,128)S(1)} %pad_maximum_fusion.1), channel_id=1, source_target_pairs={{32,0},{64,32},{96,64},{128,96},{160,128},{192,160},{224,192},{256... | collective-permute-start | bytes 786440 | tf_op jit(solution)/shard_map/ppermute | solution.py:530
  8.6 0.0 copy-start.4
  8.6 0.6 copy-done.4
  9.2 0.6 reduce_sum.9
  9.9 0.6 dynamic_slice.4
  10.4 1.3 %pad_add_fusion.info = s32[4]{0:T(128)S(1)} fusion(s32[1]{0:T(128)} %bitcast.2, s32[1]{0:T(128)} %bitcast.1, s32[1]{0:T(128)} %bitcast, s32[1]{0:T(128)} %dynamic_slice.4), kind=kLoop, calls=%fused_computation.4 | loop fusion | flops 12 | bytes 32 | tf_op jit(solution)/shard_map/stack | solution.py:518
  11.7 0.0 copy-done
  11.7 0.0 copy-done.2
  11.7 1.9 %pack.1.packed = f32[4,2,8,32,128]{4,3,2,1,0:T(8,128)S(1)} custom-call(s32[4]{0:T(128)S(1)} %pad_add_fusion.info, f32[4,3,32,512]{3,2,1,0:T(8,128)S(1)} %bitcast.23, f32[4,32,512]{2,1,0:T(8,128)S(1)} %bitcast.26), custom_call_target="tpu_custom_call" | custom-call | flops 20000000 | bytes 2000000 | tf_op jit(solution)/shard_map/pack/pallas_call | solution.py:532
  13.6 0.0 collective-permute-done.above
  13.6 0.9 collective-permute-done.1.below
  14.5 1.1 %pack_edges.1 = (f32[4,2,48,128]{3,2,1,0:T(8,128)S(1)}, f32[4,2,48,128]{3,2,1,0:T(8,128)S(1)}) custom-call(s32[4]{0:T(128)S(1)} %pad_add_fusion.info, f32[4,4,8,512]{3,2,1,0:T(8,128)S(1)} %collective-permute-done.above, f32[4,4,8,512]{3,2,1,0:T(8,128)S(1)} %collective-permute-done.1.below, f32[4,2,8,32,128]{4,3,2,1,0:T(8,128)S(1)} %pack.1.packed), custom_call_target="tpu_custom_call" | custom-call | tf_op jit(solution)/shard_map/pack_edges/pallas_call | solution.py:542
  15.6 5.0 %collective-permute-start.2 = (f32[4,2,48,128]{3,2,1,0:T(8,128)S(1)}, f32[4,2,48,128]{3,2,1,0:T(8,128)S(1)}, u32[]{:S(2)}, u32[]{:S(2)}) collective-permute-start(f32[4,2,48,128]{3,2,1,0:T(8,128)S(1)} %get-tuple-element.18), channel_id=1, source_target_pairs={{0,1},{1,0},{2,3},{3,2},{4,5},{5,4},{6,7},{7,6},{8,9},{9,8},{10,11... | collective-permute-start | bytes 589832 | tf_op jit(solution)/shard_map/ppermute | solution.py:77
  20.6 0.0 copy-start.3
  20.7 5.6 %collective-permute-start.3 = (f32[4,2,48,128]{3,2,1,0:T(8,128)S(1)}, f32[4,2,48,128]{3,2,1,0:T(8,128)S(1)}, u32[]{:S(2)}, u32[]{:S(2)}) collective-permute-start(f32[4,2,48,128]{3,2,1,0:T(8,128)S(1)} %get-tuple-element.19), channel_id=1, source_target_pairs={{1,2},{2,1},{3,4},{4,3},{5,6},{6,5},{7,8},{8,7},{9,10},{10,9},{11,... | collective-permute-start | bytes 589832 | tf_op jit(solution)/shard_map/ppermute | solution.py:77
  26.3 1.2 %pack_rim.1.rim = f32[4,2,8,16,128]{4,3,2,1,0:T(8,128)S(1)} custom-call(s32[4]{0:T(128)S(1)} %pad_add_fusion.info, f32[4,4,8,512]{3,2,1,0:T(8,128)S(1)} %collective-permute-done.above, f32[4,4,8,512]{3,2,1,0:T(8,128)S(1)} %collective-permute-done.1.below), custom_call_target="tpu_custom_call" | custom-call | flops 10000000 | bytes 1000000 | tf_op jit(solution)/shard_map/pack_rim/pallas_call | solution.py:551
  27.5 0.0 collective-permute-done.2.edge_a
  27.6 3.1 %collective-permute-done.3.edge_b = f32[4,2,48,128]{3,2,1,0:T(8,128)S(1)} collective-permute-done((f32[4,2,48,128]{3,2,1,0:T(8,128)S(1)}, f32[4,2,48,128]{3,2,1,0:T(8,128)S(1)}, u32[]{:S(2)}, u32[]{:S(2)}) %collective-permute-start.3) | collective-permute-done | bytes 196640 | tf_op jit(solution)/shard_map/ppermute | solution.py:77
  30.6 0.0 copy-done.3
  30.6 4.4 %down.1 = (f32[3,10,40,128]{3,2,1,0:T(8,128)S(1)}, f32[3,10,40,128]{3,2,1,0:T(8,128)S(1)}, f32[4,4,16,128]{3,2,1,0:T(8,128)S(1)}, f32[4,40,128]{2,1,0:T(8,128)S(...) custom-call(s32[4]{0:T(128)S(1)} %pad_add_fusion.info, f32[3]{0:T(128)S(1)} %copy-done.3, ...), custom_call_target="tpu_custom_call" | custom-call | tf_op jit(solution)/shard_map/down/pallas_call | solution.py:565
  35.0 3.6 %collective-permute-start.4 = (f32[4,40,128]{2,1,0:T(8,128)S(1)}, f32[4,40,128]{2,1,0:T(8,128)S(1)}, u32[]{:S(2)}, u32[]{:S(2)}) collective-permute-start(f32[4,40,128]{2,1,0:T(8,128)S(1)} %get-tuple-element.21), channel_id=1, source_target_pairs={{0,32},{32,0},{64,96},{96,64},{128,160},{160,128},{192,224},{224,1... | collective-permute-start | bytes 245768 | tf_op jit(solution)/shard_map/ppermute | solution.py:77
  38.6 0.7 collective-permute-start.5
  39.2 1.1 %collective-permute-done.4.layers_a = f32[4,40,128]{2,1,0:T(8,128)S(1)} collective-permute-done((f32[4,40,128]{2,1,0:T(8,128)S(1)}, f32[4,40,128]{2,1,0:T(8,128)S(1)}, u32[]{:S(2)}, u32[]{:S(2)}) %collective-permute-start.4) | collective-permute-done | bytes 81952 | tf_op jit(solution)/shard_map/ppermute | solution.py:77
  40.4 0.0 collective-permute-done.5.layers_b
  40.4 0.6 edges.1
  41.0 1.9 %collective-permute-start.6 = (f32[4,72,128]{2,1,0:T(8,128)S(1)}, f32[4,72,128]{2,1,0:T(8,128)S(1)}, u32[]{:S(2)}, u32[]{:S(2)}) collective-permute-start(f32[4,72,128]{2,1,0:T(8,128)S(1)} %get-tuple-element.25), channel_id=1, source_target_pairs={{0,1},{1,0},{2,3},{3,2},{4,5},{5,4},{6,7},{7,6},{8,9},{9,8},{10,11... | collective-permute-start | bytes 442376 | tf_op jit(solution)/shard_map/ppermute | solution.py:77
  42.9 6.5 %collective-permute-start.7 = (f32[4,72,128]{2,1,0:T(8,128)S(1)}, f32[4,72,128]{2,1,0:T(8,128)S(1)}, u32[]{:S(2)}, u32[]{:S(2)}) collective-permute-start(f32[4,72,128]{2,1,0:T(8,128)S(1)} %get-tuple-element.26), channel_id=1, source_target_pairs={{1,2},{2,1},{3,4},{4,3},{5,6},{6,5},{7,8},{8,7},{9,10},{10,9},{11,... | collective-permute-start | bytes 442376 | tf_op jit(solution)/shard_map/ppermute | solution.py:77
  50.1 0.0 collective-permute-done.6.coarse_a
  50.1 2.2 %collective-permute-done.7.coarse_b = f32[4,72,128]{2,1,0:T(8,128)S(1)} collective-permute-done((f32[4,72,128]{2,1,0:T(8,128)S(1)}, f32[4,72,128]{2,1,0:T(8,128)S(1)}, u32[]{:S(2)}, u32[]{:S(2)}) %collective-permute-start.7) | collective-permute-done | bytes 147488 | tf_op jit(solution)/shard_map/ppermute | solution.py:77
  52.3 3.0 %solve.1 = (f32[6,60,128]{2,1,0:T(8,128)S(1)}, f32[32,128]{1,0:T(8,128)S(1)}) custom-call(s32[4]{0:T(128)S(1)} %pad_add_fusion.info, f32[3]{0:T(128)S(1)} %copy-done.3, f32[1]{0:T(128)S(6)} %copy.16.previous, f32[4,4,16,128]{3,2,1,0:T(8,128)S(1)} %get-tuple-element.20.coarse, f32[4,40,128]{2,1,0:T(8,128)S(1)} %collective-permute-done.4.layers_a, ...), custom_call_target="tpu_custom_call" | custom-call | tf_op jit(solution)/shard_map/solve/pallas_call | solution.py:597
  55.3 14.8 %all_to_all.22 = f32[32,1,128]{2,1,0:T(1,128)S(1)} all-to-all(f32[32,1,128]{2,1,0:T(1,128)S(1)} %bitcast.29), channel_id=1, replica_groups=mesh['gx'=16,'gy'=8,'gz'=4] {'gy','gz'}, dimensions={0} | all-to-all | bytes 32768 | tf_op jit(solution)/shard_map/all_to_all | solution.py:630
  70.1 0.6 add.25
  70.7 17.8 %all-to-all-start.1 = ((f32[16,1,128]{2,1,0:T(1,128)}), f32[16,1,128]{2,1,0:T(1,128)S(1)}, u32[]{:S(2)}, u32[]{:S(2)}) async-start(f32[16,1,128]{2,1,0:T(1,128)} %bitcast.12), calls=%async_computation.1 | async-start | bytes 16384 | tf_op jit(solution)/shard_map/all_to_all | solution.py:639
  88.5 0.0 copy-start.1
  88.5 1.1 %copy-done.1 = f32[1,4,3,32,512]{4,3,2,1,0:T(8,128)S(1)} copy-done((f32[1,4,3,32,512]{4,3,2,1,0:T(8,128)S(1)}, f32[1,4,3,32,512]{4,3,2,1,0:T(8,128)}, u32[]{:S(2)}) %copy-start.1) | copy-done | bytes 786456
  89.6 4.7 %up.1 = (f32[4,3,32,512]{3,2,1,0:T(8,128)}, f32[4,3,32,512]{3,2,1,0:T(8,128)}) custom-call(s32[4]{0:T(128)S(1)} %pad_add_fusion.info, f32[3]{0:T(128)S(1)} %copy-done.3, f32[4,2,8,32,128]{4,3,2,1,0:T(8,128)S(1)} %pack.1.packed, f32[4,2,8,16,128]{4,3,2,1,0:T(8,128)S(1)} %pack_rim.1.rim, f32[4,2,48,128]{3,2,1,0:T(8,128)S(1)} %collective-permute-done.2.edge_a, ...), custom_call_target="tpu_custom_call" | custom-call | flops 40000000 | bytes 8000000 | tf_op jit(solution)/shard_map/up/pallas_call | solution.py:609
  94.3 5.4 %all-to-all-done.1 = f32[16,1,128]{2,1,0:T(1,128)S(1)} async-done(((f32[16,1,128]{2,1,0:T(1,128)}), f32[16,1,128]{2,1,0:T(1,128)S(1)}, u32[]{:S(2)}, u32[]{:S(2)}) %all-to-all-start.1) | async-done | bytes 8224 | tf_op jit(solution)/shard_map/all_to_all | solution.py:639
  99.7 2.8 %direction.1 = (f32[4,3,32,512]{3,2,1,0:T(8,128)}, f32[4,3,32,512]{3,2,1,0:T(8,128)}) custom-call(s32[4]{0:T(128)S(1)} %pad_add_fusion.info, f32[16,128]{1,0:T(8,128)S(1)} %bitcast.28, f32[4,3,32,512]{3,2,1,0:T(8,128)} %get-tuple-element.30.smoothed, f32[4,3,32,512]{3,2,1,0:T(8,128)} %get-tuple-element.31.old), custom_call_target="tpu_custom_call", output_to_operand_aliasing={{0}: (2, {}), {1}: (3, {})} | custom-call | tf_op jit(solution)/shard_map/direction/pallas_call | solution.py:640
  (2 shorter events, 0.0 us)
Async XLA Ops:
  1.5 10.2 %copy-start = (f32[1,4,3,32,512]{4,3,2,1,0:T(8,128)S(1)}, f32[1,4,3,32,512]{4,3,2,1,0:T(8,128)}, u32[]{:S(2)}) copy-start(f32[1,4,3,32,512]{4,3,2,1,0:T(8,128)} %param.9) | copy-start | bytes 2359300
  2.7 10.9 %collective-permute-start = (f32[4,4,8,512]{3,2,1,0:T(8,128)S(1)}, f32[4,4,8,512]{3,2,1,0:T(8,128)S(1)}, u32[]{:S(2)}, u32[]{:S(2)}) collective-permute-start(f32[4,4,8,512]{3,2,1,0:T(8,128)S(1)} %pad_maximum_fusion), channel_id=1, source_target_pairs={{0,32},{32,64},{64,96},{96,128},{128,160},{160,192},{192,224},{224... | collective-permute-start | bytes 786440 | tf_op jit(solution)/shard_map/ppermute | solution.py:529
  7.1 4.6 %copy-start.2 = (f32[1,4,32,512]{3,2,1,0:T(8,128)S(1)}, f32[1,4,32,512]{3,2,1,0:T(8,128)}, u32[]{:S(2)}) copy-start(f32[1,4,32,512]{3,2,1,0:T(8,128)} %param.8) | copy-start | bytes 786436
  7.1 7.4 %collective-permute-start.1 = (f32[4,4,8,512]{3,2,1,0:T(8,128)S(1)}, f32[4,4,8,512]{3,2,1,0:T(8,128)S(1)}, u32[]{:S(2)}, u32[]{:S(2)}) collective-permute-start(f32[4,4,8,512]{3,2,1,0:T(8,128)S(1)} %pad_maximum_fusion.1), channel_id=1, source_target_pairs={{32,0},{64,32},{96,64},{128,96},{160,128},{192,160},{224,192},{256... | collective-permute-start | bytes 786440 | tf_op jit(solution)/shard_map/ppermute | solution.py:530
  8.6 0.7 copy-start.4
  15.6 12.0 %collective-permute-start.2 = (f32[4,2,48,128]{3,2,1,0:T(8,128)S(1)}, f32[4,2,48,128]{3,2,1,0:T(8,128)S(1)}, u32[]{:S(2)}, u32[]{:S(2)}) collective-permute-start(f32[4,2,48,128]{3,2,1,0:T(8,128)S(1)} %get-tuple-element.18), channel_id=1, source_target_pairs={{0,1},{1,0},{2,3},{3,2},{4,5},{5,4},{6,7},{7,6},{8,9},{9,8},{10,11... | collective-permute-start | bytes 589832 | tf_op jit(solution)/shard_map/ppermute | solution.py:77
  20.6 10.0 %copy-start.3 = (f32[3]{0:T(128)S(1)}, f32[3]{0:T(128)}, u32[]{:S(2)}) copy-start(f32[3]{0:T(128)} %factor.5) | copy-start | bytes 40
  20.7 10.0 %collective-permute-start.3 = (f32[4,2,48,128]{3,2,1,0:T(8,128)S(1)}, f32[4,2,48,128]{3,2,1,0:T(8,128)S(1)}, u32[]{:S(2)}, u32[]{:S(2)}) collective-permute-start(f32[4,2,48,128]{3,2,1,0:T(8,128)S(1)} %get-tuple-element.19), channel_id=1, source_target_pairs={{1,2},{2,1},{3,4},{4,3},{5,6},{6,5},{7,8},{8,7},{9,10},{10,9},{11,... | collective-permute-start | bytes 589832 | tf_op jit(solution)/shard_map/ppermute | solution.py:77
  35.0 5.4 %collective-permute-start.4 = (f32[4,40,128]{2,1,0:T(8,128)S(1)}, f32[4,40,128]{2,1,0:T(8,128)S(1)}, u32[]{:S(2)}, u32[]{:S(2)}) collective-permute-start(f32[4,40,128]{2,1,0:T(8,128)S(1)} %get-tuple-element.21), channel_id=1, source_target_pairs={{0,32},{32,0},{64,96},{96,64},{128,160},{160,128},{192,224},{224,1... | collective-permute-start | bytes 245768 | tf_op jit(solution)/shard_map/ppermute | solution.py:77
  38.6 1.8 %collective-permute-start.5 = (f32[4,40,128]{2,1,0:T(8,128)S(1)}, f32[4,40,128]{2,1,0:T(8,128)S(1)}, u32[]{:S(2)}, u32[]{:S(2)}) collective-permute-start(f32[4,40,128]{2,1,0:T(8,128)S(1)} %get-tuple-element.22), channel_id=1, source_target_pairs={{32,64},{64,32},{96,128},{128,96},{160,192},{192,160},{224,256},{2... | collective-permute-start | bytes 245768 | tf_op jit(solution)/shard_map/ppermute | solution.py:77
  41.0 9.1 %collective-permute-start.6 = (f32[4,72,128]{2,1,0:T(8,128)S(1)}, f32[4,72,128]{2,1,0:T(8,128)S(1)}, u32[]{:S(2)}, u32[]{:S(2)}) collective-permute-start(f32[4,72,128]{2,1,0:T(8,128)S(1)} %get-tuple-element.25), channel_id=1, source_target_pairs={{0,1},{1,0},{2,3},{3,2},{4,5},{5,4},{6,7},{7,6},{8,9},{9,8},{10,11... | collective-permute-start | bytes 442376 | tf_op jit(solution)/shard_map/ppermute | solution.py:77
  42.9 9.4 %collective-permute-start.7 = (f32[4,72,128]{2,1,0:T(8,128)S(1)}, f32[4,72,128]{2,1,0:T(8,128)S(1)}, u32[]{:S(2)}, u32[]{:S(2)}) collective-permute-start(f32[4,72,128]{2,1,0:T(8,128)S(1)} %get-tuple-element.26), channel_id=1, source_target_pairs={{1,2},{2,1},{3,4},{4,3},{5,6},{6,5},{7,8},{8,7},{9,10},{10,9},{11,... | collective-permute-start | bytes 442376 | tf_op jit(solution)/shard_map/ppermute | solution.py:77
  70.7 29.0 %all-to-all-start.1 = ((f32[16,1,128]{2,1,0:T(1,128)}), f32[16,1,128]{2,1,0:T(1,128)S(1)}, u32[]{:S(2)}, u32[]{:S(2)}) async-start(f32[16,1,128]{2,1,0:T(1,128)} %bitcast.12), calls=%async_computation.1 | async-start | bytes 16384 | tf_op jit(solution)/shard_map/all_to_all | solution.py:639
  88.5 1.1 %copy-start.1 = (f32[1,4,3,32,512]{4,3,2,1,0:T(8,128)S(1)}, f32[1,4,3,32,512]{4,3,2,1,0:T(8,128)}, u32[]{:S(2)}) copy-start(f32[1,4,3,32,512]{4,3,2,1,0:T(8,128)} %param.10) | copy-start | bytes 2359300

commit v3 on v2

--- a/solution.py
+++ b/solution.py
@@ -21,6 +21,7 @@
 COWN = 16
 CHALO = 10
 CROWS = COWN + 2 * CHALO
+EXTRA_ROWS = (0, 8, 16, 24, 28)
 CWIDE = SLOTS + 6
 
 
@@ -125,27 +126,27 @@
 
 def pack_edges_kernel(info, above, below, packed, edge_a, edge_b):
     held, odd = info[0], info[2] == 1
-    split = split_matrix()
-    for slot, half in ((0, 0), (held - 1, 1)):
-        lanes = slice(256 * half, 256 * half + 256)
-        parts = []
-        for m in range(4):
+    parts, found = [], {}
+    places = ((0, 0), (held - 1, 1))
+    for m in range(4):
+        for slot, half in places:
+            lanes = slice(256 * half, 256 * half + 256)
             parts += [above[slot, m, :, lanes], below[slot, m, :, lanes]]
-        found = {}
-
-        def put(m, colour, value):
-            found[m, colour] = value
-
-        split_cells(jnp.concatenate(parts, axis=0), 16, split, put)
+
+    def put(m, colour, value):
+        found[m, colour] = value
+
+    split_cells(jnp.concatenate(parts, axis=0), 32, split_matrix(), put)
+    for slot, half in places:
         tile = 2 * slot + half
         for out, when in ((edge_a, odd), (edge_b, jnp.logical_not(odd))):
 
             @pl.when(when if half == 0 else jnp.logical_not(when))
             def _(out=out):
                 for (m, colour), value in found.items():
-                    out[m, colour, 0:8] = value[:8]
+                    out[m, colour, 0:8] = value[16 * half : 16 * half + 8]
                     out[m, colour, 8:40] = packed[m, colour, tile]
-                    out[m, colour, 40:48] = value[8:]
+                    out[m, colour, 40:48] = value[16 * half + 8 : 16 * half + 16]
 
 
 def load_fine(count, odd, factor, packed, rim, edge_a, edge_b, scaled, ratio, skip, rows):
@@ -225,8 +226,8 @@
 
 
 def down_kernel(
-    info, factor, packed, rim, edge_a, edge_b, pre_red, pre_black, coarse, layers_a, layers_b,
-    partial, scaled, ratio, red, black, remain
+    info, factor, packed, rim, edge_a, edge_b, red, black, coarse, layers_a, layers_b, remain,
+    scaled, ratio
 ):
     held, odd, odd_slab = info[0], info[2] == 1, info[3] == 1
     load_fine(held, odd, factor, packed, rim, edge_a, edge_b, scaled, ratio, 0, ROWS)
@@ -240,11 +241,6 @@
     fine_sweep(pre, scaled, ratio, 0, masks, chunks)
     fine_sweep(pre, scaled, ratio, 1, masks, chunks)
 
-    skip = (ROWS - NARROW) // 2
-    pre_red[...] = red[:, 1 : WIDE - 1, 8 + skip : 8 + skip + NARROW]
-    pre_black[...] = black[:, 1 : WIDE - 1, 8 + skip : 8 + skip + NARROW]
-
-    totals = [jnp.zeros((8, 128), F32) for _ in range(4)]
     for tile in range(2, 2 + TILES):
         for chunk in range(1, 5):
             row = 8 + 8 * chunk
@@ -252,33 +248,23 @@
             coef = packed[3, 0, tile - 2, out]
             for m in range(3):
                 reds = red[m, tile, row : row + 8]
-                blacks = black[m, tile, row : row + 8]
                 update = fine_update(black, scaled, ratio, m, 0, tile, chunk, masks)
                 left = (coef + 6.0 * factor[m]) * (update - reds)
-                left = jnp.where(tile < 2 * held + 2, left, 0.0)
-                remain[m, tile - 2, out] = left
-                term = (packed[m, 0, tile - 2, out] + left) * reds
-                totals[m] = totals[m] + term
-                totals[3] = totals[3] + packed[m, 1, tile - 2, out] * blacks
+                remain[m, tile - 2, out] = jnp.where(tile < 2 * held + 2, left, 0.0)
             remain[3, tile - 2, out] = coef + packed[3, 1, tile - 2, out]
-    partial[...] = (totals[0] + totals[1]) + (totals[2] + totals[3])
-    pool = pool_matrix()
+    sides = []
+    for half in range(2):
+        parts = []
+        for tile in range(half, TILES, 2):
+            for m in range(4):
+                first = remain[m, tile, pl.ds(0, COWN, stride=2)]
+                parts.append(first + remain[m, tile, pl.ds(1, COWN, stride=2)])
+        sides.append(jnp.concatenate(parts, axis=0))
+    pooled = exact_dot(jnp.concatenate(sides, axis=1), pool_matrix()) * 0.125
     for slot in range(SLOTS):
-        sides = []
-        for tile in (2 * slot, 2 * slot + 1):
-            sides.append(
-                jnp.concatenate(
-                    [
-                        remain[m, tile, pl.ds(0, COWN, stride=2)]
-                        + remain[m, tile, pl.ds(1, COWN, stride=2)]
-                        for m in range(4)
-                    ],
-                    axis=0,
-                )
-            )
-        pooled = exact_dot(jnp.concatenate(sides, axis=1), pool) * 0.125
         for m in range(4):
-            box = pooled[COWN * m : COWN * m + COWN]
+            place = COWN * (4 * slot + m)
+            box = pooled[place : place + COWN]
             coarse[m, slot] = box
             start, end = box[:CHALO], box[COWN - CHALO :]
             rows = slice(CHALO * slot, CHALO * slot + CHALO)
@@ -286,27 +272,51 @@
             layers_b[m, rows] = jnp.where(odd_slab, end, start)
 
 
-def edges_kernel(info, coarse, layers_a, layers_b, kept_red, kept_black, edge_a, edge_b):
+def keep_kernel(packed, red, black, remain, pre_red, pre_black, partial):
+    skip = (ROWS - NARROW) // 2
+    pre_red[...] = red[:, 1 : WIDE - 1, 8 + skip : 8 + skip + NARROW]
+    pre_black[...] = black[:, 1 : WIDE - 1, 8 + skip : 8 + skip + NARROW]
+    totals = [jnp.zeros((8, 128), F32) for _ in range(6)]
+    for tile in range(TILES):
+        for chunk in range(4):
+            rows, inner = slice(8 * chunk, 8 * chunk + 8), slice(16 + 8 * chunk, 24 + 8 * chunk)
+            for m in range(3):
+                both = packed[m, 0, tile, rows] + remain[m, tile, rows]
+                totals[m] = totals[m] + both * red[m, tile + 2, inner]
+                totals[m + 3] = totals[m + 3] + packed[m, 1, tile, rows] * black[m, tile + 2, inner]
+    partial[...] = sum(totals[1:], totals[0])
+
+
+def edges_kernel(info, coarse, layers_a, layers_b, kept_red, kept_black, edge_a, edge_b, tall):
     held, odd, odd_slab = info[0], info[2] == 1, info[3] == 1
 
-    def fill(out, slots):
-        for n, slot in enumerate(slots):
-            rows = slice(CHALO * slot, CHALO * slot + CHALO)
-            base = CROWS * n
-            for m in range(4):
+    group = iota((8, 128), 1) // 16
+
+    def fill(out, slot, beside, first):
+        for m in range(4):
+            for n, source in enumerate((slot, beside)):
+                rows = slice(CHALO * source, CHALO * source + CHALO)
                 one, other = layers_a[m, rows], layers_b[m, rows]
-                out[m, base : base + CHALO] = jnp.where(odd_slab, one, other)
-                out[m, base + CHALO : base + CHALO + COWN] = coarse[m, slot]
-                out[m, base + CHALO + COWN : base + CROWS] = jnp.where(odd_slab, other, one)
+                target = out if n == 0 else tall
+                target[m, 0:CHALO] = jnp.where(odd_slab, one, other)
+                target[m, CHALO : CHALO + COWN] = coarse[m, source]
+                target[m, CHALO + COWN : CROWS] = jnp.where(odd_slab, other, one)
+            extra = jnp.zeros((8, 128), F32)
+            out[m, CROWS:40] = extra[: 40 - CROWS]
+            for j, row in enumerate(EXTRA_ROWS):
+                turn = 16 * j if first else 16 * (j + 1)
+                piece = pltpu.roll(tall[m, row : row + 8], turn, 1)
+                extra = jnp.where(group == j, piece, extra)
+            out[m, 40:48] = extra
 
     for is_odd in (False, True):
         for count in range(2, SLOTS + 1):
 
             @pl.when((odd == is_odd) & (held == count))
             def _(is_odd=is_odd, count=count):
-                start, end = (0, 1), (count - 2, count - 1)
-                fill(edge_a, start if is_odd else end)
-                fill(edge_b, end if is_odd else start)
+                start, end = (0, 1, True), (count - 1, count - 2, False)
+                fill(edge_a, *(start if is_odd else end))
+                fill(edge_b, *(end if is_odd else start))
 
 
 def solve_kernel(
@@ -340,12 +350,19 @@
         put(slot + 3, 0, above)
         put(slot + 3, CHALO, [coarse[m, slot] for m in range(4)])
         put(slot + 3, CHALO + COWN, below)
-    for side in range(2):
-        rows = slice(CROWS * side, CROWS * side + CROWS)
-        put(jnp.where(odd, 1, held + 3) + side, 0, [coarse_a[m, rows] for m in range(4)])
-        put(jnp.where(odd, held + 3, 1) + side, 0, [coarse_b[m, rows] for m in range(4)])
-
     lane = iota((8, 128), 1)
+    for edge, is_left in ((coarse_a, odd), (coarse_b, jnp.logical_not(odd))):
+        put(jnp.where(is_left, 2, held + 3), 0, [edge[m, 0:CROWS] for m in range(4)])
+        tile = jnp.where(is_left, 1, held + 4)
+        for j, row in enumerate(EXTRA_ROWS):
+            pieces = []
+            for m in range(4):
+                extra = edge[m, 40:48]
+                left = jnp.where(lane >= 112, pltpu.roll(extra, (112 - 16 * j) % 128, 1), 0.0)
+                right = jnp.where(lane < 16, pltpu.roll(extra, (128 - 16 * j) % 128, 1), 0.0)
+                pieces.append(jnp.where(is_left, left, right))
+            put(tile, row, pieces)
+
     lane_low, lane_high = lane < 16, lane >= 112
     first, last = lane % 16 == 0, lane % 16 == 15
     is_red = (iota((8, 128), 0) + lane // 16 + lane % 16) % 2 == 0
@@ -558,33 +575,42 @@
         name="pack_rim",
     )(info, above, below)
 
-    padded = pltpu.VMEM((3, WIDE, ROWS + 16, 128), F32)
-    pre_shape = shape(3, WIDE - 2, NARROW, 128)
+    padded = shape(3, WIDE, ROWS + 16, 128)
     fine = pltpu.VMEM((3, 2, WIDE, ROWS, 128), F32)
     layer_shape = shape(4, SLOTS * CHALO, 128)
-    pre_red, pre_black, coarse, *layers, partial = pl.pallas_call(
+    red, black, coarse, *layers, remain = pl.pallas_call(
         down_kernel,
         in_specs=[SMEM] * 2 + [WHOLE] * 4,
         out_specs=[WHOLE] * 6,
         out_shape=[
-            pre_shape,
-            pre_shape,
+            padded,
+            padded,
             shape(4, SLOTS, COWN, 128),
             layer_shape,
             layer_shape,
-            shape(8, 128),
+            shape(4, TILES, 32, 128),
         ],
-        scratch_shapes=[fine, fine, padded, padded, pltpu.VMEM((4, TILES, 32, 128), F32)],
+        scratch_shapes=[fine, fine],
         compiler_params=params,
         name="down",
     )(info, viscosity, packed, rim, *edges)
 
     layers = exchange(*layers, SLAB_AXIS)
+    pre_red, pre_black, partial = pl.pallas_call(
+        keep_kernel,
+        in_specs=[WHOLE] * 4,
+        out_specs=[WHOLE] * 3,
+        out_shape=[shape(3, WIDE - 2, NARROW, 128)] * 2 + [shape(8, 128)],
+        compiler_params=params,
+        cost_estimate=pl.CostEstimate(flops=4000000, bytes_accessed=1000000, transcendentals=0),
+        name="keep",
+    )(packed, red, black, remain)
     coarse_edges = pl.pallas_call(
         edges_kernel,
         in_specs=[SMEM] + [WHOLE] * 5,
         out_specs=[WHOLE] * 2,
-        out_shape=[shape(4, 2 * CROWS, 128)] * 2,
+        out_shape=[shape(4, 48, 128)] * 2,
+        scratch_shapes=[pltpu.VMEM((4, 40, 128), F32)],
         compiler_params=params,
         name="edges",
     )(info, coarse, *layers, pre_red, pre_black)

time: 103 us -> 102 us (level)
  transfers between devices with their start and end apart: 9 -> 9, of which waited for: 5 -> 5; matrix products, arithmetic and copies ran while one was open for 2% -> 3% of each run, Pallas kernels for 8% -> 8%
where the time goes in v3:
time: 102 us
  starting transfers between devices  46.8 us (46%)
  Pallas kernels  20.1 us (20%)
  blocking collectives  14.8 us (15%)
  waiting for transfers between devices  12.4 us (12%)
  local copies, waits for them, and re-layouts  3.79 us (4%)
  other arithmetic  2.01 us (2%)
  between operations  1.67 us (2%)
    ppermute x6, starting transfers between devices, swap(): return lax.ppermute(value, axis, pairs)  23.4 us
    all_to_all x1, starting transfers between devices, per_device(): shares = lax.all_to_all(shares, SLAB_AXIS, 0, 0)  17.8 us
    all_to_all x1, blocking collectives, per_device(): shares = lax.all_to_all(share, GROUP_AXES, 0, 0)  14.8 us
    ppermute x6, waiting for transfers between devices, swap(): return lax.ppermute(value, axis, pairs)  5.63 us
    all_to_all x1, waiting for transfers between devices, per_device(): shares = lax.all_to_all(shares, SLAB_AXIS, 0, 0)  5.36 us
    pallas_call x1, Pallas kernels, per_device(): pl.pallas_call(up_kernel, in_specs=[SMEM] * 2 + [WHOLE] * 7 + [ANYWHERE],...  4.71 us
    ppermute x1, starting transfers between devices, per_device(): lax.ppermute(bottom, SLAB_AXIS, [(i, i + 1) for i in range(slab_n - 1)])  4.39 us
    pallas_call x1, Pallas kernels, per_device(): pl.pallas_call(down_kernel, in_specs=[SMEM] * 2 + [WHOLE] * 4, out_specs=...  4.06 us
  transfers between devices with their start and end apart: 9, of which 5 were waited for; matrix products, arithmetic and copies ran while one was open for 3% of the time, Pallas kernels for 8%

profile of v3, /device:TPU:1, one launch (start us, length us, event | category | flops | bytes accessed | tf_op | source)
XLA Modules:
  0.0 101.6 jit_solution(12922579768287096712)
XLA Ops:
  0.6 0.0 copy-start
  0.6 0.0 copy-start.2
  0.7 0.0 copy-start.4
  0.7 1.1 %fusion = (f32[4,3,8,512]{3,2,1,0:T(8,128)S(1)}, f32[4,3,8,512]{3,2,1,0:T(8,128)S(1)}) fusion(f32[4,3,32,512]{3,2,1,0:T(8,128)} %bitcast.22), kind=kLoop, calls=%fused_computation.5 | loop fusion | bytes 786432 | tf_op jit(solution)/shard_map/slice | solution.py:544
  1.8 0.9 slice_bitcast_fusion
  2.7 4.4 %collective-permute-start = (f32[4,4,8,512]{3,2,1,0:T(8,128)S(1)}, f32[4,4,8,512]{3,2,1,0:T(8,128)S(1)}, u32[]{:S(2)}, u32[]{:S(2)}) collective-permute-start(f32[4,4,8,512]{3,2,1,0:T(8,128)S(1)} %pad_maximum_fusion), channel_id=1, source_target_pairs={{0,32},{32,64},{64,96},{96,128},{128,160},{160,192},{192,224},{224... | collective-permute-start | bytes 786440 | tf_op jit(solution)/shard_map/ppermute | solution.py:546
  7.1 1.3 %collective-permute-start.1 = (f32[4,4,8,512]{3,2,1,0:T(8,128)S(1)}, f32[4,4,8,512]{3,2,1,0:T(8,128)S(1)}, u32[]{:S(2)}, u32[]{:S(2)}) collective-permute-start(f32[4,4,8,512]{3,2,1,0:T(8,128)S(1)} %pad_maximum_fusion.1), channel_id=1, source_target_pairs={{32,0},{64,32},{96,64},{128,96},{160,128},{192,160},{224,192},{256... | collective-permute-start | bytes 786440 | tf_op jit(solution)/shard_map/ppermute | solution.py:547
  8.5 0.0 copy-done.4
  8.5 0.6 reduce_sum.9
  9.1 0.6 dynamic_slice.4
  9.7 1.3 %pad_add_fusion.info = s32[4]{0:T(128)S(1)} fusion(s32[1]{0:T(128)} %bitcast.2, s32[1]{0:T(128)} %bitcast.1, s32[1]{0:T(128)} %bitcast, s32[1]{0:T(128)} %dynamic_slice.4), kind=kLoop, calls=%fused_computation.4 | loop fusion | flops 12 | bytes 32 | tf_op jit(solution)/shard_map/stack | solution.py:535
  11.1 0.0 copy-done
  11.1 0.0 copy-done.2
  11.1 1.9 %pack.1.packed = f32[4,2,8,32,128]{4,3,2,1,0:T(8,128)S(1)} custom-call(s32[4]{0:T(128)S(1)} %pad_add_fusion.info, f32[4,3,32,512]{3,2,1,0:T(8,128)S(1)} %bitcast.23, f32[4,32,512]{2,1,0:T(8,128)S(1)} %bitcast.26), custom_call_target="tpu_custom_call" | custom-call | flops 20000000 | bytes 2000000 | tf_op jit(solution)/shard_map/pack/pallas_call | solution.py:549
  13.0 0.0 copy-start.3
  13.0 0.0 collective-permute-done.above
  13.0 1.4 %collective-permute-done.1.below = f32[4,4,8,512]{3,2,1,0:T(8,128)S(1)} collective-permute-done((f32[4,4,8,512]{3,2,1,0:T(8,128)S(1)}, f32[4,4,8,512]{3,2,1,0:T(8,128)S(1)}, u32[]{:S(2)}, u32[]{:S(2)}) %collective-permute-start.1) | collective-permute-done | bytes 262176 | tf_op jit(solution)/shard_map/ppermute | solution.py:547
  14.4 0.8 pack_edges.1
  15.3 5.0 %collective-permute-start.2 = (f32[4,2,48,128]{3,2,1,0:T(8,128)S(1)}, f32[4,2,48,128]{3,2,1,0:T(8,128)S(1)}, u32[]{:S(2)}, u32[]{:S(2)}) collective-permute-start(f32[4,2,48,128]{3,2,1,0:T(8,128)S(1)} %get-tuple-element.21), channel_id=1, source_target_pairs={{0,1},{1,0},{2,3},{3,2},{4,5},{5,4},{6,7},{7,6},{8,9},{9,8},{10,11... | collective-permute-start | bytes 589832 | tf_op jit(solution)/shard_map/ppermute | solution.py:78
  20.3 5.7 %collective-permute-start.3 = (f32[4,2,48,128]{3,2,1,0:T(8,128)S(1)}, f32[4,2,48,128]{3,2,1,0:T(8,128)S(1)}, u32[]{:S(2)}, u32[]{:S(2)}) collective-permute-start(f32[4,2,48,128]{3,2,1,0:T(8,128)S(1)} %get-tuple-element.22), channel_id=1, source_target_pairs={{1,2},{2,1},{3,4},{4,3},{5,6},{6,5},{7,8},{8,7},{9,10},{10,9},{11,... | collective-permute-start | bytes 589832 | tf_op jit(solution)/shard_map/ppermute | solution.py:78
  25.9 1.2 %pack_rim.1.rim = f32[4,2,8,16,128]{4,3,2,1,0:T(8,128)S(1)} custom-call(s32[4]{0:T(128)S(1)} %pad_add_fusion.info, f32[4,4,8,512]{3,2,1,0:T(8,128)S(1)} %collective-permute-done.above, f32[4,4,8,512]{3,2,1,0:T(8,128)S(1)} %collective-permute-done.1.below), custom_call_target="tpu_custom_call" | custom-call | flops 10000000 | bytes 1000000 | tf_op jit(solution)/shard_map/pack_rim/pallas_call | solution.py:568
  27.2 0.0 collective-permute-done.2.edge_a
  27.2 3.1 %collective-permute-done.3.edge_b = f32[4,2,48,128]{3,2,1,0:T(8,128)S(1)} collective-permute-done((f32[4,2,48,128]{3,2,1,0:T(8,128)S(1)}, f32[4,2,48,128]{3,2,1,0:T(8,128)S(1)}, u32[]{:S(2)}, u32[]{:S(2)}) %collective-permute-start.3) | collective-permute-done | bytes 196640 | tf_op jit(solution)/shard_map/ppermute | solution.py:78
  30.3 0.0 copy-done.3
  30.3 4.1 %down.1 = (f32[3,12,64,128]{3,2,1,0:T(8,128)S(1)}, f32[3,12,64,128]{3,2,1,0:T(8,128)S(1)}, f32[4,4,16,128]{3,2,1,0:T(8,128)S(1)}, f32[4,40,128]{2,1,0:T(8,128)S(...) custom-call(s32[4]{0:T(128)S(1)} %pad_add_fusion.info, f32[3]{0:T(128)S(1)} %copy-done.3, ...), custom_call_target="tpu_custom_call" | custom-call | tf_op jit(solution)/shard_map/down/pallas_call | solution.py:581
  34.4 3.6 %collective-permute-start.4 = (f32[4,40,128]{2,1,0:T(8,128)S(1)}, f32[4,40,128]{2,1,0:T(8,128)S(1)}, u32[]{:S(2)}, u32[]{:S(2)}) collective-permute-start(f32[4,40,128]{2,1,0:T(8,128)S(1)} %get-tuple-element.24), channel_id=1, source_target_pairs={{0,32},{32,0},{64,96},{96,64},{128,160},{160,128},{192,224},{224,1... | collective-permute-start | bytes 245768 | tf_op jit(solution)/shard_map/ppermute | solution.py:78
  37.9 0.7 collective-permute-start.5
  38.6 0.2 keep.1
  38.8 0.9 collective-permute-done.4.layers_a
  39.7 0.0 collective-permute-done.5.layers_b
  39.7 0.7 edges.1
  40.5 1.9 %collective-permute-start.6 = (f32[4,48,128]{2,1,0:T(8,128)S(1)}, f32[4,48,128]{2,1,0:T(8,128)S(1)}, u32[]{:S(2)}, u32[]{:S(2)}) collective-permute-start(f32[4,48,128]{2,1,0:T(8,128)S(1)} %get-tuple-element.31), channel_id=1, source_target_pairs={{0,1},{1,0},{2,3},{3,2},{4,5},{5,4},{6,7},{7,6},{8,9},{9,8},{10,11... | collective-permute-start | bytes 294920 | tf_op jit(solution)/shard_map/ppermute | solution.py:78
  42.4 6.5 %collective-permute-start.7 = (f32[4,48,128]{2,1,0:T(8,128)S(1)}, f32[4,48,128]{2,1,0:T(8,128)S(1)}, u32[]{:S(2)}, u32[]{:S(2)}) collective-permute-start(f32[4,48,128]{2,1,0:T(8,128)S(1)} %get-tuple-element.32), channel_id=1, source_target_pairs={{1,2},{2,1},{3,4},{4,3},{5,6},{6,5},{7,8},{8,7},{9,10},{10,9},{11,... | collective-permute-start | bytes 294920 | tf_op jit(solution)/shard_map/ppermute | solution.py:78
  49.6 0.0 collective-permute-done.6.coarse_a
  49.6 1.6 %collective-permute-done.7.coarse_b = f32[4,48,128]{2,1,0:T(8,128)S(1)} collective-permute-done((f32[4,48,128]{2,1,0:T(8,128)S(1)}, f32[4,48,128]{2,1,0:T(8,128)S(1)}, u32[]{:S(2)}, u32[]{:S(2)}) %collective-permute-start.7) | collective-permute-done | bytes 98336 | tf_op jit(solution)/shard_map/ppermute | solution.py:78
  51.2 3.0 %solve.1 = (f32[6,60,128]{2,1,0:T(8,128)S(1)}, f32[32,128]{1,0:T(8,128)S(1)}) custom-call(s32[4]{0:T(128)S(1)} %pad_add_fusion.info, f32[3]{0:T(128)S(1)} %copy-done.3, f32[1]{0:T(128)S(6)} %copy.16.previous, f32[4,4,16,128]{3,2,1,0:T(8,128)S(1)} %get-tuple-element.23.coarse, f32[4,40,128]{2,1,0:T(8,128)S(1)} %collective-permute-done.4.layers_a, ...), custom_call_target="tpu_custom_call" | custom-call | tf_op jit(solution)/shard_map/solve/pallas_call | solution.py:623
  54.3 14.8 %all_to_all.22 = f32[32,1,128]{2,1,0:T(1,128)S(1)} all-to-all(f32[32,1,128]{2,1,0:T(1,128)S(1)} %bitcast.29), channel_id=1, replica_groups=mesh['gx'=16,'gy'=8,'gz'=4] {'gy','gz'}, dimensions={0} | all-to-all | bytes 32768 | tf_op jit(solution)/shard_map/all_to_all | solution.py:656
  69.0 0.6 add.25
  69.6 17.8 %all-to-all-start.1 = ((f32[16,1,128]{2,1,0:T(1,128)}), f32[16,1,128]{2,1,0:T(1,128)S(1)}, u32[]{:S(2)}, u32[]{:S(2)}) async-start(f32[16,1,128]{2,1,0:T(1,128)} %bitcast.12), calls=%async_computation.1 | async-start | bytes 16384 | tf_op jit(solution)/shard_map/all_to_all | solution.py:665
  87.4 0.0 copy-start.1
  87.4 1.1 %copy-done.1 = f32[1,4,3,32,512]{4,3,2,1,0:T(8,128)S(1)} copy-done((f32[1,4,3,32,512]{4,3,2,1,0:T(8,128)S(1)}, f32[1,4,3,32,512]{4,3,2,1,0:T(8,128)}, u32[]{:S(2)}) %copy-start.1) | copy-done | bytes 786456
  88.6 4.7 %up.1 = (f32[4,3,32,512]{3,2,1,0:T(8,128)}, f32[4,3,32,512]{3,2,1,0:T(8,128)}) custom-call(s32[4]{0:T(128)S(1)} %pad_add_fusion.info, f32[3]{0:T(128)S(1)} %copy-done.3, f32[4,2,8,32,128]{4,3,2,1,0:T(8,128)S(1)} %pack.1.packed, f32[4,2,8,16,128]{4,3,2,1,0:T(8,128)S(1)} %pack_rim.1.rim, f32[4,2,48,128]{3,2,1,0:T(8,128)S(1)} %collective-permute-done.2.edge_a, ...), custom_call_target="tpu_custom_call" | custom-call | flops 40000000 | bytes 8000000 | tf_op jit(solution)/shard_map/up/pallas_call | solution.py:635
  93.3 5.4 %all-to-all-done.1 = f32[16,1,128]{2,1,0:T(1,128)S(1)} async-done(((f32[16,1,128]{2,1,0:T(1,128)}), f32[16,1,128]{2,1,0:T(1,128)S(1)}, u32[]{:S(2)}, u32[]{:S(2)}) %all-to-all-start.1) | async-done | bytes 8224 | tf_op jit(solution)/shard_map/all_to_all | solution.py:665
  98.6 2.8 %direction.1 = (f32[4,3,32,512]{3,2,1,0:T(8,128)}, f32[4,3,32,512]{3,2,1,0:T(8,128)}) custom-call(s32[4]{0:T(128)S(1)} %pad_add_fusion.info, f32[16,128]{1,0:T(8,128)S(1)} %bitcast.28, f32[4,3,32,512]{3,2,1,0:T(8,128)} %get-tuple-element.36.smoothed, f32[4,3,32,512]{3,2,1,0:T(8,128)} %get-tuple-element.37.old), custom_call_target="tpu_custom_call", output_to_operand_aliasing={{0}: (2, {}), {1}: (3, {})} | custom-call | tf_op jit(solution)/shard_map/direction/pallas_call | solution.py:666
  (2 shorter events, 0.0 us)
Async XLA Ops:
  0.6 10.4 %copy-start = (f32[1,4,3,32,512]{4,3,2,1,0:T(8,128)S(1)}, f32[1,4,3,32,512]{4,3,2,1,0:T(8,128)}, u32[]{:S(2)}) copy-start(f32[1,4,3,32,512]{4,3,2,1,0:T(8,128)} %param.9) | copy-start | bytes 2359300
  0.6 10.4 %copy-start.2 = (f32[1,4,32,512]{3,2,1,0:T(8,128)S(1)}, f32[1,4,32,512]{3,2,1,0:T(8,128)}, u32[]{:S(2)}) copy-start(f32[1,4,32,512]{3,2,1,0:T(8,128)} %param.8) | copy-start | bytes 786436
  0.7 7.8 %copy-start.4 = (s32[32]{0:T(128)S(1)}, s32[32]{0:T(128)}, u32[]{:S(2)}) copy-start(s32[32]{0:T(128)} %param.6) | copy-start | bytes 388
  2.7 10.3 %collective-permute-start = (f32[4,4,8,512]{3,2,1,0:T(8,128)S(1)}, f32[4,4,8,512]{3,2,1,0:T(8,128)S(1)}, u32[]{:S(2)}, u32[]{:S(2)}) collective-permute-start(f32[4,4,8,512]{3,2,1,0:T(8,128)S(1)} %pad_maximum_fusion), channel_id=1, source_target_pairs={{0,32},{32,64},{64,96},{96,128},{128,160},{160,192},{192,224},{224... | collective-permute-start | bytes 786440 | tf_op jit(solution)/shard_map/ppermute | solution.py:546
  7.1 7.3 %collective-permute-start.1 = (f32[4,4,8,512]{3,2,1,0:T(8,128)S(1)}, f32[4,4,8,512]{3,2,1,0:T(8,128)S(1)}, u32[]{:S(2)}, u32[]{:S(2)}) collective-permute-start(f32[4,4,8,512]{3,2,1,0:T(8,128)S(1)} %pad_maximum_fusion.1), channel_id=1, source_target_pairs={{32,0},{64,32},{96,64},{128,96},{160,128},{192,160},{224,192},{256... | collective-permute-start | bytes 786440 | tf_op jit(solution)/shard_map/ppermute | solution.py:547
  13.0 17.3 %copy-start.3 = (f32[3]{0:T(128)S(1)}, f32[3]{0:T(128)}, u32[]{:S(2)}) copy-start(f32[3]{0:T(128)} %factor.5) | copy-start | bytes 40
  15.3 11.9 %collective-permute-start.2 = (f32[4,2,48,128]{3,2,1,0:T(8,128)S(1)}, f32[4,2,48,128]{3,2,1,0:T(8,128)S(1)}, u32[]{:S(2)}, u32[]{:S(2)}) collective-permute-start(f32[4,2,48,128]{3,2,1,0:T(8,128)S(1)} %get-tuple-element.21), channel_id=1, source_target_pairs={{0,1},{1,0},{2,3},{3,2},{4,5},{5,4},{6,7},{7,6},{8,9},{9,8},{10,11... | collective-permute-start | bytes 589832 | tf_op jit(solution)/shard_map/ppermute | solution.py:78
  20.3 10.0 %collective-permute-start.3 = (f32[4,2,48,128]{3,2,1,0:T(8,128)S(1)}, f32[4,2,48,128]{3,2,1,0:T(8,128)S(1)}, u32[]{:S(2)}, u32[]{:S(2)}) collective-permute-start(f32[4,2,48,128]{3,2,1,0:T(8,128)S(1)} %get-tuple-element.22), channel_id=1, source_target_pairs={{1,2},{2,1},{3,4},{4,3},{5,6},{6,5},{7,8},{8,7},{9,10},{10,9},{11,... | collective-permute-start | bytes 589832 | tf_op jit(solution)/shard_map/ppermute | solution.py:78
  34.4 5.4 %collective-permute-start.4 = (f32[4,40,128]{2,1,0:T(8,128)S(1)}, f32[4,40,128]{2,1,0:T(8,128)S(1)}, u32[]{:S(2)}, u32[]{:S(2)}) collective-permute-start(f32[4,40,128]{2,1,0:T(8,128)S(1)} %get-tuple-element.24), channel_id=1, source_target_pairs={{0,32},{32,0},{64,96},{96,64},{128,160},{160,128},{192,224},{224,1... | collective-permute-start | bytes 245768 | tf_op jit(solution)/shard_map/ppermute | solution.py:78
  37.9 1.8 %collective-permute-start.5 = (f32[4,40,128]{2,1,0:T(8,128)S(1)}, f32[4,40,128]{2,1,0:T(8,128)S(1)}, u32[]{:S(2)}, u32[]{:S(2)}) collective-permute-start(f32[4,40,128]{2,1,0:T(8,128)S(1)} %get-tuple-element.25), channel_id=1, source_target_pairs={{32,64},{64,32},{96,128},{128,96},{160,192},{192,160},{224,256},{2... | collective-permute-start | bytes 245768 | tf_op jit(solution)/shard_map/ppermute | solution.py:78
  40.5 9.1 %collective-permute-start.6 = (f32[4,48,128]{2,1,0:T(8,128)S(1)}, f32[4,48,128]{2,1,0:T(8,128)S(1)}, u32[]{:S(2)}, u32[]{:S(2)}) collective-permute-start(f32[4,48,128]{2,1,0:T(8,128)S(1)} %get-tuple-element.31), channel_id=1, source_target_pairs={{0,1},{1,0},{2,3},{3,2},{4,5},{5,4},{6,7},{7,6},{8,9},{9,8},{10,11... | collective-permute-start | bytes 294920 | tf_op jit(solution)/shard_map/ppermute | solution.py:78
  42.4 8.8 %collective-permute-start.7 = (f32[4,48,128]{2,1,0:T(8,128)S(1)}, f32[4,48,128]{2,1,0:T(8,128)S(1)}, u32[]{:S(2)}, u32[]{:S(2)}) collective-permute-start(f32[4,48,128]{2,1,0:T(8,128)S(1)} %get-tuple-element.32), channel_id=1, source_target_pairs={{1,2},{2,1},{3,4},{4,3},{5,6},{6,5},{7,8},{8,7},{9,10},{10,9},{11,... | collective-permute-start | bytes 294920 | tf_op jit(solution)/shard_map/ppermute | solution.py:78
  69.6 29.0 %all-to-all-start.1 = ((f32[16,1,128]{2,1,0:T(1,128)}), f32[16,1,128]{2,1,0:T(1,128)S(1)}, u32[]{:S(2)}, u32[]{:S(2)}) async-start(f32[16,1,128]{2,1,0:T(1,128)} %bitcast.12), calls=%async_computation.1 | async-start | bytes 16384 | tf_op jit(solution)/shard_map/all_to_all | solution.py:665
  87.4 1.1 %copy-start.1 = (f32[1,4,3,32,512]{4,3,2,1,0:T(8,128)S(1)}, f32[1,4,3,32,512]{4,3,2,1,0:T(8,128)}, u32[]{:S(2)}) copy-start(f32[1,4,3,32,512]{4,3,2,1,0:T(8,128)} %param.10) | copy-start | bytes 2359300

commit v4 on v3

--- a/solution.py
+++ b/solution.py
@@ -537,7 +537,7 @@
             lax.dynamic_index_in_dim(box_counts, place, 0, keepdims=False),
             jnp.sum(box_counts),
             place % 2,
-            lax.axis_index(SLAB_AXIS) % 2,
+            jnp.ones_like(place),
         ]
     ).astype(jnp.int32)
 
@@ -595,7 +595,11 @@
         name="down",
     )(info, viscosity, packed, rim, *edges)
 
-    layers = exchange(*layers, SLAB_AXIS)
+    start, end = layers
+    layers = (
+        lax.ppermute(end, SLAB_AXIS, [(i, i + 1) for i in range(slab_n - 1)]),
+        lax.ppermute(start, SLAB_AXIS, [(i + 1, i) for i in range(slab_n - 1)]),
+    )
     pre_red, pre_black, partial = pl.pallas_call(
         keep_kernel,
         in_specs=[WHOLE] * 4,

time: 102 us -> 102 us (level)
  starting transfers between devices: 46.8 us -> 42.4 us
  waiting for transfers between devices: 12.4 us -> 16.7 us
    all_to_all x1, starting transfers between devices: 17.8 us -> 12.5 us  [per_device(): shares = lax.all_to_all(shares, SLAB_AXIS, 0, 0)]
    ppermute x0 -> x2, waiting for transfers between devices: none -> 5.15 us  [the longest x1 5.15 us: per_device(): lax.ppermute(start, SLAB_AXIS, [(i + 1, i) for i in range(slab_n - 1)])]
    ppermute x0 -> x2, starting transfers between devices: none -> 4.86 us  [the longest x1 3.56 us: per_device(): lax.ppermute(end, SLAB_AXIS, [(i, i + 1) for i in range(slab_n - 1)])]
    ppermute x6 -> x4, starting transfers between devices: 23.4 us -> 19.4 us  [swap(): return lax.ppermute(value, axis, pairs)]
    ppermute x6 -> x4, waiting for transfers between devices: 5.63 us -> 4.71 us  [swap(): return lax.ppermute(value, axis, pairs)]
where the time goes in v4:
time: 102 us; the launch traced here: 101 us
  starting transfers between devices  42.4 us (42%)
  Pallas kernels  20.1 us (20%)
  waiting for transfers between devices  16.7 us (16%)
  blocking collectives  14.8 us (15%)
  local copies, waits for them, and re-layouts  3.77 us (4%)
  other arithmetic  2.02 us (2%)
  between operations  1.67 us (2%)
    ppermute x4, starting transfers between devices, swap(): return lax.ppermute(value, axis, pairs)  19.4 us
    all_to_all x1, blocking collectives, per_device(): shares = lax.all_to_all(share, GROUP_AXES, 0, 0)  14.8 us
    all_to_all x1, starting transfers between devices, per_device(): shares = lax.all_to_all(shares, SLAB_AXIS, 0, 0)  12.5 us
    all_to_all x1, waiting for transfers between devices, per_device(): shares = lax.all_to_all(shares, SLAB_AXIS, 0, 0)  5.36 us
    ppermute x1, waiting for transfers between devices, per_device(): lax.ppermute(start, SLAB_AXIS, [(i + 1, i) for i in range(slab_n - 1)])  5.15 us
    ppermute x4, waiting for transfers between devices, swap(): return lax.ppermute(value, axis, pairs)  4.71 us
    pallas_call x1, Pallas kernels, per_device(): pl.pallas_call(up_kernel, in_specs=[SMEM] * 2 + [WHOLE] * 7 + [ANYWHERE],...  4.71 us
    ppermute x1, starting transfers between devices, per_device(): lax.ppermute(bottom, SLAB_AXIS, [(i, i + 1) for i in range(slab_n - 1)])  4.39 us
  transfers between devices with their start and end apart: 9, of which 5 were waited for; matrix products, arithmetic and copies ran while one was open for 3% of the time, Pallas kernels for 8%

profile of v4, /device:TPU:1, one launch (start us, length us, event | category | flops | bytes accessed | tf_op | source)
XLA Modules:
  0.0 101.4 jit_solution(15121670343815075913)
XLA Ops:
  0.6 0.0 copy-start
  0.6 0.0 copy-start.2
  0.7 0.0 copy-start.4
  0.7 1.1 %fusion = (f32[4,3,8,512]{3,2,1,0:T(8,128)S(1)}, f32[4,3,8,512]{3,2,1,0:T(8,128)S(1)}) fusion(f32[4,3,32,512]{3,2,1,0:T(8,128)} %bitcast.21), kind=kLoop, calls=%fused_computation.5 | loop fusion | bytes 786432 | tf_op jit(solution)/shard_map/slice | solution.py:544
  1.8 0.9 slice_bitcast_fusion
  2.7 4.4 %collective-permute-start = (f32[4,4,8,512]{3,2,1,0:T(8,128)S(1)}, f32[4,4,8,512]{3,2,1,0:T(8,128)S(1)}, u32[]{:S(2)}, u32[]{:S(2)}) collective-permute-start(f32[4,4,8,512]{3,2,1,0:T(8,128)S(1)} %pad_maximum_fusion), channel_id=1, source_target_pairs={{0,32},{32,64},{64,96},{96,128},{128,160},{160,192},{192,224},{224... | collective-permute-start | bytes 786440 | tf_op jit(solution)/shard_map/ppermute | solution.py:546
  7.1 1.3 %collective-permute-start.1 = (f32[4,4,8,512]{3,2,1,0:T(8,128)S(1)}, f32[4,4,8,512]{3,2,1,0:T(8,128)S(1)}, u32[]{:S(2)}, u32[]{:S(2)}) collective-permute-start(f32[4,4,8,512]{3,2,1,0:T(8,128)S(1)} %pad_maximum_fusion.1), channel_id=1, source_target_pairs={{32,0},{64,32},{96,64},{128,96},{160,128},{192,160},{224,192},{256... | collective-permute-start | bytes 786440 | tf_op jit(solution)/shard_map/ppermute | solution.py:547
  8.5 0.0 copy-done.4
  8.5 0.6 reduce_sum.9
  9.1 0.6 dynamic_slice.4
  9.7 1.3 %pad_add_fusion.info = s32[4]{0:T(128)S(1)} fusion(s32[1]{0:T(128)} %constant.31.clone.1, s32[1]{0:T(128)} %bitcast.1, s32[1]{0:T(128)} %bitcast, s32[1]{0:T(128)} %dynamic_slice.4), kind=kLoop, calls=%fused_computation.4 | loop fusion | flops 12 | bytes 32 | tf_op jit(solution)/shard_map/stack | solution.py:535
  11.0 0.0 copy-done
  11.0 0.0 copy-done.2
  11.0 1.9 %pack.1.packed = f32[4,2,8,32,128]{4,3,2,1,0:T(8,128)S(1)} custom-call(s32[4]{0:T(128)S(1)} %pad_add_fusion.info, f32[4,3,32,512]{3,2,1,0:T(8,128)S(1)} %bitcast.22, f32[4,32,512]{2,1,0:T(8,128)S(1)} %bitcast.25), custom_call_target="tpu_custom_call" | custom-call | flops 20000000 | bytes 2000000 | tf_op jit(solution)/shard_map/pack/pallas_call | solution.py:549
  12.9 0.0 copy-start.3
  13.0 0.0 collective-permute-done.above
  13.0 1.5 %collective-permute-done.1.below = f32[4,4,8,512]{3,2,1,0:T(8,128)S(1)} collective-permute-done((f32[4,4,8,512]{3,2,1,0:T(8,128)S(1)}, f32[4,4,8,512]{3,2,1,0:T(8,128)S(1)}, u32[]{:S(2)}, u32[]{:S(2)}) %collective-permute-start.1) | collective-permute-done | bytes 262176 | tf_op jit(solution)/shard_map/ppermute | solution.py:547
  14.4 0.8 pack_edges.1
  15.3 5.0 %collective-permute-start.2 = (f32[4,2,48,128]{3,2,1,0:T(8,128)S(1)}, f32[4,2,48,128]{3,2,1,0:T(8,128)S(1)}, u32[]{:S(2)}, u32[]{:S(2)}) collective-permute-start(f32[4,2,48,128]{3,2,1,0:T(8,128)S(1)} %get-tuple-element.21), channel_id=1, source_target_pairs={{0,1},{1,0},{2,3},{3,2},{4,5},{5,4},{6,7},{7,6},{8,9},{9,8},{10,11... | collective-permute-start | bytes 589832 | tf_op jit(solution)/shard_map/ppermute | solution.py:78
  20.3 5.7 %collective-permute-start.3 = (f32[4,2,48,128]{3,2,1,0:T(8,128)S(1)}, f32[4,2,48,128]{3,2,1,0:T(8,128)S(1)}, u32[]{:S(2)}, u32[]{:S(2)}) collective-permute-start(f32[4,2,48,128]{3,2,1,0:T(8,128)S(1)} %get-tuple-element.22), channel_id=1, source_target_pairs={{1,2},{2,1},{3,4},{4,3},{5,6},{6,5},{7,8},{8,7},{9,10},{10,9},{11,... | collective-permute-start | bytes 589832 | tf_op jit(solution)/shard_map/ppermute | solution.py:78
  25.9 1.2 %pack_rim.1.rim = f32[4,2,8,16,128]{4,3,2,1,0:T(8,128)S(1)} custom-call(s32[4]{0:T(128)S(1)} %pad_add_fusion.info, f32[4,4,8,512]{3,2,1,0:T(8,128)S(1)} %collective-permute-done.above, f32[4,4,8,512]{3,2,1,0:T(8,128)S(1)} %collective-permute-done.1.below), custom_call_target="tpu_custom_call" | custom-call | flops 10000000 | bytes 1000000 | tf_op jit(solution)/shard_map/pack_rim/pallas_call | solution.py:568
  27.2 0.0 collective-permute-done.2.edge_a
  27.2 3.1 %collective-permute-done.3.edge_b = f32[4,2,48,128]{3,2,1,0:T(8,128)S(1)} collective-permute-done((f32[4,2,48,128]{3,2,1,0:T(8,128)S(1)}, f32[4,2,48,128]{3,2,1,0:T(8,128)S(1)}, u32[]{:S(2)}, u32[]{:S(2)}) %collective-permute-start.3) | collective-permute-done | bytes 196640 | tf_op jit(solution)/shard_map/ppermute | solution.py:78
  30.3 0.0 copy-done.3
  30.3 4.1 %down.1 = (f32[3,12,64,128]{3,2,1,0:T(8,128)S(1)}, f32[3,12,64,128]{3,2,1,0:T(8,128)S(1)}, f32[4,4,16,128]{3,2,1,0:T(8,128)S(1)}, f32[4,40,128]{2,1,0:T(8,128)S(...) custom-call(s32[4]{0:T(128)S(1)} %pad_add_fusion.info, f32[3]{0:T(128)S(1)} %copy-done.3, ...), custom_call_target="tpu_custom_call" | custom-call | tf_op jit(solution)/shard_map/down/pallas_call | solution.py:581
  34.4 3.6 %collective-permute-start.4 = (f32[4,40,128]{2,1,0:T(8,128)S(1)}, f32[4,40,128]{2,1,0:T(8,128)S(1)}, u32[]{:S(2)}, u32[]{:S(2)}) collective-permute-start(f32[4,40,128]{2,1,0:T(8,128)S(1)} %get-tuple-element.24), channel_id=1, source_target_pairs={{0,32},{32,64},{64,96},{96,128},{128,160},{160,192},{192,224},{224... | collective-permute-start | bytes 245768 | tf_op jit(solution)/shard_map/ppermute | solution.py:600
  37.9 1.3 %collective-permute-start.5 = (f32[4,40,128]{2,1,0:T(8,128)S(1)}, f32[4,40,128]{2,1,0:T(8,128)S(1)}, u32[]{:S(2)}, u32[]{:S(2)}) collective-permute-start(f32[4,40,128]{2,1,0:T(8,128)S(1)} %get-tuple-element.25), channel_id=1, source_target_pairs={{32,0},{64,32},{96,64},{128,96},{160,128},{192,160},{224,192},{256... | collective-permute-start | bytes 245768 | tf_op jit(solution)/shard_map/ppermute | solution.py:601
  39.2 0.2 keep.1
  39.5 0.0 collective-permute-done.4.layers_a
  39.5 5.2 %collective-permute-done.5.layers_b = f32[4,40,128]{2,1,0:T(8,128)S(1)} collective-permute-done((f32[4,40,128]{2,1,0:T(8,128)S(1)}, f32[4,40,128]{2,1,0:T(8,128)S(1)}, u32[]{:S(2)}, u32[]{:S(2)}) %collective-permute-start.5) | collective-permute-done | bytes 81952 | tf_op jit(solution)/shard_map/ppermute | solution.py:601
  44.6 0.7 edges.1
  45.3 1.9 %collective-permute-start.6 = (f32[4,48,128]{2,1,0:T(8,128)S(1)}, f32[4,48,128]{2,1,0:T(8,128)S(1)}, u32[]{:S(2)}, u32[]{:S(2)}) collective-permute-start(f32[4,48,128]{2,1,0:T(8,128)S(1)} %get-tuple-element.31), channel_id=1, source_target_pairs={{0,1},{1,0},{2,3},{3,2},{4,5},{5,4},{6,7},{7,6},{8,9},{9,8},{10,11... | collective-permute-start | bytes 294920 | tf_op jit(solution)/shard_map/ppermute | solution.py:78
  47.2 6.8 %collective-permute-start.7 = (f32[4,48,128]{2,1,0:T(8,128)S(1)}, f32[4,48,128]{2,1,0:T(8,128)S(1)}, u32[]{:S(2)}, u32[]{:S(2)}) collective-permute-start(f32[4,48,128]{2,1,0:T(8,128)S(1)} %get-tuple-element.32), channel_id=1, source_target_pairs={{1,2},{2,1},{3,4},{4,3},{5,6},{6,5},{7,8},{8,7},{9,10},{10,9},{11,... | collective-permute-start | bytes 294920 | tf_op jit(solution)/shard_map/ppermute | solution.py:78
  54.7 0.0 collective-permute-done.6.coarse_a
  54.7 1.6 %collective-permute-done.7.coarse_b = f32[4,48,128]{2,1,0:T(8,128)S(1)} collective-permute-done((f32[4,48,128]{2,1,0:T(8,128)S(1)}, f32[4,48,128]{2,1,0:T(8,128)S(1)}, u32[]{:S(2)}, u32[]{:S(2)}) %collective-permute-start.7) | collective-permute-done | bytes 98336 | tf_op jit(solution)/shard_map/ppermute | solution.py:78
  56.3 3.0 %solve.1 = (f32[6,60,128]{2,1,0:T(8,128)S(1)}, f32[32,128]{1,0:T(8,128)S(1)}) custom-call(s32[4]{0:T(128)S(1)} %pad_add_fusion.info, f32[3]{0:T(128)S(1)} %copy-done.3, f32[1]{0:T(128)S(6)} %copy.16.previous, f32[4,4,16,128]{3,2,1,0:T(8,128)S(1)} %get-tuple-element.23.coarse, f32[4,40,128]{2,1,0:T(8,128)S(1)} %collective-permute-done.4.layers_a, ...), custom_call_target="tpu_custom_call" | custom-call | tf_op jit(solution)/shard_map/solve/pallas_call | solution.py:627
  59.3 14.8 %all_to_all.22 = f32[32,1,128]{2,1,0:T(1,128)S(1)} all-to-all(f32[32,1,128]{2,1,0:T(1,128)S(1)} %bitcast.28), channel_id=1, replica_groups=mesh['gx'=16,'gy'=8,'gz'=4] {'gy','gz'}, dimensions={0} | all-to-all | bytes 32768 | tf_op jit(solution)/shard_map/all_to_all | solution.py:660
  74.1 0.6 add.21
  74.7 12.5 %all-to-all-start.1 = ((f32[16,1,128]{2,1,0:T(1,128)}), f32[16,1,128]{2,1,0:T(1,128)S(1)}, u32[]{:S(2)}, u32[]{:S(2)}) async-start(f32[16,1,128]{2,1,0:T(1,128)} %bitcast.11), calls=%async_computation.1 | async-start | bytes 16384 | tf_op jit(solution)/shard_map/all_to_all | solution.py:669
  87.2 0.0 copy-start.1
  87.2 1.1 %copy-done.1 = f32[1,4,3,32,512]{4,3,2,1,0:T(8,128)S(1)} copy-done((f32[1,4,3,32,512]{4,3,2,1,0:T(8,128)S(1)}, f32[1,4,3,32,512]{4,3,2,1,0:T(8,128)}, u32[]{:S(2)}) %copy-start.1) | copy-done | bytes 786456
  88.3 4.7 %up.1 = (f32[4,3,32,512]{3,2,1,0:T(8,128)}, f32[4,3,32,512]{3,2,1,0:T(8,128)}) custom-call(s32[4]{0:T(128)S(1)} %pad_add_fusion.info, f32[3]{0:T(128)S(1)} %copy-done.3, f32[4,2,8,32,128]{4,3,2,1,0:T(8,128)S(1)} %pack.1.packed, f32[4,2,8,16,128]{4,3,2,1,0:T(8,128)S(1)} %pack_rim.1.rim, f32[4,2,48,128]{3,2,1,0:T(8,128)S(1)} %collective-permute-done.2.edge_a, ...), custom_call_target="tpu_custom_call" | custom-call | flops 40000000 | bytes 8000000 | tf_op jit(solution)/shard_map/up/pallas_call | solution.py:639
  93.0 5.4 %all-to-all-done.1 = f32[16,1,128]{2,1,0:T(1,128)S(1)} async-done(((f32[16,1,128]{2,1,0:T(1,128)}), f32[16,1,128]{2,1,0:T(1,128)S(1)}, u32[]{:S(2)}, u32[]{:S(2)}) %all-to-all-start.1) | async-done | bytes 8224 | tf_op jit(solution)/shard_map/all_to_all | solution.py:669
  98.4 2.8 %direction.1 = (f32[4,3,32,512]{3,2,1,0:T(8,128)}, f32[4,3,32,512]{3,2,1,0:T(8,128)}) custom-call(s32[4]{0:T(128)S(1)} %pad_add_fusion.info, f32[16,128]{1,0:T(8,128)S(1)} %bitcast.27, f32[4,3,32,512]{3,2,1,0:T(8,128)} %get-tuple-element.36.smoothed, f32[4,3,32,512]{3,2,1,0:T(8,128)} %get-tuple-element.37.old), custom_call_target="tpu_custom_call", output_to_operand_aliasing={{0}: (2, {}), {1}: (3, {})} | custom-call | tf_op jit(solution)/shard_map/direction/pallas_call | solution.py:670
  (2 shorter events, 0.0 us)
Async XLA Ops:
  0.6 10.4 %copy-start = (f32[1,4,3,32,512]{4,3,2,1,0:T(8,128)S(1)}, f32[1,4,3,32,512]{4,3,2,1,0:T(8,128)}, u32[]{:S(2)}) copy-start(f32[1,4,3,32,512]{4,3,2,1,0:T(8,128)} %param.9) | copy-start | bytes 2359300
  0.6 10.4 %copy-start.2 = (f32[1,4,32,512]{3,2,1,0:T(8,128)S(1)}, f32[1,4,32,512]{3,2,1,0:T(8,128)}, u32[]{:S(2)}) copy-start(f32[1,4,32,512]{3,2,1,0:T(8,128)} %param.8) | copy-start | bytes 786436
  0.7 7.8 %copy-start.4 = (s32[32]{0:T(128)S(1)}, s32[32]{0:T(128)}, u32[]{:S(2)}) copy-start(s32[32]{0:T(128)} %param.6) | copy-start | bytes 388
  2.7 10.2 %collective-permute-start = (f32[4,4,8,512]{3,2,1,0:T(8,128)S(1)}, f32[4,4,8,512]{3,2,1,0:T(8,128)S(1)}, u32[]{:S(2)}, u32[]{:S(2)}) collective-permute-start(f32[4,4,8,512]{3,2,1,0:T(8,128)S(1)} %pad_maximum_fusion), channel_id=1, source_target_pairs={{0,32},{32,64},{64,96},{96,128},{128,160},{160,192},{192,224},{224... | collective-permute-start | bytes 786440 | tf_op jit(solution)/shard_map/ppermute | solution.py:546
  7.1 7.3 %collective-permute-start.1 = (f32[4,4,8,512]{3,2,1,0:T(8,128)S(1)}, f32[4,4,8,512]{3,2,1,0:T(8,128)S(1)}, u32[]{:S(2)}, u32[]{:S(2)}) collective-permute-start(f32[4,4,8,512]{3,2,1,0:T(8,128)S(1)} %pad_maximum_fusion.1), channel_id=1, source_target_pairs={{32,0},{64,32},{96,64},{128,96},{160,128},{192,160},{224,192},{256... | collective-permute-start | bytes 786440 | tf_op jit(solution)/shard_map/ppermute | solution.py:547
  12.9 17.3 %copy-start.3 = (f32[3]{0:T(128)S(1)}, f32[3]{0:T(128)}, u32[]{:S(2)}) copy-start(f32[3]{0:T(128)} %factor.5) | copy-start | bytes 40
  15.3 11.9 %collective-permute-start.2 = (f32[4,2,48,128]{3,2,1,0:T(8,128)S(1)}, f32[4,2,48,128]{3,2,1,0:T(8,128)S(1)}, u32[]{:S(2)}, u32[]{:S(2)}) collective-permute-start(f32[4,2,48,128]{3,2,1,0:T(8,128)S(1)} %get-tuple-element.21), channel_id=1, source_target_pairs={{0,1},{1,0},{2,3},{3,2},{4,5},{5,4},{6,7},{7,6},{8,9},{9,8},{10,11... | collective-permute-start | bytes 589832 | tf_op jit(solution)/shard_map/ppermute | solution.py:78
  20.3 10.0 %collective-permute-start.3 = (f32[4,2,48,128]{3,2,1,0:T(8,128)S(1)}, f32[4,2,48,128]{3,2,1,0:T(8,128)S(1)}, u32[]{:S(2)}, u32[]{:S(2)}) collective-permute-start(f32[4,2,48,128]{3,2,1,0:T(8,128)S(1)} %get-tuple-element.22), channel_id=1, source_target_pairs={{1,2},{2,1},{3,4},{4,3},{5,6},{6,5},{7,8},{8,7},{9,10},{10,9},{11,... | collective-permute-start | bytes 589832 | tf_op jit(solution)/shard_map/ppermute | solution.py:78
  34.4 5.1 %collective-permute-start.4 = (f32[4,40,128]{2,1,0:T(8,128)S(1)}, f32[4,40,128]{2,1,0:T(8,128)S(1)}, u32[]{:S(2)}, u32[]{:S(2)}) collective-permute-start(f32[4,40,128]{2,1,0:T(8,128)S(1)} %get-tuple-element.24), channel_id=1, source_target_pairs={{0,32},{32,64},{64,96},{96,128},{128,160},{160,192},{192,224},{224... | collective-permute-start | bytes 245768 | tf_op jit(solution)/shard_map/ppermute | solution.py:600
  37.9 6.7 %collective-permute-start.5 = (f32[4,40,128]{2,1,0:T(8,128)S(1)}, f32[4,40,128]{2,1,0:T(8,128)S(1)}, u32[]{:S(2)}, u32[]{:S(2)}) collective-permute-start(f32[4,40,128]{2,1,0:T(8,128)S(1)} %get-tuple-element.25), channel_id=1, source_target_pairs={{32,0},{64,32},{96,64},{128,96},{160,128},{192,160},{224,192},{256... | collective-permute-start | bytes 245768 | tf_op jit(solution)/shard_map/ppermute | solution.py:601
  45.3 9.3 %collective-permute-start.6 = (f32[4,48,128]{2,1,0:T(8,128)S(1)}, f32[4,48,128]{2,1,0:T(8,128)S(1)}, u32[]{:S(2)}, u32[]{:S(2)}) collective-permute-start(f32[4,48,128]{2,1,0:T(8,128)S(1)} %get-tuple-element.31), channel_id=1, source_target_pairs={{0,1},{1,0},{2,3},{3,2},{4,5},{5,4},{6,7},{7,6},{8,9},{9,8},{10,11... | collective-permute-start | bytes 294920 | tf_op jit(solution)/shard_map/ppermute | solution.py:78
  47.2 9.1 %collective-permute-start.7 = (f32[4,48,128]{2,1,0:T(8,128)S(1)}, f32[4,48,128]{2,1,0:T(8,128)S(1)}, u32[]{:S(2)}, u32[]{:S(2)}) collective-permute-start(f32[4,48,128]{2,1,0:T(8,128)S(1)} %get-tuple-element.32), channel_id=1, source_target_pairs={{1,2},{2,1},{3,4},{4,3},{5,6},{6,5},{7,8},{8,7},{9,10},{10,9},{11,... | collective-permute-start | bytes 294920 | tf_op jit(solution)/shard_map/ppermute | solution.py:78
  74.7 23.7 %all-to-all-start.1 = ((f32[16,1,128]{2,1,0:T(1,128)}), f32[16,1,128]{2,1,0:T(1,128)S(1)}, u32[]{:S(2)}, u32[]{:S(2)}) async-start(f32[16,1,128]{2,1,0:T(1,128)} %bitcast.11), calls=%async_computation.1 | async-start | bytes 16384 | tf_op jit(solution)/shard_map/all_to_all | solution.py:669
  87.2 1.1 %copy-start.1 = (f32[1,4,3,32,512]{4,3,2,1,0:T(8,128)S(1)}, f32[1,4,3,32,512]{4,3,2,1,0:T(8,128)}, u32[]{:S(2)}) copy-start(f32[1,4,3,32,512]{4,3,2,1,0:T(8,128)} %param.10) | copy-start | bytes 2359300
